TPU v7x, 128 devices: a whole 4x4x4 slice. The times are simulated.
128 devices in a mesh: lon: 32 (over x, y, z_lo), lat: 4 (over z_hi, core).
Axes of the slice: x: 4, y: 4, z: 4 (z_hi: 2, z_lo: 2; z = z_hi * 2 + z_lo), core: 2. Of those that a mesh axis runs over, the one named last changes fastest.
Arguments:
- state: bfloat16 [512, 3, 16, 4096], P('lat', None, None, 'lon'), may hold values from -6 to 6
- weights: bfloat16 [512, 128, 4096], P('lat', None, 'lon'), may hold values from -1.767767 to 1.767767
- owners: int32 [32, 512, 1], P('lon', 'lat'), may hold values from 0 to 127; in each aligned block of 128 rows (0 to 127, 128 to 255, ..., all dimensions but the last counted through in order) at most 2 rows name the same one
- source_rows: int32 [32, 512], P('lon', 'lat'), may hold values from 0 to 127
- cutoffs: int32 [32], replicated, may hold values from 1 to 1023
- stiffness: float32 [512, 16, 4096], P('lat', None, 'lon'), may hold values from 0.02 to 1
Outputs:
- updated: float32 [512, 3, 16, 4096], P('lat', None, None, 'lon')
Inputs may be any that keep to these rules, and one draw needn't show every extreme that they name: `owners`: device d is longitude block d // 4 and latitude band d % 4; among the 128 target blocks of one device no device is named more than 2 times, and some device is named exactly 2 times.
All inputs are finite; a program needn't handle non-finite values.
Results may differ from a plain program's by a relative error of at most 0.0003.
Values may be sent and summed in bfloat16 or wider, within the bound.
No kernel may reach another device: no remote copies, remote signals or barrier semaphores. Data moves between devices by JAX's collectives and lax.ppermute only.
A program may use at most 128 MiB of HBM per device.

v0:
```python
import math

import jax
import jax.numpy as jnp
from jax import lax
from jax.sharding import PartitionSpec as P

ITERS = 5


def extended(block, sides, width):
    for axis, dim in sides:
        count = lax.axis_size(axis)
        forward = [(i, i + 1) for i in range(count - 1)]
        forward.append((count - 1, 0))
        backward = [(target, source) for source, target in forward]
        low = lax.ppermute(
            lax.slice_in_dim(block, block.shape[dim] - width, None, axis=dim), axis, forward
        )
        high = lax.ppermute(lax.slice_in_dim(block, 0, width, axis=dim), axis, backward)
        block = jnp.concatenate([low, block, high], axis=dim)
    return block


def wave_table(positions, total, modes):
    waves = jnp.arange(modes, dtype=jnp.int32)
    phase = positions[:, None] * waves[None, :] % total
    angle = phase.astype(jnp.float32) * (2.0 * math.pi / total)
    return jnp.concatenate([jnp.cos(angle), jnp.sin(angle)], axis=1)


def keep_scale(row_cut, total, modes):
    waves = jnp.arange(modes, dtype=jnp.int32)
    scale = jnp.where(waves == 0, 1.0, 2.0).astype(jnp.float32) / total
    kept = jnp.where(waves[None, :] <= row_cut[:, None], scale[None, :], 0.0)
    return jnp.concatenate([kept, kept], axis=1)


def extend(field):
    padded = extended(field, (("lon", 2), ("lat", 0)), 1)
    band = lax.axis_index("lat")
    bands = lax.axis_size("lat")
    top = jnp.where(band == 0, 0.0, padded[:1])
    bottom = jnp.where(band == bands - 1, 0.0, padded[-1:])
    return jnp.concatenate([top, padded[1:-1], bottom], axis=0)


def operate(field, stiffness):
    padded = extend(field)
    beside = padded[2:, :, 1:-1] + padded[:-2, :, 1:-1] + padded[1:-1, :, 2:] + padded[1:-1, :, :-2]
    return (4.0 + stiffness) * field - beside


def squares(residual):
    return lax.psum(jnp.sum(residual * residual), ("lon", "lat"))


def shards(state, weights, owners, source_rows, cutoffs, stiffness):
    lat_dev, _, levels, lon_dev = state.shape
    n_lon = lax.axis_size("lon")
    n_lat = lax.axis_size("lat")
    devices = n_lon * n_lat
    capacity = max(2, (2 * lat_dev + devices - 1) // devices)
    owner = owners[0, :, 0]
    wanted = source_rows[0]
    onehot = (owner[:, None] == jnp.arange(devices, dtype=jnp.int32)[None, :]).astype(jnp.int32)
    earlier = jnp.cumsum(onehot, axis=0) - onehot
    slot = jnp.sum(earlier * onehot, axis=1)
    requests = jnp.zeros((devices, capacity), jnp.int32).at[owner, slot].set(wanted)
    blocks = state[
        lax.all_to_all(requests, ("lon", "lat"), split_axis=0, concat_axis=0, tiled=True)
    ]
    moved = lax.all_to_all(blocks, ("lon", "lat"), split_axis=0, concat_axis=0, tiled=True)
    sources = moved[owner, slot].reshape(lat_dev, 3 * levels, lon_dev)
    arrived = jnp.einsum("bci,bij->bcj", sources, weights, preferred_element_type=jnp.float32)
    arrived = arrived.reshape(lat_dev, 3, levels, lon_dev)
    polar = cutoffs.shape[0] // 2
    band = lax.axis_index("lat")
    north = band == 0
    south = band == n_lat - 1
    start = jnp.where(north, 0, lat_dev - polar).astype(jnp.int32)
    row_cut = jnp.where(north, cutoffs[:polar], cutoffs[polar:])
    row_cut_flat = jnp.repeat(row_cut, 3 * levels)
    caps = lax.dynamic_slice_in_dim(arrived, start, polar, 0)
    flat = caps.reshape(polar * 3 * levels, lon_dev)
    total_lon = lon_dev * n_lon
    modes = total_lon // 4
    highest = lax.Precision.HIGHEST
    positions = lax.axis_index("lon") * lon_dev + jnp.arange(lon_dev, dtype=jnp.int32)
    table = wave_table(positions, total_lon, modes)
    partial_spectrum = jnp.dot(flat, table, precision=highest)
    spectrum = lax.psum(partial_spectrum, "lon")
    smooth = jnp.dot(
        spectrum * keep_scale(row_cut_flat, total_lon, modes), table.T, precision=highest
    )
    smooth = smooth.reshape(polar, 3, levels, lon_dev)
    caps_new = jnp.where(north | south, smooth, caps)
    filtered = lax.dynamic_update_slice_in_dim(arrived, caps_new, start, 0)
    u_field = filtered[:, 0]
    v_field = filtered[:, 1]
    theta = filtered[:, 2]
    padded = extend(jnp.concatenate([u_field, v_field], axis=1))
    u_pad = padded[:, :levels]
    v_pad = padded[:, levels:]
    divergence = (
        u_pad[1:-1, :, 2:] - u_pad[1:-1, :, :-2] + (v_pad[2:, :, 1:-1] - v_pad[:-2, :, 1:-1])
    )
    rhs = theta - 0.5 * divergence
    phi = jnp.zeros_like(rhs)
    residual = rhs
    direction = rhs
    norm_now = squares(residual)
    for step in range(ITERS):
        image = operate(direction, stiffness)
        alpha = norm_now / lax.psum(jnp.sum(direction * image), ("lon", "lat"))
        phi = phi + alpha * direction
        residual = residual - alpha * image
        norm_next = squares(residual)
        direction = residual + norm_next / norm_now * direction
        norm_now = norm_next
    phi_pad = extend(phi)
    u_new = u_field - 0.5 * (phi_pad[1:-1, :, 2:] - phi_pad[1:-1, :, :-2])
    v_new = v_field - 0.5 * (phi_pad[2:, :, 1:-1] - phi_pad[:-2, :, 1:-1])
    return jnp.stack([u_new, v_new, theta - phi], axis=1)


def solution(mesh):
    in_specs = (
        P("lat", None, None, "lon"),
        P("lat", None, "lon"),
        P("lon", "lat", None),
        P("lon", "lat"),
        P(),
        P("lat", None, "lon"),
    )
    out_specs = P("lat", None, None, "lon")
    return jax.shard_map(shards, mesh=mesh, in_specs=in_specs, out_specs=out_specs, check_vma=False)
```

profile of v0, /device:TPU:1, one launch (start us, length us, event | category | flops | bytes accessed | tf_op | source)
XLA Modules:
  0.0 1250.9 jit_solution(15793092807090056386)
XLA Ops:
  9.1 11.0 scatter_fusion
  20.2 20.8 %all_to_all.17 = s32[128,1,2]{2,1,0:T(1,128)S(1)} all-to-all(s32[128,1,2]{2,1,0:T(1,128)S(1)} %copy.16), channel_id=1, replica_groups=mesh['lon'=32,'lat'=4] {'lon','lat'}, dimensions={0} | all-to-all | bytes 2048 | tf_op jit(solution)/shard_map/all_to_all | solution.py:71
  41.2 2.6 gather_fusion
  43.8 5.5 all-to-all-start.1
  49.6 3.2 fusion.47
  52.9 38.1 %all-to-all-done.1 = bf16[128,2,3,16,128]{4,3,2,1,0:T(8,128)(2,1)} async-done(((bf16[128,2,3,16,128]{4,3,2,1,0:T(8,128)(2,1)}), bf16[128,2,3,16,128]{4,3,2,1,0:T(8,128)(2,1)}, u32[]{:S(2)}, u32[]{:S(2)}) %all-to-all-start.1) | async-done | bytes 3145760 | tf_op jit(solution)/shard_map/all_to_all | solution.py:73
  90.9 3.9 gather_fusion.1
  94.9 4.0 fusion.64
  98.9 7.0 fusion.39
  106.8 1.9 fusion.3
  108.7 311.5 %all-reduce.3.cloned.1.call-done = f32[768,2048]{1,0:T(8,128)} async-done(((f32[768,2048]{1,0:T(8,128)}), f32[768,2048]{1,0:T(8,128)}) %all-reduce.3.cloned.1.call-update) | async-done | bytes 6291472 | tf_op jit(solution)/shard_map/psum | solution.py:92
  420.3 9.7 fusion
  430.3 3.1 pad_maximum_fusion.1
  433.3 2.7 copy.19
  436.0 3.8 collective-permute-start
  439.8 2.7 copy.21
  442.9 2.9 copy.20
  445.8 3.9 collective-permute-done.1
  449.7 2.8 copy.22
  453.6 21.6 %collective-permute-start.2 = (f32[1,32,130]{2,1,0:T(8,128)S(1)}, f32[1,32,130]{2,1,0:T(8,128)S(1)}, u32[]{:S(2)}, u32[]{:S(2)}) collective-permute-start(f32[1,32,130]{2,1,0:T(8,128)S(1)} %get-tuple-element.26), channel_id=1, source_target_pairs={{1,0},{2,1},{3,2},{0,3},{5,4},{6,5},{7,6},{4,7},{9,8},{10,9},{11,1... | collective-permute-start | bytes 49928 | tf_op jit(solution)/shard_map/ppermute | solution.py:20
  475.2 2.5 collective-permute-start.3
  477.6 1.9 collective-permute-done.2
  479.6 2.7 fusion.37
  483.6 5.7 collective-permute-start.5
  492.7 1.8 collective-permute-start.6
  494.5 2.4 collective-permute-start.7
  498.3 4.1 multiply_reduce_fusion.7
  502.4 65.9 %all-reduce = (f32[]{:T(128)}, f32[]{:T(128)}) all-reduce(f32[]{:T(128)} %get-tuple-element.6, f32[]{:T(128)} %get-tuple-element.5), channel_id=1, replica_groups=mesh['lon'=32,'lat'=4] {'lon','lat'}, use_global_device_ids=true, to_apply=%region_5.6 | all-reduce | flops 2 | bytes 16 | tf_op jit(solution)/shard_map/psum | solution.py:55
  570.5 63.7 %psum.80 = f32[]{:T(128)} all-reduce(f32[]{:T(128)} %multiply_reduce_fusion.6), channel_id=1, replica_groups=mesh['lon'=32,'lat'=4] {'lon','lat'}, use_global_device_ids=true, to_apply=%region_9.10 | all-reduce | flops 1 | bytes 8 | tf_op jit(solution)/shard_map/psum | solution.py:55
  641.8 5.7 collective-permute-start.9
  652.8 1.8 collective-permute-start.11
  656.0 3.0 multiply_reduce_fusion.5
  659.0 66.7 %psum.81 = f32[]{:T(128)} all-reduce(f32[]{:T(128)} %get-tuple-element.19), channel_id=1, replica_groups=mesh['lon'=32,'lat'=4] {'lon','lat'}, use_global_device_ids=true, to_apply=%region_11.12 | all-reduce | flops 1 | bytes 8 | tf_op jit(solution)/shard_map/psum | solution.py:115
  727.0 3.3 multiply_reduce_fusion.4
  730.3 62.5 %psum.82 = f32[]{:T(128)} all-reduce(f32[]{:T(128)} %get-tuple-element.17), channel_id=1, replica_groups=mesh['lon'=32,'lat'=4] {'lon','lat'}, use_global_device_ids=true, to_apply=%region_13.14 | all-reduce | flops 1 | bytes 8 | tf_op jit(solution)/shard_map/psum | solution.py:55
  795.5 1.7 fusion.61
  801.3 4.8 collective-permute-start.13
  811.1 2.3 collective-permute-start.15
  814.7 3.1 multiply_reduce_fusion.3
  817.8 66.3 %psum.83 = f32[]{:T(128)} all-reduce(f32[]{:T(128)} %get-tuple-element.15), channel_id=1, replica_groups=mesh['lon'=32,'lat'=4] {'lon','lat'}, use_global_device_ids=true, to_apply=%region_15.16 | all-reduce | flops 1 | bytes 8 | tf_op jit(solution)/shard_map/psum | solution.py:115
  885.4 3.3 multiply_reduce_fusion.2
  888.8 62.8 %psum.84 = f32[]{:T(128)} all-reduce(f32[]{:T(128)} %get-tuple-element.13), channel_id=1, replica_groups=mesh['lon'=32,'lat'=4] {'lon','lat'}, use_global_device_ids=true, to_apply=%region_17.18 | all-reduce | flops 1 | bytes 8 | tf_op jit(solution)/shard_map/psum | solution.py:55
  952.9 2.4 multiply_add_fusion.2
  955.3 3.2 fusion.60
  962.3 5.2 collective-permute-start.17
  972.6 2.0 collective-permute-start.19
  976.1 6.2 multiply_reduce_fusion.1
  982.2 66.5 %psum.85 = f32[]{:T(128)} all-reduce(f32[]{:T(128)} %get-tuple-element.11), channel_id=1, replica_groups=mesh['lon'=32,'lat'=4] {'lon','lat'}, use_global_device_ids=true, to_apply=%region_19.20 | all-reduce | flops 1 | bytes 8 | tf_op jit(solution)/shard_map/psum | solution.py:115
  1050.1 2.4 multiply_reduce_fusion
  1052.5 62.8 %psum.86 = f32[]{:T(128)} all-reduce(f32[]{:T(128)} %multiply_reduce_fusion), channel_id=1, replica_groups=mesh['lon'=32,'lat'=4] {'lon','lat'}, use_global_device_ids=true, to_apply=%region_21.22 | all-reduce | flops 1 | bytes 8 | tf_op jit(solution)/shard_map/psum | solution.py:55
  1116.6 3.0 multiply_add_fusion.1
  1119.7 3.2 fusion.59
  1127.1 4.8 collective-permute-start.21
  1136.9 2.1 collective-permute-start.23
  1140.5 5.1 fusion.15
  1145.6 66.4 %psum.87 = f32[]{:T(128)} all-reduce(f32[]{:T(128)} %fusion.15), channel_id=1, replica_groups=mesh['lon'=32,'lat'=4] {'lon','lat'}, use_global_device_ids=true, to_apply=%region_23.24 | all-reduce | flops 1 | bytes 8 | tf_op jit(solution)/shard_map/psum | solution.py:115
  1213.3 3.6 subtract_bitcast_fusion
  1216.9 2.9 fusion.58
  1220.2 1.6 collective-permute-start.24
  1221.9 1.8 copy.57
  1225.1 5.3 collective-permute-done.25
  1232.8 2.2 collective-permute-start.26
  1237.6 3.9 fusion.11
  1241.7 1.9 copy.61
  (168 shorter events, 65.5 us)
Async XLA Ops:
  6.5 34.6 %copy-start = (bf16[128,3,16,128]{3,2,1,0:T(8,128)(2,1)S(1)}, bf16[128,3,16,128]{3,2,1,0:T(8,128)(2,1)}, u32[]{:S(2)}) copy-start(bf16[128,3,16,128]{3,2,1,0:T(8,128)(2,1)} %param.6) | copy-start | bytes 4718596
  43.8 47.1 %all-to-all-start.1 = ((bf16[128,2,3,16,128]{4,3,2,1,0:T(8,128)(2,1)}), bf16[128,2,3,16,128]{4,3,2,1,0:T(8,128)(2,1)}, u32[]{:S(2)}, u32[]{:S(2)}) async-start(bf16[128,2,3,16,128]{4,3,2,1,0:T(8,128)(2,1)} %bitcast.58), calls=%async_computation.1 | async-start | bytes 6291456 | tf_op jit(solution)/shard_map/all_to_all | solution.py:73
  49.3 370.9 %all-reduce.3.cloned.1.call-start = ((), (), s32[]{:S(2)}) async-start(), calls=%async_computation.2 | async-start | bytes 12582912 | tf_op jit(solution)/shard_map/psum | solution.py:92
  94.9 4.0 copy-start.27
  94.9 4.0 copy-start.28
  105.9 0.7 copy-start.30
  430.1 22.5 %copy-start.2 = (f32[128,3,16,128]{3,2,1,0:T(8,128)}, f32[128,3,16,128]{3,2,1,0:T(8,128)S(1)}, u32[]{:S(2)}) copy-start(f32[128,3,16,128]{3,2,1,0:T(8,128)S(1)} %select_dynamic-update-slice_fusion) | copy-start | bytes 9437188
  430.2 3.1 copy-start.11
  430.2 3.1 copy-start.13
  436.0 6.9 collective-permute-start
  442.5 7.3 collective-permute-start.1
  452.5 27.0 %copy-start.8 = (f32[128,32,1]{2,1,0:T(8,128)S(1)}, f32[128,32,1]{2,1,0:T(8,128)}, u32[]{:S(2)}) copy-start(f32[128,32,1]{2,1,0:T(8,128)} %copy.20) | copy-start | bytes 49156
  452.5 27.0 %copy-start.9 = (f32[128,32,1]{2,1,0:T(8,128)S(1)}, f32[128,32,1]{2,1,0:T(8,128)}, u32[]{:S(2)}) copy-start(f32[128,32,1]{2,1,0:T(8,128)} %copy.22) | copy-start | bytes 49156
  452.5 27.0 %copy-start.12 = (f32[128,16,128]{2,1,0:T(8,128)S(1)}, f32[128,16,128]{2,1,0:T(8,128)}, u32[]{:S(2)}) copy-start(f32[128,16,128]{2,1,0:T(8,128)} %copy-done.11) | copy-start | bytes 3145732
  452.6 27.1 %copy-start.14 = (f32[128,16,128]{2,1,0:T(8,128)S(1)}, f32[128,16,128]{2,1,0:T(8,128)}, u32[]{:S(2)}) copy-start(f32[128,16,128]{2,1,0:T(8,128)} %copy-done.13) | copy-start | bytes 3145732
  453.6 26.0 %collective-permute-start.2 = (f32[1,32,130]{2,1,0:T(8,128)S(1)}, f32[1,32,130]{2,1,0:T(8,128)S(1)}, u32[]{:S(2)}, u32[]{:S(2)}) collective-permute-start(f32[1,32,130]{2,1,0:T(8,128)S(1)} %get-tuple-element.26), channel_id=1, source_target_pairs={{1,0},{2,1},{3,2},{0,3},{5,4},{6,5},{7,6},{4,7},{9,8},{10,9},{11,1... | collective-permute-start | bytes 49928 | tf_op jit(solution)/shard_map/ppermute | solution.py:20
  475.2 4.4 collective-permute-start.3
  483.1 6.8 collective-permute-start.4
  483.1 15.1 %copy-start.4 = (f32[128,16,128]{2,1,0:T(8,128)S(1)}, f32[128,16,128]{2,1,0:T(8,128)}, u32[]{:S(2)}) copy-start(f32[128,16,128]{2,1,0:T(8,128)} %param.11) | copy-start | bytes 3145732
  483.6 6.8 collective-permute-start.5
  490.4 7.9 copy-start.19
  491.8 6.5 copy-start.23
  492.7 5.6 collective-permute-start.6
  494.5 3.7 collective-permute-start.7
  502.4 131.8 %copy-start.10 = (f32[128,16,128]{2,1,0:T(8,128)}, f32[128,16,128]{2,1,0:T(8,128)S(1)}, u32[]{:S(2)}) copy-start(f32[128,16,128]{2,1,0:T(8,128)S(1)} %get-tuple-element.21) | copy-start | bytes 3145732
  640.1 7.4 collective-permute-start.8
  641.8 7.1 collective-permute-start.9
  650.3 5.7 copy-start.20
  650.3 5.7 copy-start.24
  651.3 4.7 collective-permute-start.10
  652.8 3.2 collective-permute-start.11
  798.7 7.4 collective-permute-start.12
  801.3 6.3 collective-permute-start.13
  809.0 5.7 copy-start.5
  809.0 5.7 copy-start.21
  809.0 5.8 copy-start.25
  809.9 4.7 collective-permute-start.14
  811.1 3.6 collective-permute-start.15
  960.1 7.4 collective-permute-start.16
  962.3 6.6 collective-permute-start.17
  970.3 5.8 copy-start.6
  970.3 5.8 copy-start.22
  970.3 5.8 copy-start.26
  971.3 4.7 collective-permute-start.18
  972.6 3.5 collective-permute-start.19
  1124.5 7.4 collective-permute-start.20
  1127.1 6.2 collective-permute-start.21
  1134.7 5.8 copy-start.7
  1134.7 5.8 copy-start.17
  1134.7 5.8 copy-start.18
  1135.7 4.7 collective-permute-start.22
  1136.9 3.6 collective-permute-start.23
  1220.2 3.5 collective-permute-start.24
  1221.9 15.7 %copy-start.3 = (f32[128,3,16,128]{3,2,1,0:T(8,128)S(1)}, f32[128,3,16,128]{3,2,1,0:T(8,128)}, u32[]{:S(2)}) copy-start(f32[128,3,16,128]{3,2,1,0:T(8,128)} %copy-done.2) | copy-start | bytes 9437188
  1223.7 6.7 collective-permute-start.25
  1231.8 5.8 copy-start.15
  1231.8 5.8 copy-start.16
  1232.8 4.7 collective-permute-start.26
  1235.0 2.5 collective-permute-start.27
  1237.6 3.9 copy-start.29
  1241.5 2.1 copy-start.1
Sparse Core Ops, SparseCore 0:
  106.1 314.1 all-reduce.2
where the time goes:
time: 1260 us; the launch traced here: 1250 us
  blocking collectives  604 us (48%)
  waiting for transfers between devices  370 us (29%)
  starting transfers between devices  85.5 us (7%)
  local copies, waits for them, and re-layouts  76.8 us (6%)
  other arithmetic  67.8 us (5%)
  between operations  26.1 us (2%)
  matrix products  20.7 us (2%)
    psum x5, blocking collectives, squares(): return lax.psum(jnp.sum(residual * residual), ('lon', 'lat'))  318 us
    psum x1, waiting for transfers between devices, shards(): spectrum = lax.psum(partial_spectrum, 'lon')  312 us
    psum x4, blocking collectives, shards(): alpha = norm_now / lax.psum(jnp.sum(direction * image), ('lon', 'lat'))  266 us
    ppermute x14, starting transfers between devices, extended(): lax.ppermute(lax.slice_in_dim(block, 0, width, axis=dim), axis, backward)  62.4 us
    all_to_all x1, waiting for transfers between devices, shards(): lax.all_to_all(blocks, ('lon', 'lat'), split_axis=0, concat_axis=0, tiled...  38.1 us
  transfers between devices with their start and end apart: 30, of which 12 were waited for; matrix products, arithmetic and copies ran while one was open for 2% of the time, Pallas kernels for 0%

commit v1 on v0

v1 whole, which is shorter than its diff:
```python
import numpy as np
import jax
import jax.numpy as jnp
from jax import lax
from jax.sharding import PartitionSpec as P

ITERS = 5
BOTH = ("lon", "lat")
HIGHEST = lax.Precision.HIGHEST


def neighbours(block, axis, dim, width, wrap):
    count = lax.axis_size(axis)
    forward = [(i, (i + 1) % count) for i in range(count if wrap else count - 1)]
    backward = [(target, source) for source, target in forward]
    size = block.shape[dim]
    low = lax.ppermute(lax.slice_in_dim(block, size - width, size, axis=dim), axis, forward)
    high = lax.ppermute(lax.slice_in_dim(block, 0, width, axis=dim), axis, backward)
    return jnp.concatenate([low, block, high], axis=dim)


def extend(block, width):
    return neighbours(neighbours(block, "lon", 2, width, True), "lat", 0, width, False)


def exchange(block, axes):
    return lax.all_to_all(block, axes, split_axis=0, concat_axis=0, tiled=True)


def fetch(state, owner, wanted):
    devices = lax.axis_size("lon") * lax.axis_size("lat")
    rows = owner.shape[0]
    same = owner[:, None] == owner[None, :]
    order = jnp.arange(rows, dtype=jnp.int32)
    slot = jnp.sum(same & (order[None, :] < order[:, None]), axis=1).astype(jnp.int32)
    named = owner[None, :] == jnp.arange(devices, dtype=jnp.int32)[:, None]
    requests = jnp.stack(
        [jnp.sum(jnp.where(named & (slot == s)[None, :], wanted[None, :], 0), axis=1) for s in range(2)],
        axis=1,
    )
    blocks = state[exchange(requests, BOTH)]
    moved = exchange(blocks, BOTH)
    return moved[owner, slot]


def low_pass(lines, cutoff):
    parts, count, points = lines.shape
    total = parts * points
    half = parts // 2 + 1
    d = np.arange(parts)
    k1 = np.arange(half)
    p = np.arange(points)
    first = 2 * np.pi * np.outer(k1, d) / parts
    twist = 2 * np.pi * np.outer(k1, p) / total
    inner = 2 * np.pi * np.outer(p, p) / points
    f32 = lambda a: jnp.asarray(a, jnp.float32)
    real = jnp.einsum("kd,dmp->kmp", f32(np.cos(first)), lines, precision=HIGHEST)
    imag = jnp.einsum("kd,dmp->kmp", f32(-np.sin(first)), lines, precision=HIGHEST)
    tc, ts = f32(np.cos(twist))[:, None, :], f32(np.sin(twist))[:, None, :]
    both = jnp.concatenate([real * tc + imag * ts, imag * tc - real * ts], axis=2)
    c, s = np.cos(inner), np.sin(inner)
    forward = f32(np.block([[c, -s], [s, c]]))
    inverse = f32(np.block([[c, s], [-s, c]]))
    spectrum = jnp.einsum("kmp,pq->kmq", both, forward, precision=HIGHEST)
    wave = jnp.asarray(k1[:, None] + parts * p[None, :], jnp.int32)
    kept = ((wave <= cutoff) | (wave >= total - cutoff)).astype(jnp.float32) / total
    kept = jnp.concatenate([kept, kept], axis=1)[:, None, :]
    back = jnp.einsum("kmp,pq->kmq", spectrum * kept, inverse, precision=HIGHEST)
    br, bi = back[..., :points], back[..., points:]
    weight = np.where((k1 == 0) | (k1 == parts // 2), 1.0, 2.0)[:, None]
    dr = br * tc - bi * ts
    di = br * ts + bi * tc
    return jnp.einsum("kd,kmp->dmp", f32(weight * np.cos(first)), dr, precision=HIGHEST) - jnp.einsum(
        "kd,kmp->dmp", f32(weight * np.sin(first)), di, precision=HIGHEST
    )


def solve(moments):
    squares, cross = moments[: ITERS], moments[ITERS :]
    mu = [squares[0], cross[0]]
    for k in range(1, ITERS):
        mu += [2.0 * squares[k] - mu[0], 2.0 * cross[k] - mu[1]]

    def inner(a, b):
        terms = [a[i] * b[j] * (0.5 * (mu[i + j] + mu[abs(i - j)])) for i in range(len(a)) for j in range(len(b))]
        return sum(terms)

    def image_of(a):
        out = [4.5 * x for x in a] + [0.0]
        for k, x in enumerate(a):
            out[k + 1] = out[k + 1] + 2.25 * x
            out[abs(k - 1)] = out[abs(k - 1)] + 2.25 * x
        return out

    phi = []
    residual = [jnp.float32(1.0)]
    direction = residual
    norm = mu[0]
    for step in range(ITERS):
        image = image_of(direction)
        alpha = norm / inner(direction, image)
        phi = [x + alpha * y for x, y in zip(phi + [0.0], direction)]
        if step < ITERS - 1:
            residual = [x - alpha * y for x, y in zip(residual + [0.0], image)]
            following = inner(residual, residual)
            ratio = following / norm
            direction = [x + ratio * y for x, y in zip(residual, direction + [0.0])]
            norm = following
    return phi


def shards(state, weights, owners, source_rows, cutoffs, stiffness):
    rows, _, levels, points = state.shape
    n_lon = lax.axis_size("lon")
    n_lat = lax.axis_size("lat")
    band = lax.axis_index("lat")
    north, south = band == 0, band == n_lat - 1
    depth = ITERS + 1
    stiff = extend(stiffness, depth)
    sources = fetch(state, owners[0, :, 0], source_rows[0]).reshape(rows, 3 * levels, points)
    arrived = jnp.einsum("bci,bij->bcj", sources, weights, preferred_element_type=jnp.float32)
    polar = cutoffs.shape[0] // 2
    start = jnp.where(north, 0, rows - polar).astype(jnp.int32)
    caps = lax.dynamic_slice_in_dim(arrived, start, polar, 0)
    lines = exchange(caps.reshape(n_lon, -1, points), "lon")
    line = lax.axis_index("lon") * polar // n_lon
    cutoff = cutoffs[jnp.where(north, line, polar + line)]
    smooth = exchange(low_pass(lines, cutoff), "lon").reshape(caps.shape)
    filtered = lax.dynamic_update_slice_in_dim(arrived, jnp.where(north | south, smooth, caps), start, 0)
    wide = extend(filtered, depth)
    u, v, theta = wide[:, :levels], wide[:, levels : 2 * levels], wide[:, 2 * levels :]
    place = jnp.arange(rows + 2 * depth) - depth + band * rows
    inside = ((place >= 0) & (place < n_lat * rows)).astype(jnp.float32)[:, None, None]

    def core(a, b):
        return a[1:-1, :, 1:-1], b

    def beside(p):
        return p[2:, :, 1:-1] + p[:-2, :, 1:-1] + p[1:-1, :, 2:] + p[1:-1, :, :-2]

    divergence = u[1:-1, :, 2:] - u[1:-1, :, :-2] + (v[2:, :, 1:-1] - v[:-2, :, 1:-1])
    table = [(theta[1:-1, :, 1:-1] - 0.5 * divergence) * inside[1:-1]]
    slope = (4.0 / 9.0) * (stiff - 0.5)
    squares, cross = [], []
    for k in range(ITERS):
        last = table[-1]
        w = depth - 2 - k
        cut = k + 2
        twice = slope[cut:-cut, :, cut:-cut] * last[1:-1, :, 1:-1] - (4.0 / 9.0) * beside(last)
        following = 0.5 * twice if k == 0 else twice - table[-2][2:-2, :, 2:-2]
        following = following * inside[cut:-cut]
        table.append(following)
    cores = []
    for k, t in enumerate(table):
        w = depth - 1 - k
        cores.append(t[w : w + rows, :, w : w + points])
    squares = [jnp.sum(cores[k] * cores[k]) for k in range(ITERS)]
    cross = [jnp.sum(cores[k] * cores[k + 1]) for k in range(ITERS)]
    moments = jnp.stack(squares + cross)
    spread = exchange(jnp.broadcast_to(moments[None], (n_lon * n_lat, 2 * ITERS)), BOTH)
    coefficients = solve(jnp.sum(spread, axis=0))
    phi = 0.0
    for k in range(ITERS):
        w = ITERS - 1 - k
        t = table[k]
        phi = phi + coefficients[k] * (t[w:-w, :, w:-w] if w else t)
    centre = filtered
    u_new = centre[:, :levels] - 0.5 * (phi[1:-1, :, 2:] - phi[1:-1, :, :-2])
    v_new = centre[:, levels : 2 * levels] - 0.5 * (phi[2:, :, 1:-1] - phi[:-2, :, 1:-1])
    t_new = centre[:, 2 * levels :] - phi[1:-1, :, 1:-1]
    return jnp.stack([u_new, v_new, t_new], axis=1)


def solution(mesh):
    in_specs = (
        P("lat", None, None, "lon"),
        P("lat", None, "lon"),
        P("lon", "lat", None),
        P("lon", "lat"),
        P(),
        P("lat", None, "lon"),
    )
    out_specs = P("lat", None, None, "lon")
    return jax.shard_map(shards, mesh=mesh, in_specs=in_specs, out_specs=out_specs, check_vma=False)
```

time: 1260 us -> 240 us (0.19)
  blocking collectives: 604 us -> 31.5 us
  waiting for transfers between devices: 370 us -> 57 us
  starting transfers between devices: 85.5 us -> 42.1 us
  local copies, waits for them, and re-layouts: 76.8 us -> 41.1 us
  other arithmetic: 67.8 us -> 40.1 us
  matrix products: 20.7 us -> 6.6 us
    psum x9 -> x0, blocking collectives: 584 us -> none  [the longest x5 318 us: squares(): return lax.psum(jnp.sum(residual * residual), ('lon', 'lat'))]
    psum x1 -> x0, waiting for transfers between devices: 312 us -> none  [shards(): spectrum = lax.psum(partial_spectrum, 'lon')]
    ppermute x28 -> x8, starting transfers between devices: 79.7 us -> 27.8 us  [the longest x4 14.2 us: neighbours(): lax.ppermute(lax.slice_in_dim(block, 0, width, axis=dim), axis, backward)]
    reduce_sum x10 -> x4, other arithmetic: 32.3 us -> 5.63 us  [the longest x1 3.73 us: shards(): cross = [jnp.sum(cores[k] * cores[k + 1]) for k in range(ITERS)]]
    mul x0 -> x7, other arithmetic: none -> 19.3 us  [the longest x5 14.9 us: shards(): following = following * inside[cut:-cut]]
    slice x20 -> x10, local copies, waits for them, and re-layouts: 34.3 us -> 15.8 us  [the longest x3 9.05 us: neighbours(): lax.slice_in_dim(block, size - width, size, axis=dim)]
    ppermute x14 -> x4, local copies, waits for them, and re-layouts: 21.7 us -> 6.44 us  [the longest x2 3.64 us: neighbours(): lax.ppermute(lax.slice_in_dim(block, 0, width, axis=dim), axis, backward)]
    ppermute x28 -> x8, waiting for transfers between devices: 19.9 us -> 5.77 us  [the longest x4 5.76 us: neighbours(): lax.ppermute(lax.slice_in_dim(block, 0, width, axis=dim), axis, backward)]
  transfers between devices with their start and end apart: 30 -> 11, of which waited for: 12 -> 4; matrix products, arithmetic and copies ran while one was open for 2% -> 13% of each run, Pallas kernels for 0% -> 0%
where the time goes in v1:
time: 240 us; the launch traced here: 239 us
  waiting for transfers between devices  57 us (24%)
  starting transfers between devices  42.1 us (18%)
  local copies, waits for them, and re-layouts  41.1 us (17%)
  other arithmetic  40.1 us (17%)
  blocking collectives  31.5 us (13%)
  between operations  20.3 us (8%)
  matrix products  6.6 us (3%)
    all_to_all x3, waiting for transfers between devices, exchange(): return lax.all_to_all(block, axes, split_axis=0, concat_axis=0, tiled=True)  51.2 us
    all_to_all x2, blocking collectives, exchange(): return lax.all_to_all(block, axes, split_axis=0, concat_axis=0, tiled=True)  31.5 us
    mul x5, other arithmetic, shards(): following = following * inside[cut:-cut]  14.9 us
    all_to_all x3, starting transfers between devices, exchange(): return lax.all_to_all(block, axes, split_axis=0, concat_axis=0, tiled=True)  14.3 us
    ppermute x4, starting transfers between devices, neighbours(): lax.ppermute(lax.slice_in_dim(block, 0, width, axis=dim), axis, backward)  14.2 us
    ppermute x4, starting transfers between devices, neighbours(): lax.ppermute(lax.slice_in_dim(block, size - width, size, axis=dim), axis,...  13.7 us
    slice x3, local copies, waits for them, and re-layouts, neighbours(): lax.slice_in_dim(block, size - width, size, axis=dim)  9.05 us
    another operation x1, local copies, waits for them, and re-layouts, shards(): moments = jnp.stack(squares + cross)  6.16 us
  transfers between devices with their start and end apart: 11, of which 4 were waited for; matrix products, arithmetic and copies ran while one was open for 13% of the time, Pallas kernels for 0%

profile of v1, /device:TPU:1, one launch (start us, length us, event | category | flops | bytes accessed | tf_op | source)
XLA Modules:
  0.0 238.8 jit_solution(3203766274965766331)
XLA Ops:
  0.0 1.0 convert_reduce_fusion
  1.0 0.8 select_reduce_fusion.1
  1.9 20.8 %all_to_all.33 = s32[128,1,2]{2,1,0:T(1,128)S(1)} all-to-all(s32[128,1,2]{2,1,0:T(1,128)S(1)} %copy.75), channel_id=1, replica_groups=mesh['lon'=32,'lat'=4] {'lon','lat'}, dimensions={0} | all-to-all | bytes 2048 | tf_op jit(solution)/shard_map/all_to_all | solution.py:27
  22.9 2.6 %gather_fusion = bf16[256,3,16,128]{3,2,1,0:T(8,128)(2,1)} fusion(bf16[128,3,16,128]{3,2,1,0:T(8,128)(2,1)S(1)} %copy-done, s32[1024]{0:T(1024)S(1)} %pad_clamp_fusion), kind=kCustom, calls=%fused_computation | custom fusion | bytes 6292480 | tf_op jit(solution)/shard_map/gather | solution.py:41
  25.5 5.7 %all-to-all-start.1 = ((bf16[128,2,3,16,128]{4,3,2,1,0:T(8,128)(2,1)}), bf16[128,2,3,16,128]{4,3,2,1,0:T(8,128)(2,1)}, u32[]{:S(2)}, u32[]{:S(2)}) async-start(bf16[128,2,3,16,128]{4,3,2,1,0:T(8,128)(2,1)} %bitcast.70), calls=%async_computation.1 | async-start | bytes 6291456 | tf_op jit(solution)/shard_map/all_to_all | solution.py:27
  31.2 41.6 %all-to-all-done.1 = bf16[128,2,3,16,128]{4,3,2,1,0:T(8,128)(2,1)} async-done(((bf16[128,2,3,16,128]{4,3,2,1,0:T(8,128)(2,1)}), bf16[128,2,3,16,128]{4,3,2,1,0:T(8,128)(2,1)}, u32[]{:S(2)}, u32[]{:S(2)}) %all-to-all-start.1) | async-done | bytes 3145760 | tf_op jit(solution)/shard_map/all_to_all | solution.py:27
  72.8 2.9 %gather_fusion.1 = bf16[128,3,16,128]{3,2,1,0:T(8,128)(2,1)S(1)} fusion(bf16[128,2,3,16,128]{4,3,2,1,0:T(8,128)(2,1)} %all-to-all-done.1, s32[128]{0:T(128)S(1)} %fusion.67), kind=kCustom, calls=%fused_computation.1 | custom fusion | bytes 3146752 | tf_op jit(solution)/shard_map/gather | solution.py:43
  75.7 3.4 %fusion.71 = f32[128,48,128]{2,1,0:T(8,128)S(1)} fusion(bf16[128,48,128]{2,1,0:T(8,128)(2,1)S(1)} %bitcast.71, bf16[128,128,128]{2,1,0:T(8,128)(2,1)} %param.16), kind=kOutput, calls=%fused_computation.143 | convolution fusion | flops 201326592 | bytes 8912896 | tf_op jit(solution)/shard_map/bci,bij->bcj/dot_general | solution.py:121
  79.2 1.7 copy-done.4
  80.9 0.8 constant_dynamic-slice_fusion
  81.6 4.0 %all-to-all-start.2 = ((f32[32,24,128]{2,1,0:T(8,128)}), f32[32,24,128]{2,1,0:T(8,128)S(1)}, u32[]{:S(2)}, u32[]{:S(2)}) async-start(f32[32,24,128]{2,1,0:T(8,128)} %bitcast.12), calls=%async_computation.2 | async-start | bytes 786432 | tf_op jit(solution)/shard_map/all_to_all | solution.py:27
  85.7 0.6 dynamic_slice.7
  86.9 0.6 or_select_fusion
  87.4 7.4 %all-to-all-done.2 = f32[32,24,128]{2,1,0:T(8,128)S(1)} async-done(((f32[32,24,128]{2,1,0:T(8,128)}), f32[32,24,128]{2,1,0:T(8,128)S(1)}, u32[]{:S(2)}, u32[]{:S(2)}) %all-to-all-start.2) | async-done | bytes 393248 | tf_op jit(solution)/shard_map/all_to_all | solution.py:27
  94.9 0.4 fusion.42
  95.3 0.5 multiply_add_fusion
  95.9 0.6 convolution_multiply_fusion
  96.5 0.7 fusion.36
  97.2 0.5 fusion.47
  97.7 0.5 fusion.22
  98.2 1.0 copy.81
  99.2 4.6 %all-to-all-start.3 = ((f32[32,24,128]{2,1,0:T(8,128)}), f32[32,24,128]{2,1,0:T(8,128)}, u32[]{:S(2)}, u32[]{:S(2)}) async-start(f32[32,24,128]{2,1,0:T(8,128)} %copy.81), calls=%async_computation.3 | async-start | bytes 786432 | tf_op jit(solution)/shard_map/all_to_all | solution.py:27
  104.2 0.4 copy.95
  104.6 1.1 collective-permute-start.4
  105.7 0.4 copy.96
  106.1 4.7 %collective-permute-start.5 = (f32[128,16,6]{0,1,2:T(8,128)S(1)}, f32[128,16,6]{0,1,2:T(8,128)S(1)}, u32[]{:S(2)}, u32[]{:S(2)}) collective-permute-start(f32[128,16,6]{0,1,2:T(8,128)S(1)} %copy.96), channel_id=1, source_target_pairs={{4,0},{8,4},{12,8},{16,12},{20,16},{24,20},{28,24},{32,28},{36,32}... | collective-permute-start | bytes 147464 | tf_op jit(solution)/shard_map/ppermute | solution.py:18
  110.8 2.2 all-to-all-done.3
  113.0 1.8 fusion.39
  114.8 6.3 %fusion.68 = (f32[128,48,6]{2,1,0:T(8,128)}, f32[128,48,6]{2,1,0:T(8,128)}) fusion(f32[128,48,128]{2,1,0:T(8,128)} %fusion.39), kind=kLoop, calls=%fused_computation.140 | loop fusion | bytes 589824 | tf_op jit(solution)/shard_map/slice | solution.py:17
  121.1 2.4 %copy.82 = f32[128,48,6]{0,1,2:T(8,128)S(1)} copy(f32[128,48,6]{2,1,0:T(8,128)} %get-tuple-element.26) | data formatting | bytes 294912 | tf_op jit(solution)/shard_map/slice | solution.py:17
  123.5 0.6 collective-permute-start
  124.1 3.0 %copy.83 = f32[128,48,6]{0,1,2:T(8,128)} copy(f32[128,48,6]{2,1,0:T(8,128)} %get-tuple-element.27) | data formatting | bytes 294912 | tf_op jit(solution)/shard_map/slice | solution.py:18
  127.1 5.4 %collective-permute-start.1 = (f32[128,48,6]{0,1,2:T(8,128)}, f32[128,48,6]{0,1,2:T(8,128)}, u32[]{:S(2)}, u32[]{:S(2)}) collective-permute-start(f32[128,48,6]{0,1,2:T(8,128)} %copy.83), channel_id=1, source_target_pairs={{4,0},{8,4},{12,8},{16,12},{20,16},{24,20},{28,24},{32,28},{36,32}... | collective-permute-start | bytes 442376 | tf_op jit(solution)/shard_map/ppermute | solution.py:18
  132.5 0.6 slice_multiply_fusion.7
  133.1 0.6 slice.276
  133.7 0.6 slice.297
  134.4 0.6 slice.306
  135.0 0.6 slice.315
  135.6 0.5 slice.322
  136.2 0.5 copy.88
  136.7 0.5 copy.89
  137.3 0.8 pad_maximum_fusion.8
  138.0 6.8 %collective-permute-start.6 = (f32[6,16,140]{2,1,0:T(8,128)}, f32[6,16,140]{2,1,0:T(8,128)}, u32[]{:S(2)}, u32[]{:S(2)}) collective-permute-start(f32[6,16,140]{2,1,0:T(8,128)} %get-tuple-element.24), channel_id=1, source_target_pairs={{0,1},{1,2},{2,3},{4,5},{5,6},{6,7},{8,9},{9,10},{10,11},{12,13},{... | collective-permute-start | bytes 161288 | tf_op jit(solution)/shard_map/ppermute | solution.py:17
  144.8 1.9 collective-permute-start.7
  146.7 2.3 copy.84
  149.0 3.1 %copy.85 = f32[128,48,6]{2,1,0:T(8,128)} copy(f32[128,48,6]{0,1,2:T(8,128)} %collective-permute-done.1) | data formatting | bytes 294912 | tf_op jit(solution)/shard_map/ppermute | solution.py:18
  152.1 1.7 pad_maximum_fusion.5
  153.8 5.3 %collective-permute-start.2 = (f32[6,48,140]{2,1,0:T(8,128)S(1)}, f32[6,48,140]{2,1,0:T(8,128)S(1)}, u32[]{:S(2)}, u32[]{:S(2)}) collective-permute-start(f32[6,48,140]{2,1,0:T(8,128)S(1)} %get-tuple-element.19), channel_id=1, source_target_pairs={{0,1},{1,2},{2,3},{4,5},{5,6},{6,7},{8,9},{9,10},{10,11},{12,13},{... | collective-permute-start | bytes 483848 | tf_op jit(solution)/shard_map/ppermute | solution.py:17
  159.1 2.2 collective-permute-start.3
  161.3 1.8 fusion
  163.2 5.8 %collective-permute-done.3 = f32[6,48,140]{2,1,0:T(8,128)S(1)} collective-permute-done((f32[6,48,140]{2,1,0:T(8,128)S(1)}, f32[6,48,140]{2,1,0:T(8,128)S(1)}, u32[]{:S(2)}, u32[]{:S(2)}) %collective-permute-start.3) | collective-permute-done | bytes 161312 | tf_op jit(solution)/shard_map/ppermute | solution.py:18
  168.9 3.1 %pad_maximum_fusion = f32[140,48,140]{2,1,0:T(8,128)S(1)} fusion(f32[6,48,140]{2,1,0:T(8,128)S(1)} %collective-permute-done.3, f32[128,48,6]{2,1,0:T(8,128)S(1)} %copy-done.10, f32[128,48,128]{2,1,0:T(8,128)S(1)} %copy-done.5, f32[128,48,6]{2,1,0:T(8,128)S(1)} %copy-done.9, f32[6,48,140]{2,1,0:T(8,128)S(1)} %collective-permute-done.2), kind=kLoop, calls=%fused_computation.2 | loop fusion | flops 3763200 | bytes 7526400 | tf_op jit(solution)/shard_map/concatenate | solution.py:19
  172.0 2.6 %fusion.4 = f32[138,16,138]{2,1,0:T(8,128)S(1)} fusion(f32[140,48,140]{2,1,0:T(8,128)S(1)} %pad_maximum_fusion, f32[138]{0:T(256)S(1)} %copy-done.25), kind=kLoop, calls=%fused_computation.10 | loop fusion | flops 1828224 | bytes 7313448 | tf_op jit(solution)/shard_map/mul | solution.py:142
  174.6 3.2 %fusion.7 = f32[136,16,136]{2,1,0:T(8,128)S(1)} fusion(f32[138,16,138]{2,1,0:T(8,128)S(1)} %fusion.4, f32[140,16,140]{2,1,0:T(8,128)S(1)} %fusion, f32[136]{0:T(256)S(1)} %copy-done.23), kind=kLoop, calls=%fused_computation.15 | loop fusion | flops 2071552 | bytes 8286752 | tf_op jit(solution)/shard_map/mul | solution.py:151
  177.9 3.8 %fusion.8 = f32[134,16,134]{2,1,0:T(8,128)S(1)} fusion(f32[138,16,138]{2,1,0:T(8,128)S(1)} %fusion.4, f32[136,16,136]{2,1,0:T(8,128)S(1)} %fusion.7, f32[140,16,140]{2,1,0:T(8,128)S(1)} %fusion, f32[134]{0:T(256)S(1)} %copy-done.24), kind=kLoop, calls=%fused_computation.20 | loop fusion | flops 2298368 | bytes 9194008 | tf_op jit(solution)/shard_map/mul | solution.py:151
  181.7 3.7 %fusion.11 = f32[132,16,132]{2,1,0:T(8,128)S(1)} fusion(f32[136,16,136]{2,1,0:T(8,128)S(1)} %fusion.7, f32[134,16,134]{2,1,0:T(8,128)S(1)} %fusion.8, f32[140,16,140]{2,1,0:T(8,128)S(1)} %fusion, f32[132]{0:T(256)S(1)} %copy-done.22), kind=kLoop, calls=%fused_computation.28 | loop fusion | flops 2230272 | bytes 8921616 | tf_op jit(solution)/shard_map/mul | solution.py:151
  185.4 3.6 %fusion.21 = f32[130,16,130]{2,1,0:T(8,128)S(1)} fusion(f32[132,16,132]{2,1,0:T(8,128)S(1)} %fusion.11, f32[140,16,140]{2,1,0:T(8,128)S(1)} %fusion, f32[134,16,134]{2,1,0:T(8,128)S(1)} %fusion.8, f32[130]{0:T(256)S(1)} %copy-done.21), kind=kLoop, calls=%fused_computation.45 | loop fusion | flops 2163200 | bytes 8653320 | tf_op jit(solution)/shard_map/mul | solution.py:151
  189.1 3.7 %fusion.35 = (f32[]{:T(128)}, f32[]{:T(128)}, f32[]{:T(128)}, f32[]{:T(128)}, f32[]{:T(128)}, /*index=5*/f32[]{:T(128)}, f32[]{:T(128)}, f32[]{:T(128)}, f32[]{:T(128)}, f32[]{:T(128)}) fusion(f32[130,16,130]{2,1,0:T(8,128)S(1)} %fusion.21, f32[140,16,140]{2,1,0:T(8,128)S(1)} %fusion, f32[132,16,132]{2,1,0:T(8,128)S(1)} %fusion.11, f32[128]{0:T(128)S(1)} %copy-done.26, ...), kind=kLoop, calls=%fused_computation.68 | loop fusion | flops 7340022 | bytes 10486312 | tf_op jit(solution)/shard_map/reduce_sum | solution.py:158
  192.8 6.2 %stack.67 = f32[10]{0:T(128)S(1)} concatenate(f32[1]{0:T(128)} %bitcast.21, f32[1]{0:T(128)} %bitcast.22, f32[1]{0:T(128)} %bitcast.23, f32[1]{0:T(128)} %bitcast.24, f32[1]{0:T(128)} %bitcast.25, f32[1]{0:T(128)} %bitcast.26, f32[1]{0:T(128)} %bitcast.27, f32[1]{0:T(128)} %bitcast.28, f32[1]{0:T(128)} %bitcast.29, f32[1]{0:T(128)} %bitcast.30), dimensions={0} | concatenate | bytes 80 | tf_op jit(solution)/shard_map/stack | solution.py:159
  199.0 10.7 %all_to_all.34 = f32[128,1,10]{2,1,0:T(1,128)S(1)} all-to-all(f32[128,1,10]{2,1,0:T(1,128)S(1)} %broadcast_in_dim.23), channel_id=1, replica_groups=mesh['lon'=32,'lat'=4] {'lon','lat'}, dimensions={0} | all-to-all | bytes 10240 | tf_op jit(solution)/shard_map/all_to_all | solution.py:27
  209.8 0.7 fusion.70
  229.6 5.9 %fusion.17 = f32[130,16,130]{2,1,0:T(8,128)S(1)} fusion(f32[136,16,136]{2,1,0:T(8,128)} %copy-done.2, f32[138,16,138]{2,1,0:T(8,128)S(1)} %fusion.4, f32[130,16,130]{2,1,0:T(8,128)} %copy-done.8, f32[134,16,134]{2,1,0:T(8,128)} %copy-done.3, f32[132,16,132]{2,1,0:T(8,128)} %copy-done.7, f32[]{:T(128)S(6)} %mul.1698, f32[]{:T(128)S(6)} %add.987, ...), kind=kLoop, calls=%fused_computation.39 | loop fusion | flops 2433600 | bytes 6489620 | tf_op jit(solution)/shard_map/add | solution.py:166
  235.5 1.1 fusion.29
  236.9 1.9 copy.91
  (78 shorter events, 1.2 us)
Async XLA Ops:
  0.0 22.9 %copy-start = (bf16[128,3,16,128]{3,2,1,0:T(8,128)(2,1)S(1)}, bf16[128,3,16,128]{3,2,1,0:T(8,128)(2,1)}, u32[]{:S(2)}) copy-start(bf16[128,3,16,128]{3,2,1,0:T(8,128)(2,1)} %param.15) | copy-start | bytes 4718596
  25.5 5.7 %copy-start.27 = (s32[1,128,1]{1,2,0:T(1,128)S(1)}, s32[1,128,1]{1,2,0:T(1,128)}, u32[]{:S(2)}) copy-start(s32[1,128,1]{1,2,0:T(1,128)} %param.17) | copy-start | bytes 1540
  25.5 47.3 %all-to-all-start.1 = ((bf16[128,2,3,16,128]{4,3,2,1,0:T(8,128)(2,1)}), bf16[128,2,3,16,128]{4,3,2,1,0:T(8,128)(2,1)}, u32[]{:S(2)}, u32[]{:S(2)}) async-start(bf16[128,2,3,16,128]{4,3,2,1,0:T(8,128)(2,1)} %bitcast.70), calls=%async_computation.1 | async-start | bytes 6291456 | tf_op jit(solution)/shard_map/all_to_all | solution.py:27
  75.7 10.0 %copy-start.28 = (s32[32]{0:T(128)S(1)}, s32[32]{0:T(128)}, u32[]{:S(2)}) copy-start(s32[32]{0:T(128)} %param.19) | copy-start | bytes 388
  75.7 11.1 %copy-start.18 = (s32[17,128]{1,0:T(8,128)S(1)}, s32[17,128]{1,0:T(8,128)}, u32[]{:S(2)}) copy-start(s32[17,128]{1,0:T(8,128)} %constant.114.clone) | copy-start | bytes 26116
  75.7 19.2 %copy-start.20 = (f32[17,32,1]{1,0,2:T(8,128)S(1)}, f32[17,32,1]{1,0,2:T(8,128)}, u32[]{:S(2)}) copy-start(f32[17,32,1]{1,0,2:T(8,128)} %constant.132) | copy-start | bytes 6532
  79.2 1.7 copy-start.4
  80.9 14.5 %copy-start.14 = (f32[17,128]{1,0:T(8,128)S(1)}, f32[17,128]{1,0:T(8,128)}, u32[]{:S(2)}) copy-start(f32[17,128]{1,0:T(8,128)} %constant.110.clone) | copy-start | bytes 26116
  80.9 14.5 %copy-start.15 = (f32[17,128]{1,0:T(8,128)S(1)}, f32[17,128]{1,0:T(8,128)}, u32[]{:S(2)}) copy-start(f32[17,128]{1,0:T(8,128)} %constant.111.clone) | copy-start | bytes 26116
  80.9 14.5 %copy-start.17 = (f32[17,32,1]{1,0,2:T(8,128)S(1)}, f32[17,32,1]{1,0,2:T(8,128)}, u32[]{:S(2)}) copy-start(f32[17,32,1]{1,0,2:T(8,128)} %constant.133) | copy-start | bytes 6532
  81.6 14.2 %copy-start.12 = (f32[256,256,1]{1,0,2:T(8,128)S(1)}, f32[256,256,1]{1,0,2:T(8,128)}, u32[]{:S(2)}) copy-start(f32[256,256,1]{1,0,2:T(8,128)} %constant.134) | copy-start | bytes 786436
  81.6 13.2 %all-to-all-start.2 = ((f32[32,24,128]{2,1,0:T(8,128)}), f32[32,24,128]{2,1,0:T(8,128)S(1)}, u32[]{:S(2)}, u32[]{:S(2)}) async-start(f32[32,24,128]{2,1,0:T(8,128)} %bitcast.12), calls=%async_computation.2 | async-start | bytes 786432 | tf_op jit(solution)/shard_map/all_to_all | solution.py:27
  85.6 10.8 %copy-start.13 = (f32[256,256,1]{1,0,2:T(8,128)S(1)}, f32[256,256,1]{1,0,2:T(8,128)}, u32[]{:S(2)}) copy-start(f32[256,256,1]{1,0,2:T(8,128)} %constant.135) | copy-start | bytes 786436
  95.3 1.8 copy-start.19
  95.8 1.9 copy-start.16
  96.5 7.4 %copy-start.11 = (f32[128,16,128]{2,1,0:T(8,128)S(1)}, f32[128,16,128]{2,1,0:T(8,128)}, u32[]{:S(2)}) copy-start(f32[128,16,128]{2,1,0:T(8,128)} %param.20) | copy-start | bytes 3145732
  99.2 13.8 %all-to-all-start.3 = ((f32[32,24,128]{2,1,0:T(8,128)}), f32[32,24,128]{2,1,0:T(8,128)}, u32[]{:S(2)}, u32[]{:S(2)}) async-start(f32[32,24,128]{2,1,0:T(8,128)} %copy.81), calls=%async_computation.3 | async-start | bytes 786432 | tf_op jit(solution)/shard_map/all_to_all | solution.py:27
  104.6 31.6 %collective-permute-start.4 = (f32[128,16,6]{0,1,2:T(8,128)S(1)}, f32[128,16,6]{0,1,2:T(8,128)S(1)}, u32[]{:S(2)}, u32[]{:S(2)}) collective-permute-start(f32[128,16,6]{0,1,2:T(8,128)S(1)} %copy.95), channel_id=1, source_target_pairs={{0,4},{4,8},{8,12},{12,16},{16,20},{20,24},{24,28},{28,32},{32,36}... | collective-permute-start | bytes 147464 | tf_op jit(solution)/shard_map/ppermute | solution.py:17
  106.1 30.6 %collective-permute-start.5 = (f32[128,16,6]{0,1,2:T(8,128)S(1)}, f32[128,16,6]{0,1,2:T(8,128)S(1)}, u32[]{:S(2)}, u32[]{:S(2)}) collective-permute-start(f32[128,16,6]{0,1,2:T(8,128)S(1)} %copy.96), channel_id=1, source_target_pairs={{4,0},{8,4},{12,8},{16,12},{20,16},{24,20},{28,24},{32,28},{36,32}... | collective-permute-start | bytes 147464 | tf_op jit(solution)/shard_map/ppermute | solution.py:18
  123.5 23.2 %collective-permute-start = (f32[128,48,6]{0,1,2:T(8,128)S(1)}, f32[128,48,6]{0,1,2:T(8,128)S(1)}, u32[]{:S(2)}, u32[]{:S(2)}) collective-permute-start(f32[128,48,6]{0,1,2:T(8,128)S(1)} %copy.82), channel_id=1, source_target_pairs={{0,4},{4,8},{8,12},{12,16},{16,20},{20,24},{24,28},{28,32},{32,36}... | collective-permute-start | bytes 442376 | tf_op jit(solution)/shard_map/ppermute | solution.py:17
  127.1 21.9 %collective-permute-start.1 = (f32[128,48,6]{0,1,2:T(8,128)}, f32[128,48,6]{0,1,2:T(8,128)}, u32[]{:S(2)}, u32[]{:S(2)}) collective-permute-start(f32[128,48,6]{0,1,2:T(8,128)} %copy.83), channel_id=1, source_target_pairs={{4,0},{8,4},{12,8},{16,12},{20,16},{24,20},{28,24},{32,28},{36,32}... | collective-permute-start | bytes 442376 | tf_op jit(solution)/shard_map/ppermute | solution.py:18
  138.0 23.3 %collective-permute-start.6 = (f32[6,16,140]{2,1,0:T(8,128)}, f32[6,16,140]{2,1,0:T(8,128)}, u32[]{:S(2)}, u32[]{:S(2)}) collective-permute-start(f32[6,16,140]{2,1,0:T(8,128)} %get-tuple-element.24), channel_id=1, source_target_pairs={{0,1},{1,2},{2,3},{4,5},{5,6},{6,7},{8,9},{9,10},{10,11},{12,13},{... | collective-permute-start | bytes 161288 | tf_op jit(solution)/shard_map/ppermute | solution.py:17
  144.8 16.5 %collective-permute-start.7 = (f32[6,16,140]{2,1,0:T(8,128)S(1)}, f32[6,16,140]{2,1,0:T(8,128)}, u32[]{:S(2)}, u32[]{:S(2)}) collective-permute-start(f32[6,16,140]{2,1,0:T(8,128)S(1)} %get-tuple-element.25), channel_id=1, source_target_pairs={{1,0},{2,1},{3,2},{5,4},{6,5},{7,6},{9,8},{10,9},{11,10},{13,12},{... | collective-permute-start | bytes 161288 | tf_op jit(solution)/shard_map/ppermute | solution.py:18
  152.1 16.8 %copy-start.9 = (f32[128,48,6]{2,1,0:T(8,128)S(1)}, f32[128,48,6]{2,1,0:T(8,128)}, u32[]{:S(2)}) copy-start(f32[128,48,6]{2,1,0:T(8,128)} %copy.84) | copy-start | bytes 442372
  152.1 16.8 %copy-start.10 = (f32[128,48,6]{2,1,0:T(8,128)S(1)}, f32[128,48,6]{2,1,0:T(8,128)}, u32[]{:S(2)}) copy-start(f32[128,48,6]{2,1,0:T(8,128)} %copy.85) | copy-start | bytes 442372
  153.8 9.3 %collective-permute-start.2 = (f32[6,48,140]{2,1,0:T(8,128)S(1)}, f32[6,48,140]{2,1,0:T(8,128)S(1)}, u32[]{:S(2)}, u32[]{:S(2)}) collective-permute-start(f32[6,48,140]{2,1,0:T(8,128)S(1)} %get-tuple-element.19), channel_id=1, source_target_pairs={{0,1},{1,2},{2,3},{4,5},{5,6},{6,7},{8,9},{9,10},{10,11},{12,13},{... | collective-permute-start | bytes 483848 | tf_op jit(solution)/shard_map/ppermute | solution.py:17
  159.1 9.8 %copy-start.5 = (f32[128,48,128]{2,1,0:T(8,128)S(1)}, f32[128,48,128]{2,1,0:T(8,128)}, u32[]{:S(2)}) copy-start(f32[128,48,128]{2,1,0:T(8,128)} %fusion.39) | copy-start | bytes 9437188
  159.1 9.8 %collective-permute-start.3 = (f32[6,48,140]{2,1,0:T(8,128)S(1)}, f32[6,48,140]{2,1,0:T(8,128)S(1)}, u32[]{:S(2)}, u32[]{:S(2)}) collective-permute-start(f32[6,48,140]{2,1,0:T(8,128)S(1)} %get-tuple-element.20), channel_id=1, source_target_pairs={{1,0},{2,1},{3,2},{5,4},{6,5},{7,6},{9,8},{10,9},{11,10},{13,12},{... | collective-permute-start | bytes 483848 | tf_op jit(solution)/shard_map/ppermute | solution.py:18
  163.2 8.9 %copy-start.25 = (f32[138]{0:T(256)S(1)}, f32[138]{0:T(256)}, u32[]{:S(2)}) copy-start(f32[138]{0:T(256)} %slice.276) | copy-start | bytes 1660
  172.0 2.6 %copy-start.23 = (f32[136]{0:T(256)S(1)}, f32[136]{0:T(256)}, u32[]{:S(2)}) copy-start(f32[136]{0:T(256)} %slice_multiply_fusion.7) | copy-start | bytes 1636
  174.6 3.2 %copy-start.24 = (f32[134]{0:T(256)S(1)}, f32[134]{0:T(256)}, u32[]{:S(2)}) copy-start(f32[134]{0:T(256)} %slice.297) | copy-start | bytes 1612
  177.9 11.2 %copy-start.2 = (f32[136,16,136]{2,1,0:T(8,128)}, f32[136,16,136]{2,1,0:T(8,128)S(1)}, u32[]{:S(2)}) copy-start(f32[136,16,136]{2,1,0:T(8,128)S(1)} %fusion.7) | copy-start | bytes 3551236
  177.9 3.8 %copy-start.22 = (f32[132]{0:T(256)S(1)}, f32[132]{0:T(256)}, u32[]{:S(2)}) copy-start(f32[132]{0:T(256)} %slice.306) | copy-start | bytes 1588
  181.6 7.4 %copy-start.3 = (f32[134,16,134]{2,1,0:T(8,128)}, f32[134,16,134]{2,1,0:T(8,128)S(1)}, u32[]{:S(2)}) copy-start(f32[134,16,134]{2,1,0:T(8,128)S(1)} %fusion.8) | copy-start | bytes 3447556
  181.6 3.7 %copy-start.21 = (f32[130]{0:T(256)S(1)}, f32[130]{0:T(256)}, u32[]{:S(2)}) copy-start(f32[130]{0:T(256)} %slice.315) | copy-start | bytes 1564
  185.3 3.7 %copy-start.7 = (f32[132,16,132]{2,1,0:T(8,128)}, f32[132,16,132]{2,1,0:T(8,128)S(1)}, u32[]{:S(2)}) copy-start(f32[132,16,132]{2,1,0:T(8,128)S(1)} %fusion.11) | copy-start | bytes 3345412
  185.4 3.7 %copy-start.26 = (f32[128]{0:T(128)S(1)}, f32[128]{0:T(128)}, u32[]{:S(2)}) copy-start(f32[128]{0:T(128)} %slice.322) | copy-start | bytes 1540
  189.0 3.7 %copy-start.8 = (f32[130,16,130]{2,1,0:T(8,128)}, f32[130,16,130]{2,1,0:T(8,128)S(1)}, u32[]{:S(2)}) copy-start(f32[130,16,130]{2,1,0:T(8,128)S(1)} %fusion.21) | copy-start | bytes 3244804
  229.6 5.9 %copy-start.6 = (f32[128,48,128]{2,1,0:T(8,128)S(1)}, f32[128,48,128]{2,1,0:T(8,128)}, u32[]{:S(2)}) copy-start(f32[128,48,128]{2,1,0:T(8,128)} %fusion.39) | copy-start | bytes 9437188
  236.7 2.1 copy-start.1

commit v2 on v1

v2 whole, which is shorter than its diff:
```python
import functools

import numpy as np
import jax
import jax.numpy as jnp
from jax import lax
from jax.experimental import pallas as pl
from jax.experimental.pallas import tpu as pltpu
from jax.sharding import PartitionSpec as P

ITERS = 5
BOTH = ("lon", "lat")
HIGHEST = lax.Precision.HIGHEST
FIELD = 16
FIELDS = 8
F32 = jnp.float32
MIB = 1024 * 1024


def params(mib):
    return pltpu.CompilerParams(vmem_limit_bytes=mib * MIB)


def in_hbm(x):
    return pltpu.with_memory_space_constraint(x, pltpu.HBM)


def exchange(block, axes):
    return lax.all_to_all(block, axes, split_axis=0, concat_axis=0, tiled=True)


def lanes(shape):
    return lax.broadcasted_iota(jnp.int32, shape, len(shape) - 1)


def pack_lanes(shape, rows):
    field = lanes(shape) // FIELD
    packed = jnp.zeros(shape, F32)
    for f, row in enumerate(rows):
        packed = jnp.where(field == f, pltpu.roll(row, (FIELD * f + 8) % 128, len(shape) - 1), packed)
    return packed


def unpack_lanes(packed, f):
    return pltpu.roll(packed, (-(FIELD * f + 8)) % 128, packed.ndim - 1)


def request_kernel(row_ref, wanted_ref, request_ref, place_ref):
    row = row_ref[...]
    size = row.shape[1]
    down = lax.broadcasted_iota(jnp.int32, (size, size), 0)
    across = lax.broadcasted_iota(jnp.int32, (size, size), 1)
    owner = jnp.broadcast_to(row, (size, size))
    earlier = (owner.T == owner) & (down < across)
    slot = jnp.sum(jnp.where(earlier, 1.0, 0.0), axis=0, keepdims=True)
    wanted = wanted_ref[...].astype(F32)
    out = jnp.zeros((size, size), F32)
    for s in range(2):
        hit = jnp.where((owner == down) & (slot == s), wanted, 0.0)
        out = jnp.where(across == s, jnp.sum(hit, axis=1, keepdims=True), out)
    request_ref[...] = out.astype(jnp.int32)
    place_ref[...] = 2 * row + slot.astype(jnp.int32)


def make_requests(owner, wanted):
    rows = wanted.shape[1]
    return pl.pallas_call(
        request_kernel,
        out_shape=(
            jax.ShapeDtypeStruct((rows, rows), jnp.int32),
            jax.ShapeDtypeStruct((1, rows), jnp.int32),
        ),
        cost_estimate=pl.CostEstimate(flops=200000, bytes_accessed=200000, transcendentals=0),
        compiler_params=params(2),
        name="requests",
    )(in_hbm(owner), in_hbm(wanted))


def ways(axis, wrap):
    count = lax.axis_size(axis)
    up = [(i, (i + 1) % count) for i in range(count if wrap else count - 1)]
    return up, [(b, a) for a, b in up]


def from_sides(to_east, to_west):
    east, west = ways("lon", True)
    return lax.ppermute(to_east, "lon", east), lax.ppermute(to_west, "lon", west)


def from_ends(last, first):
    north, south = ways("lat", False)
    return lax.ppermute(last, "lat", north), lax.ppermute(first, "lat", south)


def low_half(x):
    return lanes(x.shape) % FIELD < FIELD // 2


def shift(x, by):
    return pltpu.roll(x, by % 128, x.ndim - 1)


def for_sides(even, odd):
    low = low_half(even)
    return jnp.where(low, even, shift(odd, 8)), jnp.where(low, shift(even, -8), odd)


def merge(from_west, from_east, parity):
    low = low_half(from_west)
    if parity == 0:
        return jnp.where(low, from_west, shift(from_east, 8))
    return jnp.where(low, shift(from_west, -8), from_east)


def caps_kernel(place_ref, info_ref, moved_hbm, weights_hbm, caps_ref, held, weights_ref, sems, weights_sem):
    polar = caps_ref.shape[0]
    start = info_ref[0]
    copies = [
        pltpu.make_async_copy(moved_hbm.at[place_ref[start + i]], held.at[i], sems.at[i]) for i in range(polar)
    ]
    load = pltpu.make_async_copy(weights_hbm.at[pl.ds(start, polar)], weights_ref, weights_sem)
    load.start()
    for copy in copies:
        copy.start()
    load.wait()
    for copy in copies:
        copy.wait()
    rows = [jnp.dot(held[i], weights_ref[i], preferred_element_type=F32) for i in range(polar)]
    for i, row in enumerate(rows):
        caps_ref[i] = row


def make_caps(place, info, moved, weights, polar):
    _, depth, points = moved.shape
    smem = pl.BlockSpec(memory_space=pltpu.SMEM)
    hbm = pl.BlockSpec(memory_space=pl.ANY)
    return pl.pallas_call(
        caps_kernel,
        in_specs=[smem, smem, hbm, hbm],
        out_specs=pl.BlockSpec(memory_space=pltpu.VMEM),
        out_shape=jax.ShapeDtypeStruct((polar, depth, points), F32),
        scratch_shapes=[
            pltpu.VMEM((polar, depth, points), moved.dtype),
            pltpu.VMEM((polar, points, points), weights.dtype),
            pltpu.SemaphoreType.DMA((polar,)),
            pltpu.SemaphoreType.DMA,
        ],
        cost_estimate=pl.CostEstimate(flops=30000000, bytes_accessed=1200000, transcendentals=0),
        compiler_params=params(4),
        name="caps",
    )(place, info, in_hbm(moved), in_hbm(weights))


def arrive_kernel(
    place_ref, moved_hbm, stiffness_hbm, weights_hbm, arrived_hbm, east_ref, west_ref, ends_ref,
    moved_ref, stiffness_ref, weights_ref, arrived_ref, load_sems, weight_sems, save_sems,
):
    rows, depth, _ = arrived_ref.shape
    group = 2 * FIELDS
    pieces = rows // group
    loads = [
        pltpu.make_async_copy(moved_hbm, moved_ref, load_sems.at[0]),
        pltpu.make_async_copy(stiffness_hbm, stiffness_ref, load_sems.at[1]),
    ]

    def fetch(g):
        part = pl.ds(g * group, group)
        return pltpu.make_async_copy(weights_hbm.at[part], weights_ref.at[part], weight_sems.at[g])

    def save(g):
        part = pl.ds(g * group, group)
        return pltpu.make_async_copy(arrived_ref.at[part], arrived_hbm.at[part], save_sems.at[g])

    loads[0].start()
    fetch(0).start()
    loads[1].start()
    for g in range(1, pieces):
        fetch(g).start()
    for load in loads:
        load.wait()

    def pair(g, carry):
        fetch(g).wait()
        first = g * group
        sources = [moved_ref[place_ref[first + i]] for i in range(2 * FIELDS)]
        stiff = [stiffness_ref[first + i] for i in range(2 * FIELDS)]
        values = [
            jnp.dot(source, weights_ref[first + i], preferred_element_type=F32) for i, source in enumerate(sources)
        ]
        packed = [pack_lanes(values[0].shape, values[h * FIELDS : (h + 1) * FIELDS]) for h in range(2)]
        packed_stiff = [pack_lanes(stiff[0].shape, stiff[h * FIELDS : (h + 1) * FIELDS]) for h in range(2)]
        east, west = for_sides(*packed)
        east_stiff, west_stiff = for_sides(*packed_stiff)
        for i, value in enumerate(values):
            arrived_ref[first + i] = value
        east_ref[g, 0:depth] = east
        west_ref[g, 0:depth] = west
        east_ref[g, depth:] = east_stiff
        west_ref[g, depth:] = west_stiff
        save(g).start()
        return carry

    lax.fori_loop(0, rows // (2 * FIELDS), pair, 0)
    for f in range(FIELDS):
        for end, row in enumerate((f, rows - FIELDS + f)):
            ends_ref[end, f, 0:depth] = arrived_ref[row]
            ends_ref[end, f, depth:] = stiffness_ref[row]
    for g in range(pieces):
        save(g).wait()


def make_arrived(place, moved, weights, stiffness):
    _, depth, points = moved.shape
    rows, levels, _ = stiffness.shape
    both = depth + levels
    vmem = pl.BlockSpec(memory_space=pltpu.VMEM)
    hbm = pl.BlockSpec(memory_space=pl.ANY)
    side = jax.ShapeDtypeStruct((rows // (2 * FIELDS), both, points), F32)
    return pl.pallas_call(
        arrive_kernel,
        in_specs=[pl.BlockSpec(memory_space=pltpu.SMEM), hbm, hbm, hbm],
        out_specs=[hbm] + [vmem] * 3,
        out_shape=(
            pltpu.HBM((rows, depth, points), F32), side, side,
            jax.ShapeDtypeStruct((2, FIELDS, both, points), F32),
        ),
        scratch_shapes=[
            pltpu.VMEM(moved.shape, moved.dtype),
            pltpu.VMEM(stiffness.shape, F32),
            pltpu.VMEM(weights.shape, weights.dtype),
            pltpu.VMEM((rows, depth, points), F32),
            pltpu.SemaphoreType.DMA((2,)),
            pltpu.SemaphoreType.DMA((rows // (2 * FIELDS),)),
            pltpu.SemaphoreType.DMA((rows // (2 * FIELDS),)),
        ],
        cost_estimate=pl.CostEstimate(flops=20000000000, bytes_accessed=30000000, transcendentals=0),
        compiler_params=params(18),
        name="arrive",
    )(place, in_hbm(moved), in_hbm(stiffness), in_hbm(weights))


def ends_kernel(ends_ref, west_ref, east_ref, last_ref, first_ref):
    pairs = west_ref.shape[0]
    first_ref[0:FIELDS] = ends_ref[0]
    last_ref[0:FIELDS] = ends_ref[1]
    first_ref[FIELDS] = merge(west_ref[0], east_ref[0], 0)
    last_ref[FIELDS] = merge(west_ref[pairs - 1], east_ref[pairs - 1], 1)


def make_ends(ends, west, east):
    _, _, both, points = ends.shape
    shape = jax.ShapeDtypeStruct((FIELDS + 1, both, points), F32)
    return pl.pallas_call(
        ends_kernel,
        out_shape=(shape, shape),
        cost_estimate=pl.CostEstimate(flops=100000, bytes_accessed=2000000, transcendentals=0),
        compiler_params=params(4),
        name="ends",
    )(ends, west, east)


def filter_tables(parts, points):
    total = parts * points
    half = parts // 2 + 1
    k1, p = np.arange(half), np.arange(points)
    twist = 2 * np.pi * np.outer(k1, p) / total
    inner = 2 * np.pi * np.outer(p, p) / points
    c, s = np.cos(inner), np.sin(inner)
    forward = np.block([[c, -s], [s, c]]).astype(np.float32)
    inverse = np.block([[c, s], [-s, c]]).astype(np.float32)
    return np.concatenate([np.cos(twist), np.sin(twist)]).astype(np.float32), forward, inverse


def filter_kernel(
    info_ref, lines_ref, twist_hbm, forward_hbm, inverse_hbm, out_ref,
    work, back, twist_ref, forward_ref, inverse_ref, sems,
):
    parts, count, points = lines_ref.shape
    pairs = [(twist_hbm, twist_ref), (forward_hbm, forward_ref), (inverse_hbm, inverse_ref)]
    loads = [pltpu.make_async_copy(a, b, sems.at[i]) for i, (a, b) in enumerate(pairs)]
    for load in loads:
        load.start()
    total = parts * points
    mid = parts // 2
    cutoff = info_ref[4]
    tiles = count // 8
    loads[0].wait()
    c = [float(np.cos(2 * np.pi * i / parts)) for i in range(parts)]
    s = [float(np.sin(2 * np.pi * i / parts)) for i in range(parts)]
    for t in range(tiles):
        x = [lines_ref[d, 8 * t : 8 * t + 8, :] for d in range(parts)]
        even = [x[d] + x[parts - d] for d in range(1, mid)]
        odd = [x[d] - x[parts - d] for d in range(1, mid)]
        for k in range(mid + 1):
            real = x[0] + x[mid] if k % 2 == 0 else x[0] - x[mid]
            for d in range(1, mid):
                real = real + c[d * k % parts] * even[d - 1]
            row = k * count + 8 * t
            tc, ts = twist_ref[k : k + 1, :], twist_ref[mid + 1 + k : mid + 2 + k, :]
            if k in (0, mid):
                work[row : row + 8, 0:points] = real * tc
                work[row : row + 8, points:] = -real * ts
            else:
                imag = sum(s[d * k % parts] * odd[d - 1] for d in range(1, mid))
                work[row : row + 8, 0:points] = real * tc - imag * ts
                work[row : row + 8, points:] = -imag * tc - real * ts
    loads[1].wait()
    spectrum = jnp.dot(work[...], forward_ref[...], precision=HIGHEST, preferred_element_type=F32)
    shape = spectrum.shape
    wave = lax.broadcasted_iota(jnp.int32, shape, 0) // count + parts * (lanes(shape) % points)
    kept = (wave <= cutoff) | (wave >= total - cutoff)
    spectrum = jnp.where(kept, spectrum * (1.0 / total), 0.0)
    loads[2].wait()
    back[...] = jnp.dot(spectrum, inverse_ref[...], precision=HIGHEST, preferred_element_type=F32)
    for t in range(tiles):
        real, imag = [], []
        for k in range(mid + 1):
            row = k * count + 8 * t
            br, bi = back[row : row + 8, 0:points], back[row : row + 8, points:]
            tc, ts = twist_ref[k : k + 1, :], twist_ref[mid + 1 + k : mid + 2 + k, :]
            if k in (0, mid):
                real.append(br * tc - bi * ts)
                imag.append(None)
            else:
                real.append(2.0 * (br * tc - bi * ts))
                imag.append(2.0 * (br * ts + bi * tc))
        for d in range(mid + 1):
            even = real[0] + real[mid] if d % 2 == 0 else real[0] - real[mid]
            for k in range(1, mid):
                even = even + c[d * k % parts] * real[k]
            if d in (0, mid):
                out_ref[d, 8 * t : 8 * t + 8, :] = even
            else:
                odd = sum(s[d * k % parts] * imag[k] for k in range(1, mid))
                out_ref[d, 8 * t : 8 * t + 8, :] = even - odd
                out_ref[parts - d, 8 * t : 8 * t + 8, :] = even + odd
    shape = (8, points)
    low = lanes(shape) < points // 2
    for d in range(parts):
        rows = [
            jnp.where(
                low,
                out_ref[(d + 1) % parts, 8 * t : 8 * t + 8, :],
                out_ref[(d - 1) % parts, 8 * t : 8 * t + 8, :],
            )
            for t in range(tiles)
        ]
        out_ref[d, count : count + 8, :] = pack_lanes(shape, rows)


def low_pass(info, lines):
    parts, count, points = lines.shape
    tables = filter_tables(parts, points)
    rows = (parts // 2 + 1) * count
    vmem = pl.BlockSpec(memory_space=pltpu.VMEM)
    return pl.pallas_call(
        filter_kernel,
        in_specs=[pl.BlockSpec(memory_space=pltpu.SMEM)] + [vmem] + [pl.BlockSpec(memory_space=pl.ANY)] * 3,
        out_specs=vmem,
        out_shape=pltpu.HBM((parts, count + 8, points), F32),
        scratch_shapes=[pltpu.VMEM((rows, 2 * points), F32)] * 2
        + [pltpu.VMEM(x.shape, F32) for x in tables]
        + [pltpu.SemaphoreType.DMA((3,))],
        cost_estimate=pl.CostEstimate(flops=700000000, bytes_accessed=1400000, transcendentals=0),
        compiler_params=params(8),
        name="low_pass",
    )(info, lines, *[in_hbm(jnp.asarray(x)) for x in tables])


def split(x):
    high = x.astype(jnp.bfloat16)
    return high, (x - high.astype(F32)).astype(jnp.bfloat16)


def shift_matrix(rows, columns, left, right):
    source = lax.broadcasted_iota(jnp.int32, (rows, columns), 0)
    target = lax.broadcasted_iota(jnp.int32, (rows, columns), 1)
    west = (source + 1 == target) | ((source == rows - 1) & (target == 0))
    east = (source == target + 1) | ((source == 0) & (target == rows - 1))
    return (jnp.where(west, left, 0.0) + jnp.where(east, right, 0.0)).astype(jnp.bfloat16)


def shifted(x, matrix):
    flat = x.reshape(-1, x.shape[-1])
    high, low = split(flat)
    count = flat.shape[0]
    both = jnp.dot(jnp.concatenate([high, low], axis=0), matrix, preferred_element_type=F32)
    out = both[:count] + both[count:]
    return out.reshape(x.shape[:-1] + (matrix.shape[1],))


def basis_kernel(
    info_ref, arrived_hbm, west_hbm, east_hbm, above_hbm, below_hbm, stiffness_hbm, smooth_ref,
    filtered_hbm, t0, t1, t2, t3, t4, moments_ref,
    edge, filtered_ref, slope_ref, west_ref, east_ref, above_ref, below_ref, stiffness_ref, sems,
):
    rows, depth, points = filtered_ref.shape
    levels = depth // 3
    span = 2 * points
    groups = rows // FIELDS
    polar = smooth_ref.shape[0] // 2
    table = [t0, t1, t2, t3, t4]
    start, is_polar = info_ref[0], info_ref[1]
    top, bottom = info_ref[2].astype(F32), info_ref[3].astype(F32)
    stride = 32
    pairs = [
        (west_hbm, west_ref), (east_hbm, east_ref), (stiffness_hbm, stiffness_ref), (above_hbm, above_ref),
        (below_hbm, below_ref), (arrived_hbm, filtered_ref),
    ]
    loads = [pltpu.make_async_copy(a, b, sems.at[i]) for i, (a, b) in enumerate(pairs)]
    for load in loads:
        load.start()
    save = pltpu.make_async_copy(
        filtered_ref.at[pl.ds(start, polar)], filtered_hbm.at[pl.ds(start, polar)], sems.at[len(pairs)]
    )

    def unpack_group(first, packed, stiff):
        values = [unpack_lanes(packed, f) for f in range(FIELDS)]
        for f, value in enumerate(values):
            edge[first + f] = value[0:depth]
            slope_ref[first + f, :, 0:points] = (4.0 / 9.0) * (stiff[f] - 0.5)
            slope_ref[first + f, :, points:] = (4.0 / 9.0) * (value[depth:] - 0.5)

    def unpack(g, carry):
        for parity in range(2):
            first = (2 * g + parity) * FIELDS
            stiff = [stiffness_ref[first + f] for f in range(FIELDS)]
            unpack_group(first + FIELDS, merge(west_ref[g], east_ref[g], parity), stiff)
        return carry

    for load in loads[:3]:
        load.wait()
    lax.fori_loop(0, groups // 2, unpack, 0)
    for load in loads[3:5]:
        load.wait()
    unpack_group(0, above_ref[FIELDS], [above_ref[f, depth:] for f in range(FIELDS)])
    unpack_group(FIELDS + rows, below_ref[FIELDS], [below_ref[f, depth:] for f in range(FIELDS)])
    loads[5].wait()

    @pl.when(is_polar == 1)
    def _():
        half = depth // 2

        def put(i, carry):
            for h in range(2):
                line = smooth_ref[2 * i + h]
                filtered_ref[start + i, h * half : (h + 1) * half] = line[0:half]
                for t in range(half // 8):
                    low = h * half + 8 * t
                    edge[FIELDS + start + i, low : low + 8] = unpack_lanes(line[half:], t)
            return carry

        lax.fori_loop(0, polar, put, 0)
        save.start()

    difference = shift_matrix(span, span, -0.5, 0.5)
    neighbours = shift_matrix(span, span, 1.0, 1.0)

    def centre_of(e, count, part):
        low, high = part * levels, (part + 1) * levels
        rows_of = lambda ref, first: ref[pl.ds(first, count), low:high]
        if not isinstance(e, int) or FIELDS <= e < FIELDS + rows:
            centre = rows_of(filtered_ref, e - FIELDS)
        elif e < FIELDS:
            centre = rows_of(above_ref, e)
        else:
            centre = rows_of(below_ref, e - FIELDS - rows)
        return jnp.concatenate([centre, edge[pl.ds(e, count), low:high]], axis=2)

    def rhs(u, theta, north, south):
        return theta - (shifted(u, difference) + 0.5 * (south - north))

    def inner_rhs(e, count):
        return rhs(
            centre_of(e, count, 0), centre_of(e, count, 2), centre_of(e - 1, count, 1), centre_of(e + 1, count, 1)
        )

    def centre_rhs(i, carry):
        e = FIELDS + 1 + i * 14
        t0[pl.ds(e, 14)] = inner_rhs(e, 14)
        return carry

    lax.fori_loop(0, (rows - 2) // 14, centre_rhs, 0)
    first, last = FIELDS, FIELDS + rows - 1
    reach = ITERS
    t0[first - reach : first - 1] = top * inner_rhs(first - reach, reach - 1)
    t0[last + 2 : last + 1 + reach] = bottom * inner_rhs(last + 2, reach - 1)
    for e, scale in ((first - 1, top), (first, None), (last, None), (last + 1, bottom)):
        value = inner_rhs(e, 1)
        t0[e : e + 1] = value if scale is None else value * scale

    sums = []
    for k in range(ITERS):
        now = table[k]

        def following(e, count):
            here = now[pl.ds(e, count)]
            beside = shifted(here, neighbours) + (now[pl.ds(e - 1, count)] + now[pl.ds(e + 1, count)])
            twice = slope_ref[pl.ds(e, count)] * here - (4.0 / 9.0) * beside
            if k == 0:
                return here, 0.5 * twice
            return here, twice - table[k - 1][pl.ds(e, count)]

        def step(i, carry):
            squares, cross = carry
            e = FIELDS + i * stride
            here, value = following(e, stride)
            if k < ITERS - 1:
                table[k + 1][pl.ds(e, stride)] = value
            here, value = here[:, :, 0:points], value[:, :, 0:points]
            return squares + jnp.sum(here * here, axis=0), cross + jnp.sum(here * value, axis=0)

        zero = jnp.zeros((levels, points), F32)
        sums.append(lax.fori_loop(0, rows // stride, step, (zero, zero)))
        if k < ITERS - 1:
            reach = ITERS - 1 - k
            for e, scale in ((FIELDS - reach, top), (FIELDS + rows, bottom)):
                table[k + 1][e : e + reach] = scale * following(e, reach)[1]

    lane = lanes((1, points))
    moments = jnp.zeros((1, points), F32)
    for i, value in enumerate([a for a, _ in sums] + [b for _, b in sums]):
        total = jnp.sum(jnp.sum(value, axis=0, keepdims=True), axis=1, keepdims=True)
        moments = jnp.where(lane == i, total, moments)
    moments_ref[...] = jnp.broadcast_to(moments, moments_ref.shape)

    @pl.when(is_polar == 1)
    def _():
        save.wait()


def make_basis(info, arrived, west, east, above, below, stiffness, smooth, devices):
    rows, depth, points = arrived.shape
    levels = depth // 3
    extent = rows + 2 * FIELDS
    vmem = pl.BlockSpec(memory_space=pltpu.VMEM)
    hbm = pl.BlockSpec(memory_space=pl.ANY)
    halo = [west, east, above, below, stiffness]
    return pl.pallas_call(
        basis_kernel,
        in_specs=[pl.BlockSpec(memory_space=pltpu.SMEM)] + [hbm] * 6 + [vmem],
        out_specs=(hbm,) + (vmem,) * (ITERS + 1),
        out_shape=(pltpu.HBM((rows, depth, points), F32),)
        + (pltpu.VMEM((extent, levels, 2 * points), F32),) * ITERS
        + (jax.ShapeDtypeStruct((devices, points), F32),),
        scratch_shapes=[
            pltpu.VMEM((extent, depth, points), F32),
            pltpu.VMEM((rows, depth, points), F32),
            pltpu.VMEM((extent, levels, 2 * points), F32),
        ]
        + [pltpu.VMEM(x.shape, F32) for x in halo]
        + [pltpu.SemaphoreType.DMA((7,))],
        input_output_aliases={1: 0},
        cost_estimate=pl.CostEstimate(flops=40000000, bytes_accessed=24000000, transcendentals=0),
        compiler_params=params(24),
        name="basis",
    )(info, in_hbm(arrived), *[in_hbm(x) for x in halo], smooth)


def tree(terms):
    while len(terms) > 1:
        terms = [a + b for a, b in zip(terms[::2], terms[1::2])] + terms[len(terms) // 2 * 2 :]
    return terms[0]


def solve(mu):
    gram = [[0.5 * (mu[i + j] + mu[abs(i - j)]) for j in range(ITERS + 1)] for i in range(ITERS)]

    def inner(a, b):
        return tree([x * tree([y * gram[i][j] for j, y in enumerate(b)]) for i, x in enumerate(a)])

    def image_of(a):
        out = [4.5 * x for x in a] + [jnp.zeros_like(a[0])]
        for k, x in enumerate(a):
            out[k + 1] = out[k + 1] + 2.25 * x
            out[abs(k - 1)] = out[abs(k - 1)] + 2.25 * x
        return out

    zero = jnp.zeros_like(mu[0])
    phi = []
    residual = [zero + 1.0]
    direction = residual
    norm = mu[0]
    for step in range(ITERS):
        image = image_of(direction)
        alpha = norm / inner(direction, image)
        phi = [x + alpha * y for x, y in zip(phi + [zero], direction)]
        if step < ITERS - 1:
            residual = [x - alpha * y for x, y in zip(residual + [zero], image)]
            following = inner(residual, residual)
            ratio = following / norm
            direction = [x + ratio * y for x, y in zip(residual, direction + [zero])]
            norm = following
    return phi


def finish_kernel(spread_ref, filtered_hbm, t0, t1, t2, t3, t4, out_ref, coefficient_ref, filtered_ref, sems):
    table = [t0, t1, t2, t3, t4]
    _, levels, span = t0.shape
    points = span // 2
    block = out_ref.shape[0]
    g = pl.program_id(0)

    def fetch(i):
        part = pl.ds(i * block, block)
        return pltpu.make_async_copy(filtered_hbm.at[part], filtered_ref.at[part], sems.at[i])

    @pl.when(g == 0)
    def _():
        for i in range(filtered_ref.shape[0] // block):
            fetch(i).start()
        total = jnp.sum(spread_ref[...], axis=0, keepdims=True)
        lane = lanes(total.shape)
        picked = [
            jnp.sum(jnp.where(lane == i, total, 0.0), axis=1, keepdims=True) for i in range(2 * ITERS)
        ]
        mu = [picked[0], picked[ITERS]]
        for k in range(1, ITERS):
            mu += [2.0 * picked[k] - mu[0], 2.0 * picked[ITERS + k] - mu[1]]
        for k, value in enumerate(solve(mu)):
            coefficient_ref[k] = jnp.broadcast_to(value, (8, points))

    c = [
        jnp.concatenate([jnp.concatenate([coefficient_ref[k]] * (levels // 8), axis=0)] * 2, axis=1)
        for k in range(ITERS)
    ]

    fetch(g).wait()

    def phi_of(e):
        return tree([c[k] * table[k][e] for k in range(ITERS)])

    stride = 4

    def step(i, carry):
        before, here = carry
        first = i * stride
        e = FIELDS + g * block + first
        near = [before, here] + [phi_of(e + 1 + j) for j in range(stride)]
        old = [filtered_ref[g * block + first + j] for j in range(stride)]
        new = []
        for j in range(stride):
            here = near[j + 1]
            across = pltpu.roll(here, span - 1, 1) - pltpu.roll(here, 1, 1)
            new.append(old[j][0:levels] - 0.5 * across[:, 0:points])
            new.append(old[j][levels : 2 * levels] - 0.5 * (near[j + 2] - near[j])[:, 0:points])
            new.append(old[j][2 * levels :] - here[:, 0:points])
        for j in range(stride):
            for part in range(3):
                out_ref[first + j, part * levels : (part + 1) * levels] = new[3 * j + part]
        return near[stride], near[stride + 1]

    e = FIELDS + g * block
    lax.fori_loop(0, block // stride, step, (phi_of(e - 1), phi_of(e)))


def finish(spread, filtered, table):
    rows, depth, points = filtered.shape
    block = 32
    vmem = pl.BlockSpec(memory_space=pltpu.VMEM)
    piece = pl.BlockSpec((block, depth, points), lambda g: (g, 0, 0))
    return pl.pallas_call(
        finish_kernel,
        grid=(rows // block,),
        in_specs=[vmem, pl.BlockSpec(memory_space=pl.ANY)] + [vmem] * ITERS,
        out_specs=piece,
        out_shape=jax.ShapeDtypeStruct((rows, depth, points), F32),
        scratch_shapes=[
            pltpu.VMEM((ITERS, 8, points), F32),
            pltpu.VMEM((rows, depth, points), F32),
            pltpu.SemaphoreType.DMA((rows // block,)),
        ],
        cost_estimate=pl.CostEstimate(flops=20000000, bytes_accessed=17000000, transcendentals=0),
        compiler_params=params(12),
        name="finish",
    )(spread, in_hbm(filtered), *table)


def shards(state, weights, owners, source_rows, cutoffs, stiffness):
    rows, comps, levels, points = state.shape
    depth = comps * levels
    n_lon = lax.axis_size("lon")
    n_lat = lax.axis_size("lat")
    devices = n_lon * n_lat
    band = lax.axis_index("lat")
    north, south = band == 0, band == n_lat - 1
    polar = cutoffs.shape[0] // 2
    line = lax.axis_index("lon") * polar // n_lon
    info = jnp.stack(
        [
            jnp.where(north, 0, rows - polar),
            (north | south).astype(jnp.int32),
            (band > 0).astype(jnp.int32),
            (band < n_lat - 1).astype(jnp.int32),
            cutoffs[jnp.where(north, line, polar + line)],
        ]
    ).astype(jnp.int32)

    requests, place = make_requests(owners[:, :, 0], source_rows)
    asked = exchange(requests, BOTH)[:, :2]
    moved = exchange(state[asked], BOTH).reshape(2 * devices, depth, points)

    place = place[0]
    caps = make_caps(place, info, moved, weights, polar)
    lines = exchange(caps.reshape(n_lon, -1, points), "lon")
    place, caps = lax.optimization_barrier((place, caps))
    arrived, to_east, to_west, ends = make_arrived(place, moved, weights, stiffness)
    west, east = from_sides(to_east, to_west)
    smooth = exchange(low_pass(info, lines), "lon")
    above, below = from_ends(*make_ends(ends, west, east))
    filtered, *table, moments = make_basis(
        info, arrived, west, east, above, below, stiffness, smooth, devices
    )
    out = finish(exchange(moments, BOTH), filtered, table)
    return out.reshape(rows, comps, levels, points)


def solution(mesh):
    in_specs = (
        P("lat", None, None, "lon"),
        P("lat", None, "lon"),
        P("lon", "lat", None),
        P("lon", "lat"),
        P(),
        P("lat", None, "lon"),
    )
    out_specs = P("lat", None, None, "lon")
    return jax.shard_map(shards, mesh=mesh, in_specs=in_specs, out_specs=out_specs, check_vma=False)
```

time: 240 us -> 154 us (0.64)
  other arithmetic: 40.1 us -> 0.02 us
  Pallas kernels: 0 us -> 37.8 us
  local copies, waits for them, and re-layouts: 41.1 us -> 4.7 us
  between operations: 20.3 us -> 0.2 us
  starting transfers between devices: 42.1 us -> 25.5 us
  waiting for transfers between devices: 57 us -> 48.6 us
  matrix products: 6.6 us -> 0 us
  blocking collectives: 31.5 us -> 36.4 us
    pallas_call x0 -> x7, Pallas kernels: none -> 37.8 us  [the longest x1 14.6 us: make_basis(): pl.pallas_call(basis_kernel, in_specs=[pl.BlockSpec(memory_space=pltpu.SM...]
    mul x7 -> x0, other arithmetic: 19.3 us -> none  [the longest x5 14.9 us: shards(): following = following * inside[cut:-cut]]
    slice x10 -> x0, local copies, waits for them, and re-layouts: 15.8 us -> none  [the longest x3 9.05 us: neighbours(): lax.slice_in_dim(block, size - width, size, axis=dim)]
    ppermute x8 -> x4, starting transfers between devices: 27.8 us -> 12.1 us  [the longest x2 6.31 us: from_ends(): return (lax.ppermute(last, 'lat', north), lax.ppermute(first, 'lat', south))]
    all_to_all x3, waiting for transfers between devices: 51.2 us -> 40.3 us  [exchange(): return lax.all_to_all(block, axes, split_axis=0, concat_axis=0, tiled=True)]
    another operation x2 -> x1, local copies, waits for them, and re-layouts: 8.03 us -> 0.65 us  [shards(): jnp.stack([jnp.where(north, 0, rows - polar), (north | south).astype(jnp....]
    dot_general x7 -> x0, matrix products: 6.6 us -> none  [the longest x1 3.45 us: shards(): jnp.einsum('bci,bij->bcj', sources, weights, preferred_element_type=jnp.f...]
    ppermute x4 -> x0, local copies, waits for them, and re-layouts: 6.44 us -> none  [the longest x2 3.64 us: neighbours(): lax.ppermute(lax.slice_in_dim(block, 0, width, axis=dim), axis, backward)]
  transfers between devices with their start and end apart: 11 -> 7, of which waited for: 4 -> 3; matrix products, arithmetic and copies ran while one was open for 13% -> 1% of each run, Pallas kernels for 0% -> 9%
where the time goes in v2:
time: 154 us; the launch traced here: 153 us
  waiting for transfers between devices  48.6 us (32%)
  Pallas kernels  37.8 us (25%)
  blocking collectives  36.4 us (24%)
  starting transfers between devices  25.5 us (17%)
  local copies, waits for them, and re-layouts  4.7 us (3%)
    all_to_all x3, waiting for transfers between devices, exchange(): return lax.all_to_all(block, axes, split_axis=0, concat_axis=0, tiled=True)  40.3 us
    all_to_all x2, blocking collectives, exchange(): return lax.all_to_all(block, axes, split_axis=0, concat_axis=0, tiled=True)  36.4 us
    pallas_call x1, Pallas kernels, make_basis(): pl.pallas_call(basis_kernel, in_specs=[pl.BlockSpec(memory_space=pltpu.SM...  14.6 us
    all_to_all x3, starting transfers between devices, exchange(): return lax.all_to_all(block, axes, split_axis=0, concat_axis=0, tiled=True)  13.5 us
    pallas_call x1, Pallas kernels, make_arrived(): pl.pallas_call(arrive_kernel, in_specs=[pl.BlockSpec(memory_space=pltpu.S...  8.76 us
    ppermute x2, waiting for transfers between devices, from_ends(): return (lax.ppermute(last, 'lat', north), lax.ppermute(first, 'lat', south))  8.25 us
    ppermute x2, starting transfers between devices, from_ends(): return (lax.ppermute(last, 'lat', north), lax.ppermute(first, 'lat', south))  6.31 us
    pallas_call x1, Pallas kernels, finish(): pl.pallas_call(finish_kernel, grid=(rows // block,), in_specs=[vmem, pl.B...  5.9 us
  transfers between devices with their start and end apart: 7, of which 3 were waited for; matrix products, arithmetic and copies ran while one was open for 1% of the time, Pallas kernels for 9%

profile of v2, /device:TPU:1, one launch (start us, length us, event | category | flops | bytes accessed | tf_op | source)
XLA Modules:
  0.0 153.3 jit_solution(3197232400085402696)
XLA Ops:
  0.0 0.0 copy-start
  0.0 1.0 requests.1
  1.0 20.8 %all_to_all.38 = s32[128,1,128]{2,1,0:T(1,128)S(1)} all-to-all(s32[128,1,128]{2,1,0:T(1,128)S(1)} %bitcast.20), channel_id=1, replica_groups=mesh['lon'=32,'lat'=4] {'lon','lat'}, dimensions={0} | all-to-all | bytes 131072 | tf_op jit(solution)/shard_map/all_to_all | solution.py:29
  21.9 0.1 reshape.21
  22.0 0.0 copy-done
  22.0 2.6 %gather_fusion = bf16[256,3,16,128]{3,2,1,0:T(8,128)(2,1)} fusion(bf16[128,3,16,128]{3,2,1,0:T(8,128)(2,1)S(1)} %copy-done, s32[1024]{0:T(1024)S(1)} %pad_clamp_fusion), kind=kCustom, calls=%fused_computation | custom fusion | bytes 6292480 | tf_op jit(solution)/shard_map/gather | solution.py:701
  24.7 0.0 copy-start.5
  24.7 5.7 %all-to-all-start.1 = ((bf16[128,2,3,16,128]{4,3,2,1,0:T(8,128)(2,1)}), bf16[128,2,3,16,128]{4,3,2,1,0:T(8,128)(2,1)}, u32[]{:S(2)}, u32[]{:S(2)}) async-start(bf16[128,2,3,16,128]{4,3,2,1,0:T(8,128)(2,1)} %bitcast.23), calls=%async_computation.1 | async-start | bytes 6291456 | tf_op jit(solution)/shard_map/all_to_all | solution.py:29
  30.4 0.0 copy-done.5
  30.4 0.6 dynamic_slice.3
  31.0 0.6 stack.31.info_ref
  31.6 40.3 %all-to-all-done.1 = bf16[128,2,3,16,128]{4,3,2,1,0:T(8,128)(2,1)} async-done(((bf16[128,2,3,16,128]{4,3,2,1,0:T(8,128)(2,1)}), bf16[128,2,3,16,128]{4,3,2,1,0:T(8,128)(2,1)}, u32[]{:S(2)}, u32[]{:S(2)}) %all-to-all-start.1) | async-done | bytes 3145760 | tf_op jit(solution)/shard_map/all_to_all | solution.py:29
  71.9 3.0 %caps.1 = f32[16,48,128]{2,1,0:T(8,128)} custom-call(s32[128]{0:T(128)S(1)} %bitcast.21, s32[5]{0:T(128)S(1)} %stack.31.info_ref, bf16[256,48,128]{2,1,0:T(8,128)(2,1)} %bitcast.10.moved_hbm, bf16[128,128,128]{2,1,0:T(8,128)(2,1)} %weights_hbm.3), custom_call_target="tpu_custom_call" | custom-call | flops 30000000 | bytes 1200000 | tf_op jit(solution)/shard_map/caps/pallas_call | solution.py:137
  74.9 3.9 %all-to-all-start.2 = ((f32[32,24,128]{2,1,0:T(8,128)}), f32[32,24,128]{2,1,0:T(8,128)S(1)}, u32[]{:S(2)}, u32[]{:S(2)}) async-start(f32[32,24,128]{2,1,0:T(8,128)} %bitcast.11), calls=%async_computation.2 | async-start | bytes 786432 | tf_op jit(solution)/shard_map/all_to_all | solution.py:29
  78.8 8.8 %arrive.1 = (f32[128,48,128]{2,1,0:T(8,128)}, f32[8,64,128]{2,1,0:T(8,128)}, f32[8,64,128]{2,1,0:T(8,128)S(1)}, f32[2,8,64,128]{3,2,1,0:T(8,128)S(1)}) custom-call(s32[128]{0:T(128)S(1)} %bitcast.22, bf16[256,48,128]{2,1,0:T(8,128)(2,1)} %bitcast.10.moved_hbm, f32[128,16,128]{2,1,0:T(8,128)} %stiffness_hbm.3, bf16[128,128,128]{2,1,0:T(8,128)(2,1)} %weights_hbm.3), custom_call_target="tpu_custom_call" | custom-call | flops 20000000000 | bytes 30000000 | tf_op jit(solution)/shard_map/arrive/pallas_call | solution.py:219
  87.6 1.2 collective-permute-start
  88.8 4.6 %collective-permute-start.1 = (f32[8,64,128]{2,1,0:T(8,128)S(1)}, f32[8,64,128]{2,1,0:T(8,128)S(1)}, u32[]{:S(2)}, u32[]{:S(2)}) collective-permute-start(f32[8,64,128]{2,1,0:T(8,128)S(1)} %get-tuple-element.26), channel_id=1, source_target_pairs={{4,0},{8,4},{12,8},{16,12},{20,16},{24,20},{28,24},{32,28},{36,32}... | collective-permute-start | bytes 786440 | tf_op jit(solution)/shard_map/ppermute | solution.py:87
  93.3 0.0 all-to-all-done.2.lines_ref
  93.3 4.5 %low_pass.1 = f32[32,32,128]{2,1,0:T(8,128)} custom-call(s32[5]{0:T(128)S(1)} %stack.31.info_ref, f32[32,24,128]{2,1,0:T(8,128)S(1)} %all-to-all-done.2.lines_ref, f32[34,128]{1,0:T(8,128)} %constant.42.clone.twist_hbm, f32[256,256]{1,0:T(8,128)} %constant.43.clone.forward_hbm, f32[256,256]{1,0:T(8,128)} %constant.44.clone.inverse_hbm), custom_call_target="tpu_custom_call" | custom-call | flops 700000000 | bytes 1400000 | tf_op jit(solution)/shard_map/low_pass/pallas_call | solution.py:356
  97.9 3.9 %all-to-all-start.3 = ((f32[32,32,128]{2,1,0:T(8,128)}), f32[32,32,128]{2,1,0:T(8,128)S(1)}, u32[]{:S(2)}, u32[]{:S(2)}) async-start(f32[32,32,128]{2,1,0:T(8,128)} %low_pass.1), calls=%async_computation.3 | async-start | bytes 1048576 | tf_op jit(solution)/shard_map/all_to_all | solution.py:29
  101.8 0.0 collective-permute-done.west_ref.west_hbm
  101.8 0.0 copy-start.1
  101.8 0.0 collective-permute-done.1.east_ref.east_hbm
  101.8 0.0 copy-start.2
  101.8 0.1 ends.1
  101.9 4.4 %collective-permute-start.2 = (f32[9,64,128]{2,1,0:T(8,128)S(1)}, f32[9,64,128]{2,1,0:T(8,128)S(1)}, u32[]{:S(2)}, u32[]{:S(2)}) collective-permute-start(f32[9,64,128]{2,1,0:T(8,128)S(1)} %get-tuple-element.28), channel_id=1, source_target_pairs={{0,1},{1,2},{2,3},{4,5},{5,6},{6,7},{8,9},{9,10},{10,11},{12,13},{... | collective-permute-start | bytes 884744 | tf_op jit(solution)/shard_map/ppermute | solution.py:92
  106.3 1.9 %collective-permute-start.3 = (f32[9,64,128]{2,1,0:T(8,128)S(1)}, f32[9,64,128]{2,1,0:T(8,128)S(1)}, u32[]{:S(2)}, u32[]{:S(2)}) collective-permute-start(f32[9,64,128]{2,1,0:T(8,128)S(1)} %get-tuple-element.29), channel_id=1, source_target_pairs={{1,0},{2,1},{3,2},{5,4},{6,5},{7,6},{9,8},{10,9},{11,10},{13,12},{... | collective-permute-start | bytes 884744 | tf_op jit(solution)/shard_map/ppermute | solution.py:92
  108.2 5.5 %collective-permute-done.2.above_hbm = f32[9,64,128]{2,1,0:T(8,128)S(1)} collective-permute-done((f32[9,64,128]{2,1,0:T(8,128)S(1)}, f32[9,64,128]{2,1,0:T(8,128)S(1)}, u32[]{:S(2)}, u32[]{:S(2)}) %collective-permute-start.2) | collective-permute-done | bytes 294944 | tf_op jit(solution)/shard_map/ppermute | solution.py:92
  113.8 0.0 copy-start.3
  113.8 2.7 %collective-permute-done.3.below_hbm = f32[9,64,128]{2,1,0:T(8,128)S(1)} collective-permute-done((f32[9,64,128]{2,1,0:T(8,128)S(1)}, f32[9,64,128]{2,1,0:T(8,128)S(1)}, u32[]{:S(2)}, u32[]{:S(2)}) %collective-permute-start.3) | collective-permute-done | bytes 294944 | tf_op jit(solution)/shard_map/ppermute | solution.py:92
  116.5 0.0 copy-start.4
  116.5 0.0 all-to-all-done.3.smooth_ref
  116.5 0.0 copy-done.1
  116.5 0.0 copy-done.2
  116.5 0.0 copy-done.3
  116.5 0.7 copy-done.4
  117.2 14.6 %basis.1 = (f32[128,48,128]{2,1,0:T(8,128)}, f32[144,16,256]{2,1,0:T(8,128)S(1)}, f32[144,16,256]{2,1,0:T(8,128)S(1)}, f32[144,16,256]{2,1,0:T(8,128)S(1)}, f32[...) custom-call(s32[5]{0:T(128)S(1)} %stack.31.info_ref, ...), custom_call_target="tpu_custom_call", output_to_operand_aliasing={{0}: (1, {})} | custom-call | flops 40000000 | bytes 24000000 | tf_op jit(solution)/shard_map/basis/pallas_call | solution.py:539
  131.8 15.6 %all_to_all.39 = f32[128,1,128]{2,1,0:T(1,128)S(1)} all-to-all(f32[128,1,128]{2,1,0:T(1,128)S(1)} %bitcast.19), channel_id=1, replica_groups=mesh['lon'=32,'lat'=4] {'lon','lat'}, dimensions={0} | all-to-all | bytes 131072 | tf_op jit(solution)/shard_map/all_to_all | solution.py:29
  147.4 5.9 %finish.1 = f32[128,48,128]{2,1,0:T(8,128)} custom-call(f32[128,128]{1,0:T(8,128)S(1)} %bitcast.18, f32[128,48,128]{2,1,0:T(8,128)} %get-tuple-element.31.filtered_hbm, f32[144,16,256]{2,1,0:T(8,128)S(1)} %get-tuple-element.32.t0, f32[144,16,256]{2,1,0:T(8,128)S(1)} %get-tuple-element.33.t1, f32[144,16,256]{2,1,0:T(8,128)S(1)} %get-tuple-element.34.t2, ...), custom_call_target="tpu_custom_call" | custom-call | flops 20000000 | bytes 17000000 | tf_op jit(solution)/shard_map/finish/pallas_call | solution.py:662
  (2 shorter events, 0.0 us)
Async XLA Ops:
  0.0 22.0 %copy-start = (bf16[128,3,16,128]{3,2,1,0:T(8,128)(2,1)S(1)}, bf16[128,3,16,128]{3,2,1,0:T(8,128)(2,1)}, u32[]{:S(2)}) copy-start(bf16[128,3,16,128]{3,2,1,0:T(8,128)(2,1)} %param.9) | copy-start | bytes 4718596
  24.7 5.7 %copy-start.5 = (s32[32]{0:T(128)S(1)}, s32[32]{0:T(128)}, u32[]{:S(2)}) copy-start(s32[32]{0:T(128)} %param.13) | copy-start | bytes 388
  24.7 47.3 %all-to-all-start.1 = ((bf16[128,2,3,16,128]{4,3,2,1,0:T(8,128)(2,1)}), bf16[128,2,3,16,128]{4,3,2,1,0:T(8,128)(2,1)}, u32[]{:S(2)}, u32[]{:S(2)}) async-start(bf16[128,2,3,16,128]{4,3,2,1,0:T(8,128)(2,1)} %bitcast.23), calls=%async_computation.1 | async-start | bytes 6291456 | tf_op jit(solution)/shard_map/all_to_all | solution.py:29
  74.9 18.4 %all-to-all-start.2 = ((f32[32,24,128]{2,1,0:T(8,128)}), f32[32,24,128]{2,1,0:T(8,128)S(1)}, u32[]{:S(2)}, u32[]{:S(2)}) async-start(f32[32,24,128]{2,1,0:T(8,128)} %bitcast.11), calls=%async_computation.2 | async-start | bytes 786432 | tf_op jit(solution)/shard_map/all_to_all | solution.py:29
  87.6 14.2 %collective-permute-start = (f32[8,64,128]{2,1,0:T(8,128)}, f32[8,64,128]{2,1,0:T(8,128)S(1)}, u32[]{:S(2)}, u32[]{:S(2)}) collective-permute-start(f32[8,64,128]{2,1,0:T(8,128)} %get-tuple-element.25), channel_id=1, source_target_pairs={{0,4},{4,8},{8,12},{12,16},{16,20},{20,24},{24,28},{28,32},{32,36}... | collective-permute-start | bytes 786440 | tf_op jit(solution)/shard_map/ppermute | solution.py:87
  88.8 13.1 %collective-permute-start.1 = (f32[8,64,128]{2,1,0:T(8,128)S(1)}, f32[8,64,128]{2,1,0:T(8,128)S(1)}, u32[]{:S(2)}, u32[]{:S(2)}) collective-permute-start(f32[8,64,128]{2,1,0:T(8,128)S(1)} %get-tuple-element.26), channel_id=1, source_target_pairs={{4,0},{8,4},{12,8},{16,12},{20,16},{24,20},{28,24},{32,28},{36,32}... | collective-permute-start | bytes 786440 | tf_op jit(solution)/shard_map/ppermute | solution.py:87
  97.9 18.6 %all-to-all-start.3 = ((f32[32,32,128]{2,1,0:T(8,128)}), f32[32,32,128]{2,1,0:T(8,128)S(1)}, u32[]{:S(2)}, u32[]{:S(2)}) async-start(f32[32,32,128]{2,1,0:T(8,128)} %low_pass.1), calls=%async_computation.3 | async-start | bytes 1048576 | tf_op jit(solution)/shard_map/all_to_all | solution.py:29
  101.8 14.7 %copy-start.1 = (f32[8,64,128]{2,1,0:T(8,128)}, f32[8,64,128]{2,1,0:T(8,128)S(1)}, u32[]{:S(2)}) copy-start(f32[8,64,128]{2,1,0:T(8,128)S(1)} %collective-permute-done.west_ref.west_hbm) | copy-start | bytes 786436
  101.8 14.7 %copy-start.2 = (f32[8,64,128]{2,1,0:T(8,128)}, f32[8,64,128]{2,1,0:T(8,128)S(1)}, u32[]{:S(2)}) copy-start(f32[8,64,128]{2,1,0:T(8,128)S(1)} %collective-permute-done.1.east_ref.east_hbm) | copy-start | bytes 786436
  101.9 11.8 %collective-permute-start.2 = (f32[9,64,128]{2,1,0:T(8,128)S(1)}, f32[9,64,128]{2,1,0:T(8,128)S(1)}, u32[]{:S(2)}, u32[]{:S(2)}) collective-permute-start(f32[9,64,128]{2,1,0:T(8,128)S(1)} %get-tuple-element.28), channel_id=1, source_target_pairs={{0,1},{1,2},{2,3},{4,5},{5,6},{6,7},{8,9},{9,10},{10,11},{12,13},{... | collective-permute-start | bytes 884744 | tf_op jit(solution)/shard_map/ppermute | solution.py:92
  106.3 10.2 %collective-permute-start.3 = (f32[9,64,128]{2,1,0:T(8,128)S(1)}, f32[9,64,128]{2,1,0:T(8,128)S(1)}, u32[]{:S(2)}, u32[]{:S(2)}) collective-permute-start(f32[9,64,128]{2,1,0:T(8,128)S(1)} %get-tuple-element.29), channel_id=1, source_target_pairs={{1,0},{2,1},{3,2},{5,4},{6,5},{7,6},{9,8},{10,9},{11,10},{13,12},{... | collective-permute-start | bytes 884744 | tf_op jit(solution)/shard_map/ppermute | solution.py:92
  113.8 2.8 %copy-start.3 = (f32[9,64,128]{2,1,0:T(8,128)}, f32[9,64,128]{2,1,0:T(8,128)S(1)}, u32[]{:S(2)}) copy-start(f32[9,64,128]{2,1,0:T(8,128)S(1)} %collective-permute-done.2.above_hbm) | copy-start | bytes 884740
  116.5 0.7 copy-start.4

commit v3 on v2

v3 whole, which is shorter than its diff:
```python
import functools

import numpy as np
import jax
import jax.numpy as jnp
from jax import lax
from jax.experimental import pallas as pl
from jax.experimental.pallas import tpu as pltpu
from jax.sharding import PartitionSpec as P

ITERS = 5
BOTH = ("lon", "lat")
HIGHEST = lax.Precision.HIGHEST
FIELD = 16
FIELDS = 8
F32 = jnp.float32
MIB = 1024 * 1024


def params(mib):
    return pltpu.CompilerParams(vmem_limit_bytes=mib * MIB)


def in_hbm(x):
    return pltpu.with_memory_space_constraint(x, pltpu.HBM)


def exchange(block, axes):
    return lax.all_to_all(block, axes, split_axis=0, concat_axis=0, tiled=True)


def lanes(shape):
    return lax.broadcasted_iota(jnp.int32, shape, len(shape) - 1)


def pack_lanes(shape, rows):
    field = lanes(shape) // FIELD
    packed = jnp.zeros(shape, F32)
    for f, row in enumerate(rows):
        packed = jnp.where(field == f, pltpu.roll(row, (FIELD * f + 8) % 128, len(shape) - 1), packed)
    return packed


def unpack_lanes(packed, f):
    return pltpu.roll(packed, (-(FIELD * f + 8)) % 128, packed.ndim - 1)


def request_kernel(row_ref, wanted_ref, request_ref, place_ref):
    row = row_ref[...]
    size = row.shape[1]
    down = lax.broadcasted_iota(jnp.int32, (size, size), 0)
    across = lax.broadcasted_iota(jnp.int32, (size, size), 1)
    owner = jnp.broadcast_to(row, (size, size))
    earlier = (owner.T == owner) & (down < across)
    slot = jnp.sum(jnp.where(earlier, 1.0, 0.0), axis=0, keepdims=True)
    wanted = wanted_ref[...].astype(F32)
    out = jnp.zeros((size, size), F32)
    for s in range(2):
        hit = jnp.where((owner == down) & (slot == s), wanted, 0.0)
        out = jnp.where(across == s, jnp.sum(hit, axis=1, keepdims=True), out)
    request_ref[...] = out.astype(jnp.int32)
    place_ref[...] = 2 * row + slot.astype(jnp.int32)


def make_requests(owner, wanted):
    rows = wanted.shape[1]
    return pl.pallas_call(
        request_kernel,
        out_shape=(
            jax.ShapeDtypeStruct((rows, rows), jnp.int32),
            jax.ShapeDtypeStruct((1, rows), jnp.int32),
        ),
        cost_estimate=pl.CostEstimate(flops=200000, bytes_accessed=200000, transcendentals=0),
        compiler_params=params(2),
        name="requests",
    )(in_hbm(owner), in_hbm(wanted))


def ways(axis, wrap):
    count = lax.axis_size(axis)
    up = [(i, (i + 1) % count) for i in range(count if wrap else count - 1)]
    return up, [(b, a) for a, b in up]


def from_sides(to_east, to_west):
    east, west = ways("lon", True)
    return lax.ppermute(to_east, "lon", east), lax.ppermute(to_west, "lon", west)


def from_ends(last, first):
    north, south = ways("lat", False)
    return lax.ppermute(last, "lat", north), lax.ppermute(first, "lat", south)


def low_half(x):
    return lanes(x.shape) % FIELD < FIELD // 2


def shift(x, by):
    return pltpu.roll(x, by % 128, x.ndim - 1)


def for_sides(even, odd):
    low = low_half(even)
    return jnp.where(low, even, shift(odd, 8)), jnp.where(low, shift(even, -8), odd)


def strips(from_west, from_east, own, parity):
    low = low_half(own)
    if parity == 0:
        return jnp.where(low, from_west, own), jnp.where(low, own, shift(from_east, 8))
    return jnp.where(low, shift(from_west, -8), own), jnp.where(low, own, from_east)


def beyond(left, right):
    return jnp.where(lanes(left.shape) % FIELD == FIELD // 2, shift(left, 1), shift(right, -1))


def insertion(packed, f):
    lane = lanes(packed.shape)
    return jnp.where((lane == 0) | (lane == 127), unpack_lanes(packed, f), 0.0)


def insertions(packed, first, count):
    return jnp.stack([insertion(packed[(first + i) // FIELDS], (first + i) % FIELDS) for i in range(count)])


def caps_kernel(
    place_ref, info_ref, moved_hbm, weights_hbm, stiffness_hbm, caps_ref, last_ref, first_ref,
    held, weights_ref, stiffness_ref, row_sems, sems,
):
    polar = caps_ref.shape[0]
    depth = caps_ref.shape[1]
    rows = weights_hbm.shape[0]
    start = info_ref[0]
    spans = [(start, 0, polar), (0, polar, FIELDS), (rows - FIELDS, polar + FIELDS, FIELDS)]
    copies = []
    for n, (row, at, count) in enumerate(spans):
        copies.append(
            pltpu.make_async_copy(weights_hbm.at[pl.ds(row, count)], weights_ref.at[pl.ds(at, count)], sems.at[n])
        )
        copies += [
            pltpu.make_async_copy(moved_hbm.at[place_ref[row + i]], held.at[at + i], row_sems.at[at + i])
            for i in range(count)
        ]
    for end, row in enumerate((0, rows - FIELDS)):
        copies.append(
            pltpu.make_async_copy(stiffness_hbm.at[pl.ds(row, FIELDS)], stiffness_ref.at[end], sems.at[3 + end])
        )
    for copy in copies:
        copy.start()
    for copy in copies:
        copy.wait()
    values = [
        jnp.dot(held[i], weights_ref[i], preferred_element_type=F32) for i in range(polar + 2 * FIELDS)
    ]
    for i in range(polar):
        caps_ref[i] = values[i]
    for end, ref in enumerate((first_ref, last_ref)):
        low = polar + end * FIELDS
        rim = values[low : low + FIELDS]
        stiff = [stiffness_ref[end, f] for f in range(FIELDS)]
        for f in range(FIELDS):
            ref[f, 0:depth] = rim[f]
            ref[f, depth:] = stiff[f]
        ref[FIELDS, 0:depth] = pack_lanes(rim[0].shape, rim)
        ref[FIELDS, depth:] = pack_lanes(stiff[0].shape, stiff)


def make_caps(place, info, moved, weights, stiffness, polar):
    _, depth, points = moved.shape
    levels = stiffness.shape[1]
    smem = pl.BlockSpec(memory_space=pltpu.SMEM)
    hbm = pl.BlockSpec(memory_space=pl.ANY)
    count = polar + 2 * FIELDS
    rim = jax.ShapeDtypeStruct((FIELDS + 1, depth + levels, points), F32)
    return pl.pallas_call(
        caps_kernel,
        in_specs=[smem, smem, hbm, hbm, hbm],
        out_specs=[pl.BlockSpec(memory_space=pltpu.VMEM)] * 3,
        out_shape=(jax.ShapeDtypeStruct((polar, depth, points), F32), rim, rim),
        scratch_shapes=[
            pltpu.VMEM((count, depth, points), moved.dtype),
            pltpu.VMEM((count, points, points), weights.dtype),
            pltpu.VMEM((2, FIELDS, levels, points), F32),
            pltpu.SemaphoreType.DMA((count,)),
            pltpu.SemaphoreType.DMA((5,)),
        ],
        cost_estimate=pl.CostEstimate(flops=60000000, bytes_accessed=2400000, transcendentals=0),
        compiler_params=params(6),
        name="caps",
    )(place, info, in_hbm(moved), in_hbm(weights), in_hbm(stiffness))


def stiff_kernel(stiffness_ref, east_ref, west_ref, own_ref):
    def pair(g, carry):
        packed = []
        for h in range(2):
            rows = [stiffness_ref[(2 * g + h) * FIELDS + f] for f in range(FIELDS)]
            packed.append(pack_lanes(rows[0].shape, rows))
        east_ref[g], west_ref[g] = for_sides(*packed)
        own_ref[2 * g], own_ref[2 * g + 1] = packed
        return carry

    lax.fori_loop(0, east_ref.shape[0], pair, 0)


def pack_stiffness(stiffness):
    rows, levels, points = stiffness.shape
    side = pltpu.HBM((rows // (2 * FIELDS), levels, points), F32)
    return pl.pallas_call(
        stiff_kernel,
        out_shape=(side, side, pltpu.HBM((rows // FIELDS, levels, points), F32)),
        cost_estimate=pl.CostEstimate(flops=1000000, bytes_accessed=1300000, transcendentals=0),
        compiler_params=params(4),
        name="pack_stiffness",
    )(in_hbm(stiffness))


def edge_weights_kernel(weights_ref, out_ref):
    rows = [weights_ref[f].astype(F32) for f in range(FIELDS)]
    out_ref[0] = pack_lanes(rows[0].shape, rows).astype(out_ref.dtype)


def edge_weights(weights):
    rows, points, _ = weights.shape
    return pl.pallas_call(
        edge_weights_kernel,
        grid=(rows // FIELDS,),
        in_specs=[pl.BlockSpec((FIELDS, points, points), lambda g: (g, 0, 0))],
        out_specs=pl.BlockSpec((1, points, points), lambda g: (g, 0, 0)),
        out_shape=pltpu.HBM((rows // FIELDS, points, points), weights.dtype),
        cost_estimate=pl.CostEstimate(flops=2000000, bytes_accessed=5000000, transcendentals=0),
        compiler_params=params(6),
        name="edge_weights",
    )(in_hbm(weights))


def edges_kernel(
    place_ref, moved_hbm, east_hbm, west_hbm, own_hbm, weights_hbm, east_ref, west_ref, own_ref,
    moved_ref, weights_ref, sems,
):
    depth = moved_ref.shape[1]
    levels = own_hbm.shape[1]
    loads = [
        pltpu.make_async_copy(moved_hbm, moved_ref, sems.at[0]),
        pltpu.make_async_copy(weights_hbm, weights_ref, sems.at[1]),
        pltpu.make_async_copy(east_hbm, east_ref.at[:, pl.ds(depth, levels)], sems.at[2]),
        pltpu.make_async_copy(west_hbm, west_ref.at[:, pl.ds(depth, levels)], sems.at[3]),
        pltpu.make_async_copy(own_hbm, own_ref.at[:, pl.ds(depth, levels)], sems.at[4]),
    ]
    for load in loads:
        load.start()
    for load in loads[:2]:
        load.wait()
    shape = (depth, moved_ref.shape[2])
    field = lanes(shape) // FIELD

    def pair(g, carry):
        packed = []
        for h in range(2):
            group = 2 * g + h
            sources = [moved_ref[place_ref[group * FIELDS + f]] for f in range(FIELDS)]
            product = jnp.dot(
                jnp.concatenate(sources, axis=0), weights_ref[group], preferred_element_type=F32
            )
            value = jnp.zeros(shape, F32)
            for f in range(FIELDS):
                value = jnp.where(field == f, product[f * depth : (f + 1) * depth], value)
            packed.append(value)
        east, west = for_sides(*packed)
        east_ref[g, 0:depth] = east
        west_ref[g, 0:depth] = west
        for h in range(2):
            own_ref[2 * g + h, 0:depth] = packed[h]
        return carry

    lax.fori_loop(0, east_ref.shape[0], pair, 0, unroll=2)
    for load in loads[2:]:
        load.wait()


def make_edges(place, moved, weights, stiff):
    _, depth, points = moved.shape
    groups, levels, _ = stiff[2].shape
    both = depth + levels
    vmem = pl.BlockSpec(memory_space=pltpu.VMEM)
    hbm = pl.BlockSpec(memory_space=pl.ANY)
    side = jax.ShapeDtypeStruct((groups // 2, both, points), F32)
    return pl.pallas_call(
        edges_kernel,
        in_specs=[pl.BlockSpec(memory_space=pltpu.SMEM)] + [hbm] * 5,
        out_specs=[vmem] * 3,
        out_shape=(side, side, pltpu.HBM((groups, both, points), F32)),
        scratch_shapes=[
            pltpu.VMEM(moved.shape, moved.dtype),
            pltpu.VMEM(weights.shape, weights.dtype),
            pltpu.SemaphoreType.DMA((5,)),
        ],
        cost_estimate=pl.CostEstimate(flops=10000000000, bytes_accessed=5000000, transcendentals=0),
        compiler_params=params(10),
        name="edges",
    )(place, in_hbm(moved), *[in_hbm(x) for x in stiff], in_hbm(weights))


def ends_kernel(last_rim_ref, first_rim_ref, west_ref, east_ref, last_ref, first_ref):
    pairs = west_ref.shape[0]
    for rim, ref, end, pair in ((first_rim_ref, first_ref, 0, 0), (last_rim_ref, last_ref, 1, pairs - 1)):
        ref[0:FIELDS] = rim[0:FIELDS]
        ref[FIELDS], ref[FIELDS + 1] = strips(west_ref[pair], east_ref[pair], rim[FIELDS], end)


def make_ends(last, first, west, east):
    _, both, points = last.shape
    shape = jax.ShapeDtypeStruct((FIELDS + 2, both, points), F32)
    return pl.pallas_call(
        ends_kernel,
        out_shape=(shape, shape),
        cost_estimate=pl.CostEstimate(flops=100000, bytes_accessed=2000000, transcendentals=0),
        compiler_params=params(6),
        name="ends",
    )(last, first, west, east)


def tree(terms):
    while len(terms) > 1:
        terms = [a + b for a, b in zip(terms[::2], terms[1::2])] + terms[len(terms) // 2 * 2 :]
    return terms[0]


def halves(table):
    high = table.astype(jnp.bfloat16)
    return np.stack([high, (table - high.astype(np.float64)).astype(jnp.bfloat16)])


def filter_tables(parts, points):
    total = parts * points
    half = parts // 2 + 1
    k1, p = np.arange(half), np.arange(points)
    twist = 2 * np.pi * np.outer(k1, p) / total
    inner = 2 * np.pi * np.outer(p, p) / points
    c, s = np.cos(inner), np.sin(inner)
    forward = np.block([[c, -s], [s, c]])
    inverse = np.block([[c, s], [-s, c]])
    twist = np.concatenate([np.cos(twist), np.sin(twist)]).astype(np.float32)
    return twist, halves(forward), halves(inverse)


def cosine_sums(v, parts):
    mid, quarter = parts // 2, parts // 4
    plus = [v[j - 1] + v[mid - j - 1] for j in range(1, quarter)]
    minus = [v[j - 1] - v[mid - j - 1] for j in range(1, quarter)]
    out = []
    for m in range(mid + 1):
        folded = plus if m % 2 == 0 else minus
        terms = [float(np.cos(2 * np.pi * m * j / parts)) * folded[j - 1] for j in range(1, quarter)]
        if m % 2 == 0:
            terms.append(v[quarter - 1] if m % 4 == 0 else -v[quarter - 1])
        out.append(tree(terms))
    return out


def sine_sums(v, parts):
    mid, quarter = parts // 2, parts // 4
    plus = [v[j - 1] + v[mid - j - 1] for j in range(1, quarter)]
    minus = [v[j - 1] - v[mid - j - 1] for j in range(1, quarter)]
    out = []
    for m in range(1, mid):
        folded = minus if m % 2 == 0 else plus
        terms = [float(np.sin(2 * np.pi * m * j / parts)) * folded[j - 1] for j in range(1, quarter)]
        if m % 2 == 1:
            terms.append(v[quarter - 1] if m % 4 == 1 else -v[quarter - 1])
        out.append(tree(terms))
    return out


def product(x, table_ref):
    high, low = split(x)
    count = x.shape[0]
    both = jnp.dot(jnp.concatenate([high, low], axis=0), table_ref[0], preferred_element_type=F32)
    return both[:count] + both[count:] + jnp.dot(high, table_ref[1], preferred_element_type=F32)


def filter_kernel(
    info_ref, lines_ref, twist_hbm, forward_hbm, inverse_hbm, out_ref,
    work, back, twist_ref, forward_ref, inverse_ref, sems,
):
    parts, count, points = lines_ref.shape
    pairs = [(twist_hbm, twist_ref), (forward_hbm, forward_ref), (inverse_hbm, inverse_ref)]
    loads = [pltpu.make_async_copy(a, b, sems.at[i]) for i, (a, b) in enumerate(pairs)]
    for load in loads:
        load.start()
    total = parts * points
    mid = parts // 2
    cutoff = info_ref[4]
    tiles = count // 8
    loads[0].wait()
    for t in range(tiles):
        x = [lines_ref[d, 8 * t : 8 * t + 8, :] for d in range(parts)]
        even = cosine_sums([x[d] + x[parts - d] for d in range(1, mid)], parts)
        odd = sine_sums([x[d] - x[parts - d] for d in range(1, mid)], parts)
        ends = (x[0] + x[mid], x[0] - x[mid])
        for k in range(mid + 1):
            real = ends[k % 2] + even[k]
            row = k * count + 8 * t
            tc, ts = twist_ref[k : k + 1, :], twist_ref[mid + 1 + k : mid + 2 + k, :]
            if k in (0, mid):
                work[row : row + 8, 0:points] = real * tc
                work[row : row + 8, points:] = -real * ts
            else:
                imag = odd[k - 1]
                work[row : row + 8, 0:points] = real * tc - imag * ts
                work[row : row + 8, points:] = -imag * tc - real * ts
    loads[1].wait()
    spectrum = product(work[...], forward_ref)
    shape = spectrum.shape
    wave = lax.broadcasted_iota(jnp.int32, shape, 0) // count + parts * (lanes(shape) % points)
    kept = (wave <= cutoff) | (wave >= total - cutoff)
    spectrum = jnp.where(kept, spectrum * (1.0 / total), 0.0)
    loads[2].wait()
    back[...] = product(spectrum, inverse_ref)
    for t in range(tiles):
        real, imag = [], []
        for k in range(mid + 1):
            row = k * count + 8 * t
            br, bi = back[row : row + 8, 0:points], back[row : row + 8, points:]
            tc, ts = twist_ref[k : k + 1, :], twist_ref[mid + 1 + k : mid + 2 + k, :]
            real.append(br * tc - bi * ts)
            if k not in (0, mid):
                imag.append(br * ts + bi * tc)
        even = cosine_sums(real[1:mid], parts)
        odd = sine_sums(imag, parts)
        ends = (real[0] + real[mid], real[0] - real[mid])
        for d in range(mid + 1):
            value = ends[d % 2] + 2.0 * even[d]
            if d in (0, mid):
                out_ref[d, 8 * t : 8 * t + 8, :] = value
            else:
                out_ref[d, 8 * t : 8 * t + 8, :] = value - 2.0 * odd[d - 1]
                out_ref[parts - d, 8 * t : 8 * t + 8, :] = value + 2.0 * odd[d - 1]
    shape = (8, points)
    low = lanes(shape) < points // 2
    for d in range(parts):
        rows = [
            jnp.where(
                low,
                out_ref[(d + 1) % parts, 8 * t : 8 * t + 8, :],
                out_ref[(d - 1) % parts, 8 * t : 8 * t + 8, :],
            )
            for t in range(tiles)
        ]
        out_ref[d, count : count + 8, :] = pack_lanes(shape, rows)


def low_pass(info, lines):
    parts, count, points = lines.shape
    tables = filter_tables(parts, points)
    rows = (parts // 2 + 1) * count
    vmem = pl.BlockSpec(memory_space=pltpu.VMEM)
    return pl.pallas_call(
        filter_kernel,
        in_specs=[pl.BlockSpec(memory_space=pltpu.SMEM)] + [vmem] + [pl.BlockSpec(memory_space=pl.ANY)] * 3,
        out_specs=vmem,
        out_shape=pltpu.HBM((parts, count + 8, points), F32),
        scratch_shapes=[pltpu.VMEM((rows, 2 * points), F32)] * 2
        + [pltpu.VMEM(x.shape, x.dtype) for x in tables]
        + [pltpu.SemaphoreType.DMA((3,))],
        cost_estimate=pl.CostEstimate(flops=700000000, bytes_accessed=1400000, transcendentals=0),
        compiler_params=params(8),
        name="low_pass",
    )(info, lines, *[in_hbm(jnp.asarray(x)) for x in tables])


def split(x):
    high = x.astype(jnp.bfloat16)
    return high, (x - high.astype(F32)).astype(jnp.bfloat16)


def shift_matrix(points, left, right):
    source = lax.broadcasted_iota(jnp.int32, (2 * points, points), 0) % points
    target = lax.broadcasted_iota(jnp.int32, (2 * points, points), 1)
    west, east = source + 1 == target, source == target + 1
    return (jnp.where(west, left, 0.0) + jnp.where(east, right, 0.0)).astype(jnp.bfloat16)


def shifted(x, matrix):
    flat = x.reshape(-1, x.shape[-1])
    out = jnp.dot(jnp.concatenate(split(flat), axis=1), matrix, preferred_element_type=F32)
    return out.reshape(x.shape)


def prepare_kernel(
    place_ref, info_ref, moved_hbm, weights_hbm, west_hbm, east_hbm, own_hbm,
    arrived_hbm, begun_hbm, strips_ref, ends_ref,
    moved_ref, weights_ref, begun_ref, wide, past, west_ref, east_ref, own_ref, sems, weight_sems, row_sems, save_sems,
):
    rows, levels, points = begun_ref.shape
    depth = wide.shape[1]
    polar = 16
    pieces, stride = rows // polar, 2 * polar
    start, is_polar = info_ref[0], info_ref[1]
    pairs = [(west_hbm, west_ref), (east_hbm, east_ref), (own_hbm, own_ref), (moved_hbm, moved_ref)]
    loads = [pltpu.make_async_copy(a, b, sems.at[i]) for i, (a, b) in enumerate(pairs)]

    def fetch(i):
        piece = pl.ds(i * polar, polar)
        return pltpu.make_async_copy(weights_hbm.at[piece], weights_ref.at[piece], weight_sems.at[i])

    def save_rows(i):
        return pltpu.make_async_copy(
            wide.at[pl.ds(1 + i * polar, polar)], arrived_hbm.at[pl.ds(i * polar, polar)], row_sems.at[i]
        )

    def save(i):
        piece = pl.ds(i * stride, stride)
        return pltpu.make_async_copy(begun_ref.at[piece], begun_hbm.at[piece], save_sems.at[i])

    for load in loads:
        load.start()
    for i in range(pieces):
        fetch(i).start()
    zero = jnp.zeros((1, depth, points), F32)
    for row in (0, rows + 1):
        wide[row : row + 1] = zero
    for load in loads[:3]:
        load.wait()
    for g in range(rows // FIELDS):
        left, right = strips(west_ref[g // 2], east_ref[g // 2], own_ref[g], g % 2)
        strips_ref[0, g], strips_ref[1, g] = left, right
        past[g] = beyond(left[0:levels], right[0:levels])

    @pl.when(is_polar == 1)
    def _():
        past[pl.ds(start // FIELDS, polar // FIELDS)] = jnp.zeros((polar // FIELDS, levels, points), F32)

    loads[3].wait()
    difference = shift_matrix(points, -0.5, 0.5)
    half_sign = jnp.where(lanes((1, 1, points)) == 0, 0.5, -0.5)

    def interpolate(i):
        fetch(i).wait()
        first = i * polar
        sources = [moved_ref[place_ref[first + j]] for j in range(polar)]
        values = [
            jnp.dot(source, weights_ref[first + j], preferred_element_type=F32) for j, source in enumerate(sources)
        ]
        for j, value in enumerate(values):
            wide[1 + first + j] = value

        @pl.when((is_polar == 1) & (start // polar == i))
        def _():
            wide[1 + first : 1 + first + polar] = jnp.zeros((polar, depth, points), F32)

        save_rows(i).start()

    def step(i):
        e = 1 + i * stride
        part = lambda e, which: wide[pl.ds(e, stride), which * levels : (which + 1) * levels]
        groups = past[pl.ds(i * (stride // FIELDS), stride // FIELDS)]
        across = shifted(part(e, 0), difference) - half_sign * insertions(groups, 0, stride)
        begun_ref[pl.ds(i * stride, stride)] = part(e, 2) - (across + 0.5 * (part(e + 1, 1) - part(e - 1, 1)))
        save(i).start()

    for i in range(pieces):
        interpolate(i)
        if i % 2 == 0 and i > 0:
            step(i // 2 - 1)
    step(pieces // 2 - 1)
    ends_ref[0] = wide[1, levels : 2 * levels]
    ends_ref[1] = wide[rows, levels : 2 * levels]
    for i in range(pieces):
        save_rows(i).wait()
    for i in range(rows // stride):
        save(i).wait()


def prepare(place, info, moved, weights, west, east, own):
    rows, points, _ = weights.shape
    groups, both, _ = own.shape
    depth = moved.shape[1]
    levels = both - depth
    vmem = pl.BlockSpec(memory_space=pltpu.VMEM)
    hbm = pl.BlockSpec(memory_space=pl.ANY)
    return pl.pallas_call(
        prepare_kernel,
        in_specs=[pl.BlockSpec(memory_space=pltpu.SMEM)] * 2 + [hbm] * 5,
        out_specs=[hbm, hbm, vmem, vmem],
        out_shape=(
            pltpu.HBM((rows, depth, points), F32),
            pltpu.HBM((rows, levels, points), F32),
            pltpu.HBM((2, groups, both, points), F32),
            jax.ShapeDtypeStruct((2, levels, points), F32),
        ),
        scratch_shapes=[
            pltpu.VMEM(moved.shape, moved.dtype),
            pltpu.VMEM(weights.shape, weights.dtype),
            pltpu.VMEM((rows, levels, points), F32),
            pltpu.VMEM((rows + 2, depth, points), F32),
            pltpu.VMEM((groups, levels, points), F32),
            pltpu.VMEM(west.shape, F32),
            pltpu.VMEM(east.shape, F32),
            pltpu.VMEM(own.shape, F32),
            pltpu.SemaphoreType.DMA((4,)),
            pltpu.SemaphoreType.DMA((rows // 16,)),
            pltpu.SemaphoreType.DMA((rows // 16,)),
            pltpu.SemaphoreType.DMA((rows // 32,)),
        ],
        cost_estimate=pl.CostEstimate(flops=20000000000, bytes_accessed=16000000, transcendentals=0),
        compiler_params=params(22),
        name="prepare",
    )(place, info, *[in_hbm(x) for x in (moved, weights, west, east, own)])


def basis_kernel(
    info_ref, above_hbm, below_hbm, begun_hbm, strips_hbm, stiffness_hbm, ends_ref, smooth_ref,
    t0, t1, t2, t3, t4, past_ref, caps_ref, moments_ref,
    held, slope_ref, wide, polar_strips, side, side_slope, above_ref, below_ref, sems,
):
    rows, levels, points = slope_ref.shape
    depth = 3 * levels
    polar = caps_ref.shape[0]
    groups = rows // FIELDS
    table = [t0, t1, t2, t3, t4]
    start, is_polar = info_ref[0], info_ref[1]
    top, bottom = info_ref[2].astype(F32), info_ref[3].astype(F32)
    stride = 128
    first, last = FIELDS, FIELDS + rows - 1
    loads = [
        pltpu.make_async_copy(strips_hbm, held.at[:, pl.ds(1, groups)], sems.at[0]),
        pltpu.make_async_copy(begun_hbm, t0.at[pl.ds(first, rows)], sems.at[1]),
        pltpu.make_async_copy(stiffness_hbm, slope_ref, sems.at[2]),
    ]
    halo = [
        pltpu.make_async_copy(above_hbm, above_ref, sems.at[3]),
        pltpu.make_async_copy(below_hbm, below_ref, sems.at[4]),
    ]
    for load in halo + loads:
        load.start()
    difference = shift_matrix(points, -0.5, 0.5)
    neighbours = shift_matrix(points, 1.0, 1.0)
    half_sign = jnp.where(lanes((1, 1, points)) == 0, 0.5, -0.5)

    def component(x, which):
        return x[..., which * levels : (which + 1) * levels, :]

    def rhs(u, theta, north, south, inserted):
        return theta - (shifted(u, difference) - half_sign * inserted + 0.5 * (south - north))

    for load in halo:
        load.wait()
    nearest = []
    for end, ref in enumerate((above_ref, below_ref)):
        group = 0 if end == 0 else groups + 1
        left, right = ref[FIELDS], ref[FIELDS + 1]
        held[0, group], held[1, group] = left, right
        packed = beyond(left[0:levels], right[0:levels])[None]
        fields = ref[0:FIELDS, 0:depth]
        v = component(fields, 1)
        low, count = (FIELDS - ITERS, ITERS) if end == 0 else (0, ITERS)
        if end == 0:
            north = v[low - 1 : FIELDS - 1]
            south = jnp.concatenate([v[low + 1 :], ends_ref[0:1]], axis=0)
            nearest.append(0.5 * v[FIELDS - 1 :])
        else:
            north = jnp.concatenate([ends_ref[1:2], v[0 : count - 1]], axis=0)
            south = v[1 : count + 1]
            nearest.append(0.5 * v[0:1])
        value = rhs(
            component(fields, 0)[low : low + count], component(fields, 2)[low : low + count], north, south,
            insertions(packed, low, count),
        )
        place = first - FIELDS + low if end == 0 else last + 1
        t0[place : place + count] = (top if end == 0 else bottom) * value
    loads[0].wait()
    loads[1].wait()
    t0[first : first + 1] = t0[first : first + 1] + nearest[0]
    t0[last : last + 1] = t0[last : last + 1] - nearest[1]

    @pl.when(is_polar == 1)
    def _():
        half = depth // 2
        zero = jnp.zeros((1, depth, points), F32)
        wide[0:1] = zero
        wide[polar + 1 :] = zero
        shape = (depth, points)
        field = lanes(shape) // FIELD
        low = low_half(jnp.zeros(shape, F32))
        for group in range(polar // FIELDS):
            own, outer = jnp.zeros(shape, F32), jnp.zeros(shape, F32)
            for f in range(FIELDS):
                i = group * FIELDS + f
                lines = [smooth_ref[2 * i], smooth_ref[2 * i + 1]]
                row = jnp.concatenate([line[0:half] for line in lines], axis=0)
                caps_ref[i] = row
                wide[1 + i] = row
                edges = [shift(line[half:], FIELD * (f - t)) for line in lines for t in range(half // 8)]
                own = jnp.where(field == f, shift(row, FIELD * f + 8), own)
                outer = jnp.where(field == f, jnp.concatenate(edges, axis=0), outer)
            left, right = jnp.where(low, outer, own), jnp.where(low, own, outer)
            place = 1 + start // FIELDS + group
            held[0, place, 0:depth] = left
            held[1, place, 0:depth] = right
            polar_strips[group] = beyond(left[0:levels], right[0:levels])
        u, v, theta = [component(wide[...], which) for which in range(3)]
        here = pl.ds(first + start, polar)
        t0[here] = t0[here] + rhs(
            u[1:-1], theta[1:-1], v[:-2], v[2:], insertions(polar_strips[...], 0, polar)
        )

        @pl.when(start == 0)
        def _():
            e = first + polar
            t0[e : e + 1] = t0[e : e + 1] + 0.5 * v[polar : polar + 1]

        @pl.when(start != 0)
        def _():
            e = last - polar
            t0[e : e + 1] = t0[e : e + 1] - 0.5 * v[1:2]

    def beside_rows(x):
        lane = lanes(x.shape)
        down, up = shift(x, FIELD), shift(x, -FIELD)
        before = jnp.concatenate([down[:, :1], down[:, :-1]], axis=1)
        after = jnp.concatenate([up[:, 1:], up[:, -1:]], axis=1)
        return jnp.where(lane < FIELD, before, down), jnp.where(lane >= 128 - FIELD, after, up)

    def masked(x):
        return jnp.concatenate([top * x[:, :1], x[:, 1:-1], bottom * x[:, -1:]], axis=1)

    def keep(k, x):
        side[k] = x
        past_ref[k] = beyond(x[0], x[1])

    u = held[:, :, 0:levels]
    north, south = beside_rows(held[:, :, levels : 2 * levels])
    keep(0, masked(
        held[:, :, 2 * levels : depth] - 0.5 * (shift(u, -1) - shift(u, 1) + (south - north))
    ))
    side_slope[...] = (4.0 / 9.0) * (held[:, :, depth:] - 0.5)
    for k in range(ITERS - 1):
        here = side[k]
        north, south = beside_rows(here)
        twice = side_slope[...] * here - (4.0 / 9.0) * (shift(here, 1) + shift(here, -1) + (north + south))
        keep(k + 1, masked(0.5 * twice if k == 0 else twice - side[k - 1]))

    loads[2].wait()
    sums = []
    for k in range(ITERS):
        now = table[k]

        def following(e, count, stiff, inserted):
            here = now[pl.ds(e, count)]
            beside = shifted(here, neighbours) + inserted + (now[pl.ds(e - 1, count)] + now[pl.ds(e + 1, count)])
            twice = (4.0 / 9.0) * ((stiff - 0.5) * here - beside)
            if k == 0:
                return here, 0.5 * twice
            return here, twice - table[k - 1][pl.ds(e, count)]

        def step(i, carry):
            squares, cross = carry
            e = FIELDS + i * stride
            packed = past_ref[k, pl.ds(1 + i * (stride // FIELDS), stride // FIELDS)]
            here, value = following(e, stride, slope_ref[pl.ds(i * stride, stride)], insertions(packed, 0, stride))
            if k < ITERS - 1:
                table[k + 1][pl.ds(e, stride)] = value
            return squares + jnp.sum(here * here, axis=0), cross + jnp.sum(here * value, axis=0)

        zero = jnp.zeros((levels, points), F32)
        sums.append(lax.fori_loop(0, rows // stride, step, (zero, zero)))
        if k < ITERS - 1:
            reach = ITERS - 1 - k
            table[k + 1][first - reach : first] = top * following(
                first - reach, reach, above_ref[FIELDS - reach : FIELDS, depth:],
                insertions(past_ref[k, 0:1], FIELDS - reach, reach),
            )[1]
            table[k + 1][last + 1 : last + 1 + reach] = bottom * following(
                last + 1, reach, below_ref[0:reach, depth:], insertions(past_ref[k, groups + 1 :], 0, reach)
            )[1]

    lane = lanes((1, points))
    moments = jnp.zeros((1, points), F32)
    for i, value in enumerate([a for a, _ in sums] + [b for _, b in sums]):
        total = jnp.sum(jnp.sum(value, axis=0, keepdims=True), axis=1, keepdims=True)
        moments = jnp.where(lane == i, total, moments)
    moments_ref[...] = jnp.broadcast_to(moments, moments_ref.shape)


def make_basis(info, above, below, begun, sides, stiffness, ends, smooth, polar, devices):
    rows, levels, points = stiffness.shape
    depth = 3 * levels
    groups = rows // FIELDS + 2
    both = depth + levels
    vmem = pl.BlockSpec(memory_space=pltpu.VMEM)
    return pl.pallas_call(
        basis_kernel,
        in_specs=[pl.BlockSpec(memory_space=pltpu.SMEM)] + [pl.BlockSpec(memory_space=pl.ANY)] * 5 + [vmem] * 2,
        out_specs=(vmem,) * (ITERS + 3),
        out_shape=(pltpu.VMEM((rows + 2 * FIELDS, levels, points), F32),) * ITERS
        + (
            pltpu.VMEM((ITERS, groups, levels, points), F32),
            pltpu.HBM((polar, depth, points), F32),
            jax.ShapeDtypeStruct((devices, points), F32),
        ),
        scratch_shapes=[
            pltpu.VMEM((2, groups, both, points), F32),
            pltpu.VMEM(stiffness.shape, F32),
            pltpu.VMEM((polar + 2, depth, points), F32),
            pltpu.VMEM((polar // FIELDS, levels, points), F32),
            pltpu.VMEM((ITERS, 2, groups, levels, points), F32),
            pltpu.VMEM((2, groups, levels, points), F32),
            pltpu.VMEM(above.shape, F32),
            pltpu.VMEM(below.shape, F32),
            pltpu.SemaphoreType.DMA((5,)),
        ],
        cost_estimate=pl.CostEstimate(flops=40000000, bytes_accessed=24000000, transcendentals=0),
        compiler_params=params(16),
        name="basis",
    )(info, *[in_hbm(x) for x in (above, below, begun, sides, stiffness)], ends, smooth)


def solve(mu):
    gram = [[0.5 * (mu[i + j] + mu[abs(i - j)]) for j in range(ITERS + 1)] for i in range(ITERS)]

    def inner(a, b):
        return tree([x * tree([y * gram[i][j] for j, y in enumerate(b)]) for i, x in enumerate(a)])

    def image_of(a):
        out = [4.5 * x for x in a] + [jnp.zeros_like(a[0])]
        for k, x in enumerate(a):
            out[k + 1] = out[k + 1] + 2.25 * x
            out[abs(k - 1)] = out[abs(k - 1)] + 2.25 * x
        return out

    zero = jnp.zeros_like(mu[0])
    phi = []
    residual = [zero + 1.0]
    direction = residual
    norm = mu[0]
    for step in range(ITERS):
        image = image_of(direction)
        alpha = norm / inner(direction, image)
        phi = [x + alpha * y for x, y in zip(phi + [zero], direction)]
        if step < ITERS - 1:
            residual = [x - alpha * y for x, y in zip(residual + [zero], image)]
            following = inner(residual, residual)
            ratio = following / norm
            direction = [x + ratio * y for x, y in zip(residual, direction + [zero])]
            norm = following
    return phi


def finish_kernel(
    info_ref, spread_ref, filtered_hbm, caps_hbm, t0, t1, t2, t3, t4, past_ref, out_ref,
    coefficient_ref, filtered_ref, caps_ref, sems,
):
    table = [t0, t1, t2, t3, t4]
    _, levels, points = t0.shape
    block = out_ref.shape[0]
    g = pl.program_id(0)

    def fetch(i):
        part = pl.ds(i * block, block)
        return pltpu.make_async_copy(filtered_hbm.at[part], filtered_ref.at[part], sems.at[i])

    polar = caps_ref.shape[0]
    start, is_polar = info_ref[0], info_ref[1]
    fetch_caps = pltpu.make_async_copy(caps_hbm, caps_ref, sems.at[filtered_ref.shape[0] // block])

    @pl.when(g == 0)
    def _():
        fetch_caps.start()
        for i in range(filtered_ref.shape[0] // block):
            fetch(i).start()
        total = jnp.sum(spread_ref[...], axis=0, keepdims=True)
        lane = lanes(total.shape)
        picked = [
            jnp.sum(jnp.where(lane == i, total, 0.0), axis=1, keepdims=True) for i in range(2 * ITERS)
        ]
        mu = [picked[0], picked[ITERS]]
        for k in range(1, ITERS):
            mu += [2.0 * picked[k] - mu[0], 2.0 * picked[ITERS + k] - mu[1]]
        for k, value in enumerate(solve(mu)):
            coefficient_ref[k] = jnp.broadcast_to(value, (8, points))

    c = [jnp.concatenate([coefficient_ref[k]] * (levels // 8), axis=0) for k in range(ITERS)]

    fetch(g).wait()

    @pl.when(g == 0)
    def _():
        fetch_caps.wait()

    @pl.when((is_polar == 1) & (g == start // block))
    def _():
        filtered_ref[pl.ds(start, polar)] = caps_ref[...]

    def phi_of(e):
        return tree([c[k] * table[k][e] for k in range(ITERS)])

    lane = lanes((levels, points))
    stride = FIELDS

    def step(i, carry):
        first = i * stride
        row = g * block + first
        near = list(carry) + [phi_of(FIELDS + row + 1 + j) for j in range(stride)]
        packed = tree([c[k] * past_ref[k, 1 + row // FIELDS] for k in range(ITERS)])
        old = [filtered_ref[row + j] for j in range(stride)]
        new = []
        for j in range(stride):
            here = near[j + 1]
            inserted = unpack_lanes(packed, j)
            east = jnp.where(lane == points - 1, inserted, shift(here, -1))
            west = jnp.where(lane == 0, inserted, shift(here, 1))
            new.append(old[j][0:levels] - 0.5 * (east - west))
            new.append(old[j][levels : 2 * levels] - 0.5 * (near[j + 2] - near[j]))
            new.append(old[j][2 * levels :] - here)
        for j in range(stride):
            for part in range(3):
                out_ref[first + j, part * levels : (part + 1) * levels] = new[3 * j + part]
        return near[stride], near[stride + 1]

    e = FIELDS + g * block
    lax.fori_loop(0, block // stride, step, (phi_of(e - 1), phi_of(e)))


def finish(info, spread, filtered, caps, table):
    rows, depth, points = filtered.shape
    block = 32
    vmem = pl.BlockSpec(memory_space=pltpu.VMEM)
    piece = pl.BlockSpec((block, depth, points), lambda g: (g, 0, 0))
    return pl.pallas_call(
        finish_kernel,
        grid=(rows // block,),
        in_specs=[pl.BlockSpec(memory_space=pltpu.SMEM), vmem] + [pl.BlockSpec(memory_space=pl.ANY)] * 2 + [vmem] * (ITERS + 1),
        out_specs=piece,
        out_shape=jax.ShapeDtypeStruct((rows, depth, points), F32),
        scratch_shapes=[
            pltpu.VMEM((ITERS, 8, points), F32),
            pltpu.VMEM((rows, depth, points), F32),
            pltpu.VMEM(caps.shape, F32),
            pltpu.SemaphoreType.DMA((rows // block + 1,)),
        ],
        cost_estimate=pl.CostEstimate(flops=20000000, bytes_accessed=17000000, transcendentals=0),
        compiler_params=params(12),
        name="finish",
    )(info, spread, in_hbm(filtered), in_hbm(caps), *table)


def shards(state, weights, owners, source_rows, cutoffs, stiffness):
    rows, comps, levels, points = state.shape
    depth = comps * levels
    n_lon = lax.axis_size("lon")
    n_lat = lax.axis_size("lat")
    devices = n_lon * n_lat
    band = lax.axis_index("lat")
    north, south = band == 0, band == n_lat - 1
    polar = cutoffs.shape[0] // 2
    line = lax.axis_index("lon") * polar // n_lon
    info = jnp.stack(
        [
            jnp.where(north, 0, rows - polar),
            (north | south).astype(jnp.int32),
            (band > 0).astype(jnp.int32),
            (band < n_lat - 1).astype(jnp.int32),
            cutoffs[jnp.where(north, line, polar + line)],
        ]
    ).astype(jnp.int32)

    requests, place = make_requests(owners[:, :, 0], source_rows)
    asked = exchange(requests, BOTH)[:, :2]
    asked, ahead, ahead_weights = lax.optimization_barrier((asked, stiffness, weights))
    moved = exchange(state[asked], BOTH).reshape(2 * devices, depth, points)
    moved, rim_weights, *stiff = lax.optimization_barrier(
        (moved, edge_weights(ahead_weights)) + tuple(pack_stiffness(ahead))
    )

    place = place[0]
    caps, last, first = make_caps(place, info, moved, weights, stiffness, polar)
    lines = exchange(caps.reshape(n_lon, -1, points), "lon")
    place, caps = lax.optimization_barrier((place, caps))
    to_east, to_west, own = make_edges(place, moved, rim_weights, stiff)
    west, east = from_sides(to_east, to_west)
    passed = low_pass(info, lines)
    smooth = exchange(passed, "lon")
    _, west_late, east_late = lax.optimization_barrier((passed, west, east))
    above, below = from_ends(*make_ends(last, first, west_late, east_late))
    arrived, begun, sides, near = prepare(place, info, moved, weights, west, east, own)
    *table, caps, moments = make_basis(info, above, below, begun, sides, stiffness, near, smooth, polar, devices)
    out = finish(info, exchange(moments, BOTH), arrived, caps, table)
    return out.reshape(rows, comps, levels, points)


def solution(mesh):
    in_specs = (
        P("lat", None, None, "lon"),
        P("lat", None, "lon"),
        P("lon", "lat", None),
        P("lon", "lat"),
        P(),
        P("lat", None, "lon"),
    )
    out_specs = P("lat", None, None, "lon")
    return jax.shard_map(shards, mesh=mesh, in_specs=in_specs, out_specs=out_specs, check_vma=False)
```

time: 154 us -> 148 us (0.961)
  waiting for transfers between devices: 48.6 us -> 28.2 us
  Pallas kernels: 37.8 us -> 49.6 us
  blocking collectives: 36.4 us -> 38.3 us
    pallas_call x3 -> x6, Pallas kernels: 17.6 us -> 36.4 us  [the longest x1 10.3 us: edge_weights(): pl.pallas_call(edge_weights_kernel, grid=(rows // FIELDS,), in_specs=[pl....]
    all_to_all x3, waiting for transfers between devices: 40.3 us -> 26.7 us  [exchange(): return lax.all_to_all(block, axes, split_axis=0, concat_axis=0, tiled=True)]
    ppermute x2, waiting for transfers between devices: 8.25 us -> 0.01 us  [from_ends(): return (lax.ppermute(last, 'lat', north), lax.ppermute(first, 'lat', south))]
    pallas_call x1, Pallas kernels: 14.6 us -> 8.65 us  [make_basis(): pl.pallas_call(basis_kernel, in_specs=[pl.BlockSpec(memory_space=pltpu.SM...]
    all_to_all x2, blocking collectives: 36.4 us -> 38.3 us  [exchange(): return lax.all_to_all(block, axes, split_axis=0, concat_axis=0, tiled=True)]
  transfers between devices with their start and end apart: 7 -> 7, of which waited for: 3 -> 3; matrix products, arithmetic and copies ran while one was open for 1% -> 1% of each run, Pallas kernels for 9% -> 21%
where the time goes in v3:
time: 148 us
  Pallas kernels  49.6 us (34%)
  blocking collectives  38.3 us (26%)
  waiting for transfers between devices  28.2 us (19%)
  starting transfers between devices  26.1 us (18%)
  local copies, waits for them, and re-layouts  4.93 us (3%)
    all_to_all x2, blocking collectives, exchange(): return lax.all_to_all(block, axes, split_axis=0, concat_axis=0, tiled=True)  38.3 us
    all_to_all x3, waiting for transfers between devices, exchange(): return lax.all_to_all(block, axes, split_axis=0, concat_axis=0, tiled=True)  26.7 us
    all_to_all x3, starting transfers between devices, exchange(): return lax.all_to_all(block, axes, split_axis=0, concat_axis=0, tiled=True)  13.5 us
    pallas_call x1, Pallas kernels, edge_weights(): pl.pallas_call(edge_weights_kernel, grid=(rows // FIELDS,), in_specs=[pl....  10.3 us
    pallas_call x1, Pallas kernels, prepare(): pl.pallas_call(prepare_kernel, in_specs=[pl.BlockSpec(memory_space=pltpu....  9.36 us
    pallas_call x1, Pallas kernels, make_basis(): pl.pallas_call(basis_kernel, in_specs=[pl.BlockSpec(memory_space=pltpu.SM...  8.65 us
    ppermute x2, starting transfers between devices, from_ends(): return (lax.ppermute(last, 'lat', north), lax.ppermute(first, 'lat', south))  6.92 us
    pallas_call x1, Pallas kernels, finish(): pl.pallas_call(finish_kernel, grid=(rows // block,), in_specs=[pl.BlockSp...  5.34 us
  transfers between devices with their start and end apart: 7, of which 3 were waited for; matrix products, arithmetic and copies ran while one was open for 1% of the time, Pallas kernels for 21%

profile of v3, /device:TPU:1, one launch (start us, length us, event | category | flops | bytes accessed | tf_op | source)
XLA Modules:
  0.0 147.6 jit_solution(14728895537446816170)
XLA Ops:
  0.0 0.0 copy-start
  0.0 1.0 requests.1
  1.0 20.8 %all_to_all.38 = s32[128,1,128]{2,1,0:T(1,128)S(1)} all-to-all(s32[128,1,128]{2,1,0:T(1,128)S(1)} %bitcast.21), channel_id=1, replica_groups=mesh['lon'=32,'lat'=4] {'lon','lat'}, dimensions={0} | all-to-all | bytes 131072 | tf_op jit(solution)/shard_map/all_to_all | solution.py:29
  21.9 0.1 reshape.21
  22.0 0.0 copy-done
  22.0 2.6 %gather_fusion = bf16[256,3,16,128]{3,2,1,0:T(8,128)(2,1)} fusion(bf16[128,3,16,128]{3,2,1,0:T(8,128)(2,1)S(1)} %copy-done, s32[1024]{0:T(1024)S(1)} %pad_clamp_fusion), kind=kCustom, calls=%fused_computation | custom fusion | bytes 6292480 | tf_op jit(solution)/shard_map/gather | solution.py:973
  24.7 0.0 copy-start.5
  24.7 5.7 %all-to-all-start.1 = ((bf16[128,2,3,16,128]{4,3,2,1,0:T(8,128)(2,1)}), bf16[128,2,3,16,128]{4,3,2,1,0:T(8,128)(2,1)}, u32[]{:S(2)}, u32[]{:S(2)}) async-start(bf16[128,2,3,16,128]{4,3,2,1,0:T(8,128)(2,1)} %bitcast.25), calls=%async_computation.1 | async-start | bytes 6291456 | tf_op jit(solution)/shard_map/all_to_all | solution.py:29
  30.4 0.0 copy-done.5
  30.4 0.6 dynamic_slice.3
  31.0 0.7 stack.31.info_ref
  31.7 3.3 %pack_stiffness.1 = (f32[8,16,128]{2,1,0:T(8,128)}, f32[8,16,128]{2,1,0:T(8,128)}, f32[16,16,128]{2,1,0:T(8,128)}) custom-call(f32[128,16,128]{2,1,0:T(8,128)} %stiffness_hbm.3), custom_call_target="tpu_custom_call" | custom-call | flops 1000000 | bytes 1300000 | tf_op jit(solution)/shard_map/pack_stiffness/pallas_call | solution.py:211
  35.0 10.3 %edge_weights.1.weights_hbm = bf16[16,128,128]{2,1,0:T(8,128)(2,1)} custom-call(bf16[128,128,128]{2,1,0:T(8,128)(2,1)} %weights_hbm.3), custom_call_target="tpu_custom_call" | custom-call | flops 2000000 | bytes 5000000 | tf_op jit(solution)/shard_map/edge_weights/pallas_call | solution.py:227
  45.3 26.6 %all-to-all-done.1 = bf16[128,2,3,16,128]{4,3,2,1,0:T(8,128)(2,1)} async-done(((bf16[128,2,3,16,128]{4,3,2,1,0:T(8,128)(2,1)}), bf16[128,2,3,16,128]{4,3,2,1,0:T(8,128)(2,1)}, u32[]{:S(2)}, u32[]{:S(2)}) %all-to-all-start.1) | async-done | bytes 3145760 | tf_op jit(solution)/shard_map/all_to_all | solution.py:29
  71.9 3.3 %caps.1 = (f32[16,48,128]{2,1,0:T(8,128)}, f32[9,64,128]{2,1,0:T(8,128)S(1)}, f32[9,64,128]{2,1,0:T(8,128)S(1)}) custom-call(s32[128]{0:T(128)S(1)} %bitcast.22, s32[5]{0:T(128)S(1)} %stack.31.info_ref, bf16[256,48,128]{2,1,0:T(8,128)(2,1)} %bitcast.10.moved_hbm, bf16[128,128,128]{2,1,0:T(8,128)(2,1)} %weights_hbm.3, f32[128,16,128]{2,1,0:T(8,128)} %stiffness_hbm.3), custom_call_target="tpu_custom_call" | custom-call | flops 60000000 | bytes 2400000 | tf_op jit(solution)/shard_map/caps/pallas_call | solution.py:177
  75.3 3.9 %all-to-all-start.2 = ((f32[32,24,128]{2,1,0:T(8,128)}), f32[32,24,128]{2,1,0:T(8,128)S(1)}, u32[]{:S(2)}, u32[]{:S(2)}) async-start(f32[32,24,128]{2,1,0:T(8,128)} %bitcast.11), calls=%async_computation.2 | async-start | bytes 786432 | tf_op jit(solution)/shard_map/all_to_all | solution.py:29
  79.2 4.7 %edges.1 = (f32[8,64,128]{2,1,0:T(8,128)}, f32[8,64,128]{2,1,0:T(8,128)S(1)}, f32[16,64,128]{2,1,0:T(8,128)}) custom-call(s32[128]{0:T(128)S(1)} %bitcast.23, bf16[256,48,128]{2,1,0:T(8,128)(2,1)} %bitcast.10.moved_hbm, f32[8,16,128]{2,1,0:T(8,128)} %get-tuple-element.54.east_hbm, f32[8,16,128]{2,1,0:T(8,128)} %get-tuple-element.55.west_hbm, ...), custom_call_target="tpu_custom_call" | custom-call | flops 10000000000 | bytes 5000000 | tf_op jit(solution)/shard_map/edges/pallas_call | solution.py:290
  83.9 1.2 collective-permute-start
  85.1 4.6 %collective-permute-start.1 = (f32[8,64,128]{2,1,0:T(8,128)S(1)}, f32[8,64,128]{2,1,0:T(8,128)S(1)}, u32[]{:S(2)}, u32[]{:S(2)}) collective-permute-start(f32[8,64,128]{2,1,0:T(8,128)S(1)} %get-tuple-element.59), channel_id=1, source_target_pairs={{4,0},{8,4},{12,8},{16,12},{20,16},{24,20},{28,24},{32,28},{36,32}... | collective-permute-start | bytes 786440 | tf_op jit(solution)/shard_map/ppermute | solution.py:87
  89.7 0.0 all-to-all-done.2.lines_ref
  89.7 3.5 %low_pass.1 = f32[32,32,128]{2,1,0:T(8,128)} custom-call(s32[5]{0:T(128)S(1)} %stack.31.info_ref, f32[32,24,128]{2,1,0:T(8,128)S(1)} %all-to-all-done.2.lines_ref, f32[34,128]{1,0:T(8,128)} %constant.42.clone.twist_hbm, bf16[2,256,256]{2,1,0:T(8,128)(2,1)} %constant.43.clone.forward_hbm, bf16[2,256,256]{2,1,0:T(8,128)(2,1)} %constant.44.clone.inverse_hbm), custom_call_target="tpu_custom_call" | custom-call | flops 700000000 | bytes 1400000 | tf_op jit(solution)/shard_map/low_pass/pallas_call | solution.py:460
  93.2 3.9 %all-to-all-start.3 = ((f32[32,32,128]{2,1,0:T(8,128)}), f32[32,32,128]{2,1,0:T(8,128)S(1)}, u32[]{:S(2)}, u32[]{:S(2)}) async-start(f32[32,32,128]{2,1,0:T(8,128)} %low_pass.1), calls=%async_computation.3 | async-start | bytes 1048576 | tf_op jit(solution)/shard_map/all_to_all | solution.py:29
  97.1 0.3 collective-permute-done.west_ref.west_hbm
  97.4 0.0 copy-start.1
  97.4 1.3 collective-permute-done.1.east_ref.east_hbm
  98.7 0.0 copy-start.2
  98.7 0.1 ends.1
  98.8 5.0 %collective-permute-start.2 = (f32[10,64,128]{2,1,0:T(8,128)S(1)}, f32[10,64,128]{2,1,0:T(8,128)S(1)}, u32[]{:S(2)}, u32[]{:S(2)}) collective-permute-start(f32[10,64,128]{2,1,0:T(8,128)S(1)} %get-tuple-element.62), channel_id=1, source_target_pairs={{0,1},{1,2},{2,3},{4,5},{5,6},{6,7},{8,9},{9,10},{10,11},{12,13},{... | collective-permute-start | bytes 983048 | tf_op jit(solution)/shard_map/ppermute | solution.py:92
  103.8 1.9 %collective-permute-start.3 = (f32[10,64,128]{2,1,0:T(8,128)S(1)}, f32[10,64,128]{2,1,0:T(8,128)S(1)}, u32[]{:S(2)}, u32[]{:S(2)}) collective-permute-start(f32[10,64,128]{2,1,0:T(8,128)S(1)} %get-tuple-element.63), channel_id=1, source_target_pairs={{1,0},{2,1},{3,2},{5,4},{6,5},{7,6},{9,8},{10,9},{11,10},{13,12},{... | collective-permute-start | bytes 983048 | tf_op jit(solution)/shard_map/ppermute | solution.py:92
  105.7 0.0 copy-done.1
  105.7 0.0 copy-done.2
  105.7 9.4 %prepare.1 = (f32[128,48,128]{2,1,0:T(8,128)}, f32[128,16,128]{2,1,0:T(8,128)}, f32[2,16,64,128]{3,2,1,0:T(8,128)}, f32[2,16,128]{2,1,0:T(8,128)S(1)}) custom-call(s32[128]{0:T(128)S(1)} %bitcast.24, s32[5]{0:T(128)S(1)} %stack.31.info_ref, bf16[256,48,128]{2,1,0:T(8,128)(2,1)} %bitcast.10.moved_hbm, bf16[128,128,128]{2,1,0:T(8,128)(2,1)} %weights_hbm.3, ...), custom_call_target="tpu_custom_call" | custom-call | flops 20000000000 | bytes 16000000 | tf_op jit(solution)/shard_map/prepare/pallas_call | solution.py:584
  115.1 0.0 collective-permute-done.2.above_hbm
  115.1 0.0 copy-start.3
  115.1 0.0 collective-permute-done.3.below_hbm
  115.1 0.0 copy-start.4
  115.1 0.0 all-to-all-done.3.smooth_ref
  115.1 0.7 copy-done.3
  115.8 0.1 copy-done.4
  116.0 8.7 %basis.1 = (f32[144,16,128]{2,1,0:T(8,128)S(1)}, f32[144,16,128]{2,1,0:T(8,128)S(1)}, f32[144,16,128]{2,1,0:T(8,128)S(1)}, f32[144,16,128]{2,1,0:T(8,128)S(1)}, ...) custom-call(s32[5]{0:T(128)S(1)} %stack.31.info_ref, ...), custom_call_target="tpu_custom_call" | custom-call | flops 40000000 | bytes 24000000 | tf_op jit(solution)/shard_map/basis/pallas_call | solution.py:794
  124.6 17.5 %all_to_all.39 = f32[128,1,128]{2,1,0:T(1,128)S(1)} all-to-all(f32[128,1,128]{2,1,0:T(1,128)S(1)} %bitcast.20), channel_id=1, replica_groups=mesh['lon'=32,'lat'=4] {'lon','lat'}, dimensions={0} | all-to-all | bytes 131072 | tf_op jit(solution)/shard_map/all_to_all | solution.py:29
  142.1 5.3 %finish.1 = f32[128,48,128]{2,1,0:T(8,128)} custom-call(s32[5]{0:T(128)S(1)} %stack.31.info_ref, f32[128,128]{1,0:T(8,128)S(1)} %bitcast.19, f32[128,48,128]{2,1,0:T(8,128)} %get-tuple-element.69.filtered_hbm, f32[16,48,128]{2,1,0:T(8,128)} %get-tuple-element.70.caps_hbm, f32[144,16,128]{2,1,0:T(8,128)S(1)} %get-tuple-element.71.t0, ...), custom_call_target="tpu_custom_call" | custom-call | flops 20000000 | bytes 17000000 | tf_op jit(solution)/shard_map/finish/pallas_call | solution.py:932
  (2 shorter events, 0.0 us)
Async XLA Ops:
  0.0 22.0 %copy-start = (bf16[128,3,16,128]{3,2,1,0:T(8,128)(2,1)S(1)}, bf16[128,3,16,128]{3,2,1,0:T(8,128)(2,1)}, u32[]{:S(2)}) copy-start(bf16[128,3,16,128]{3,2,1,0:T(8,128)(2,1)} %param.9) | copy-start | bytes 4718596
  24.7 5.7 %copy-start.5 = (s32[32]{0:T(128)S(1)}, s32[32]{0:T(128)}, u32[]{:S(2)}) copy-start(s32[32]{0:T(128)} %param.13) | copy-start | bytes 388
  24.7 47.3 %all-to-all-start.1 = ((bf16[128,2,3,16,128]{4,3,2,1,0:T(8,128)(2,1)}), bf16[128,2,3,16,128]{4,3,2,1,0:T(8,128)(2,1)}, u32[]{:S(2)}, u32[]{:S(2)}) async-start(bf16[128,2,3,16,128]{4,3,2,1,0:T(8,128)(2,1)} %bitcast.25), calls=%async_computation.1 | async-start | bytes 6291456 | tf_op jit(solution)/shard_map/all_to_all | solution.py:29
  75.3 14.4 %all-to-all-start.2 = ((f32[32,24,128]{2,1,0:T(8,128)}), f32[32,24,128]{2,1,0:T(8,128)S(1)}, u32[]{:S(2)}, u32[]{:S(2)}) async-start(f32[32,24,128]{2,1,0:T(8,128)} %bitcast.11), calls=%async_computation.2 | async-start | bytes 786432 | tf_op jit(solution)/shard_map/all_to_all | solution.py:29
  83.9 13.4 %collective-permute-start = (f32[8,64,128]{2,1,0:T(8,128)}, f32[8,64,128]{2,1,0:T(8,128)S(1)}, u32[]{:S(2)}, u32[]{:S(2)}) collective-permute-start(f32[8,64,128]{2,1,0:T(8,128)} %get-tuple-element.58), channel_id=1, source_target_pairs={{0,4},{4,8},{8,12},{12,16},{16,20},{20,24},{24,28},{28,32},{32,36}... | collective-permute-start | bytes 786440 | tf_op jit(solution)/shard_map/ppermute | solution.py:87
  85.1 13.5 %collective-permute-start.1 = (f32[8,64,128]{2,1,0:T(8,128)S(1)}, f32[8,64,128]{2,1,0:T(8,128)S(1)}, u32[]{:S(2)}, u32[]{:S(2)}) collective-permute-start(f32[8,64,128]{2,1,0:T(8,128)S(1)} %get-tuple-element.59), channel_id=1, source_target_pairs={{4,0},{8,4},{12,8},{16,12},{20,16},{24,20},{28,24},{32,28},{36,32}... | collective-permute-start | bytes 786440 | tf_op jit(solution)/shard_map/ppermute | solution.py:87
  93.2 21.9 %all-to-all-start.3 = ((f32[32,32,128]{2,1,0:T(8,128)}), f32[32,32,128]{2,1,0:T(8,128)S(1)}, u32[]{:S(2)}, u32[]{:S(2)}) async-start(f32[32,32,128]{2,1,0:T(8,128)} %low_pass.1), calls=%async_computation.3 | async-start | bytes 1048576 | tf_op jit(solution)/shard_map/all_to_all | solution.py:29
  97.4 8.3 %copy-start.1 = (f32[8,64,128]{2,1,0:T(8,128)}, f32[8,64,128]{2,1,0:T(8,128)S(1)}, u32[]{:S(2)}) copy-start(f32[8,64,128]{2,1,0:T(8,128)S(1)} %collective-permute-done.west_ref.west_hbm) | copy-start | bytes 786436
  98.7 7.0 %copy-start.2 = (f32[8,64,128]{2,1,0:T(8,128)}, f32[8,64,128]{2,1,0:T(8,128)S(1)}, u32[]{:S(2)}) copy-start(f32[8,64,128]{2,1,0:T(8,128)S(1)} %collective-permute-done.1.east_ref.east_hbm) | copy-start | bytes 786436
  98.8 16.3 %collective-permute-start.2 = (f32[10,64,128]{2,1,0:T(8,128)S(1)}, f32[10,64,128]{2,1,0:T(8,128)S(1)}, u32[]{:S(2)}, u32[]{:S(2)}) collective-permute-start(f32[10,64,128]{2,1,0:T(8,128)S(1)} %get-tuple-element.62), channel_id=1, source_target_pairs={{0,1},{1,2},{2,3},{4,5},{5,6},{6,7},{8,9},{9,10},{10,11},{12,13},{... | collective-permute-start | bytes 983048 | tf_op jit(solution)/shard_map/ppermute | solution.py:92
  103.8 11.3 %collective-permute-start.3 = (f32[10,64,128]{2,1,0:T(8,128)S(1)}, f32[10,64,128]{2,1,0:T(8,128)S(1)}, u32[]{:S(2)}, u32[]{:S(2)}) collective-permute-start(f32[10,64,128]{2,1,0:T(8,128)S(1)} %get-tuple-element.63), channel_id=1, source_target_pairs={{1,0},{2,1},{3,2},{5,4},{6,5},{7,6},{9,8},{10,9},{11,10},{13,12},{... | collective-permute-start | bytes 983048 | tf_op jit(solution)/shard_map/ppermute | solution.py:92
  115.1 0.7 copy-start.3
  115.1 0.9 copy-start.4

commit v4 on v3

--- a/solution.py
+++ b/solution.py
@@ -275,7 +275,7 @@
             own_ref[2 * g + h, 0:depth] = packed[h]
         return carry
 
-    lax.fori_loop(0, east_ref.shape[0], pair, 0, unroll=2)
+    lax.fori_loop(0, east_ref.shape[0], pair, 0, unroll=True)
     for load in loads[2:]:
         load.wait()
 
@@ -921,7 +921,7 @@
         return near[stride], near[stride + 1]
 
     e = FIELDS + g * block
-    lax.fori_loop(0, block // stride, step, (phi_of(e - 1), phi_of(e)))
+    lax.fori_loop(0, block // stride, step, (phi_of(e - 1), phi_of(e)), unroll=True)
 
 
 def finish(info, spread, filtered, caps, table):

time: 148 us -> 147 us (level)
  no operation moved by 1% of the time
where the time goes in v4:
time: 147 us; the launch traced here: 146 us
  Pallas kernels  48.2 us (33%)
  blocking collectives  37.6 us (26%)
  waiting for transfers between devices  29.2 us (20%)
  starting transfers between devices  25.9 us (18%)
  local copies, waits for them, and re-layouts  4.93 us (3%)
    all_to_all x2, blocking collectives, exchange(): return lax.all_to_all(block, axes, split_axis=0, concat_axis=0, tiled=True)  37.6 us
    all_to_all x3, waiting for transfers between devices, exchange(): return lax.all_to_all(block, axes, split_axis=0, concat_axis=0, tiled=True)  26.7 us
    all_to_all x3, starting transfers between devices, exchange(): return lax.all_to_all(block, axes, split_axis=0, concat_axis=0, tiled=True)  13.5 us
    pallas_call x1, Pallas kernels, edge_weights(): pl.pallas_call(edge_weights_kernel, grid=(rows // FIELDS,), in_specs=[pl....  10.3 us
    pallas_call x1, Pallas kernels, prepare(): pl.pallas_call(prepare_kernel, in_specs=[pl.BlockSpec(memory_space=pltpu....  9.37 us
    pallas_call x1, Pallas kernels, make_basis(): pl.pallas_call(basis_kernel, in_specs=[pl.BlockSpec(memory_space=pltpu.SM...  8.65 us
    ppermute x2, starting transfers between devices, from_ends(): return (lax.ppermute(last, 'lat', north), lax.ppermute(first, 'lat', south))  6.66 us
    pallas_call x1, Pallas kernels, finish(): pl.pallas_call(finish_kernel, grid=(rows // block,), in_specs=[pl.BlockSp...  4.61 us
  transfers between devices with their start and end apart: 7, of which 3 were waited for; matrix products, arithmetic and copies ran while one was open for 1% of the time, Pallas kernels for 21%

profile of v4, /device:TPU:1, one launch (start us, length us, event | category | flops | bytes accessed | tf_op | source)
XLA Modules:
  0.0 146.2 jit_solution(6186333377307495895)
XLA Ops:
  0.0 0.0 copy-start
  0.0 1.0 requests.1
  1.0 20.8 %all_to_all.38 = s32[128,1,128]{2,1,0:T(1,128)S(1)} all-to-all(s32[128,1,128]{2,1,0:T(1,128)S(1)} %bitcast.21), channel_id=1, replica_groups=mesh['lon'=32,'lat'=4] {'lon','lat'}, dimensions={0} | all-to-all | bytes 131072 | tf_op jit(solution)/shard_map/all_to_all | solution.py:29
  21.9 0.1 reshape.21
  22.0 0.0 copy-done
  22.0 2.6 %gather_fusion = bf16[256,3,16,128]{3,2,1,0:T(8,128)(2,1)} fusion(bf16[128,3,16,128]{3,2,1,0:T(8,128)(2,1)S(1)} %copy-done, s32[1024]{0:T(1024)S(1)} %pad_clamp_fusion), kind=kCustom, calls=%fused_computation | custom fusion | bytes 6292480 | tf_op jit(solution)/shard_map/gather | solution.py:973
  24.7 0.0 copy-start.5
  24.7 5.7 %all-to-all-start.1 = ((bf16[128,2,3,16,128]{4,3,2,1,0:T(8,128)(2,1)}), bf16[128,2,3,16,128]{4,3,2,1,0:T(8,128)(2,1)}, u32[]{:S(2)}, u32[]{:S(2)}) async-start(bf16[128,2,3,16,128]{4,3,2,1,0:T(8,128)(2,1)} %bitcast.25), calls=%async_computation.1 | async-start | bytes 6291456 | tf_op jit(solution)/shard_map/all_to_all | solution.py:29
  30.4 0.0 copy-done.5
  30.4 0.6 dynamic_slice.3
  31.0 0.7 stack.31.info_ref
  31.7 3.3 %pack_stiffness.1 = (f32[8,16,128]{2,1,0:T(8,128)}, f32[8,16,128]{2,1,0:T(8,128)}, f32[16,16,128]{2,1,0:T(8,128)}) custom-call(f32[128,16,128]{2,1,0:T(8,128)} %stiffness_hbm.3), custom_call_target="tpu_custom_call" | custom-call | flops 1000000 | bytes 1300000 | tf_op jit(solution)/shard_map/pack_stiffness/pallas_call | solution.py:211
  35.0 10.3 %edge_weights.1.weights_hbm = bf16[16,128,128]{2,1,0:T(8,128)(2,1)} custom-call(bf16[128,128,128]{2,1,0:T(8,128)(2,1)} %weights_hbm.3), custom_call_target="tpu_custom_call" | custom-call | flops 2000000 | bytes 5000000 | tf_op jit(solution)/shard_map/edge_weights/pallas_call | solution.py:227
  45.3 26.6 %all-to-all-done.1 = bf16[128,2,3,16,128]{4,3,2,1,0:T(8,128)(2,1)} async-done(((bf16[128,2,3,16,128]{4,3,2,1,0:T(8,128)(2,1)}), bf16[128,2,3,16,128]{4,3,2,1,0:T(8,128)(2,1)}, u32[]{:S(2)}, u32[]{:S(2)}) %all-to-all-start.1) | async-done | bytes 3145760 | tf_op jit(solution)/shard_map/all_to_all | solution.py:29
  71.9 3.3 %caps.1 = (f32[16,48,128]{2,1,0:T(8,128)}, f32[9,64,128]{2,1,0:T(8,128)S(1)}, f32[9,64,128]{2,1,0:T(8,128)S(1)}) custom-call(s32[128]{0:T(128)S(1)} %bitcast.22, s32[5]{0:T(128)S(1)} %stack.31.info_ref, bf16[256,48,128]{2,1,0:T(8,128)(2,1)} %bitcast.10.moved_hbm, bf16[128,128,128]{2,1,0:T(8,128)(2,1)} %weights_hbm.3, f32[128,16,128]{2,1,0:T(8,128)} %stiffness_hbm.3), custom_call_target="tpu_custom_call" | custom-call | flops 60000000 | bytes 2400000 | tf_op jit(solution)/shard_map/caps/pallas_call | solution.py:177
  75.3 3.9 %all-to-all-start.2 = ((f32[32,24,128]{2,1,0:T(8,128)}), f32[32,24,128]{2,1,0:T(8,128)S(1)}, u32[]{:S(2)}, u32[]{:S(2)}) async-start(f32[32,24,128]{2,1,0:T(8,128)} %bitcast.11), calls=%async_computation.2 | async-start | bytes 786432 | tf_op jit(solution)/shard_map/all_to_all | solution.py:29
  79.2 4.1 %edges.1 = (f32[8,64,128]{2,1,0:T(8,128)}, f32[8,64,128]{2,1,0:T(8,128)S(1)}, f32[16,64,128]{2,1,0:T(8,128)}) custom-call(s32[128]{0:T(128)S(1)} %bitcast.23, bf16[256,48,128]{2,1,0:T(8,128)(2,1)} %bitcast.10.moved_hbm, f32[8,16,128]{2,1,0:T(8,128)} %get-tuple-element.54.east_hbm, f32[8,16,128]{2,1,0:T(8,128)} %get-tuple-element.55.west_hbm, ...), custom_call_target="tpu_custom_call" | custom-call | flops 10000000000 | bytes 5000000 | tf_op jit(solution)/shard_map/edges/pallas_call | solution.py:290
  83.3 1.2 collective-permute-start
  84.5 4.6 %collective-permute-start.1 = (f32[8,64,128]{2,1,0:T(8,128)S(1)}, f32[8,64,128]{2,1,0:T(8,128)S(1)}, u32[]{:S(2)}, u32[]{:S(2)}) collective-permute-start(f32[8,64,128]{2,1,0:T(8,128)S(1)} %get-tuple-element.59), channel_id=1, source_target_pairs={{4,0},{8,4},{12,8},{16,12},{20,16},{24,20},{28,24},{32,28},{36,32}... | collective-permute-start | bytes 786440 | tf_op jit(solution)/shard_map/ppermute | solution.py:87
  89.0 0.0 all-to-all-done.2.lines_ref
  89.0 3.5 %low_pass.1 = f32[32,32,128]{2,1,0:T(8,128)} custom-call(s32[5]{0:T(128)S(1)} %stack.31.info_ref, f32[32,24,128]{2,1,0:T(8,128)S(1)} %all-to-all-done.2.lines_ref, f32[34,128]{1,0:T(8,128)} %constant.42.clone.twist_hbm, bf16[2,256,256]{2,1,0:T(8,128)(2,1)} %constant.43.clone.forward_hbm, bf16[2,256,256]{2,1,0:T(8,128)(2,1)} %constant.44.clone.inverse_hbm), custom_call_target="tpu_custom_call" | custom-call | flops 700000000 | bytes 1400000 | tf_op jit(solution)/shard_map/low_pass/pallas_call | solution.py:460
  92.5 3.9 %all-to-all-start.3 = ((f32[32,32,128]{2,1,0:T(8,128)}), f32[32,32,128]{2,1,0:T(8,128)S(1)}, u32[]{:S(2)}, u32[]{:S(2)}) async-start(f32[32,32,128]{2,1,0:T(8,128)} %low_pass.1), calls=%async_computation.3 | async-start | bytes 1048576 | tf_op jit(solution)/shard_map/all_to_all | solution.py:29
  96.4 0.9 collective-permute-done.west_ref.west_hbm
  97.4 0.0 copy-start.1
  97.4 1.6 %collective-permute-done.1.east_ref.east_hbm = f32[8,64,128]{2,1,0:T(8,128)S(1)} collective-permute-done((f32[8,64,128]{2,1,0:T(8,128)S(1)}, f32[8,64,128]{2,1,0:T(8,128)S(1)}, u32[]{:S(2)}, u32[]{:S(2)}) %collective-permute-start.1) | collective-permute-done | bytes 262176 | tf_op jit(solution)/shard_map/ppermute | solution.py:87
  99.0 0.0 copy-start.2
  99.0 0.1 ends.1
  99.1 4.7 %collective-permute-start.2 = (f32[10,64,128]{2,1,0:T(8,128)S(1)}, f32[10,64,128]{2,1,0:T(8,128)S(1)}, u32[]{:S(2)}, u32[]{:S(2)}) collective-permute-start(f32[10,64,128]{2,1,0:T(8,128)S(1)} %get-tuple-element.62), channel_id=1, source_target_pairs={{0,1},{1,2},{2,3},{4,5},{5,6},{6,7},{8,9},{9,10},{10,11},{12,13},{... | collective-permute-start | bytes 983048 | tf_op jit(solution)/shard_map/ppermute | solution.py:92
  103.8 1.9 %collective-permute-start.3 = (f32[10,64,128]{2,1,0:T(8,128)S(1)}, f32[10,64,128]{2,1,0:T(8,128)S(1)}, u32[]{:S(2)}, u32[]{:S(2)}) collective-permute-start(f32[10,64,128]{2,1,0:T(8,128)S(1)} %get-tuple-element.63), channel_id=1, source_target_pairs={{1,0},{2,1},{3,2},{5,4},{6,5},{7,6},{9,8},{10,9},{11,10},{13,12},{... | collective-permute-start | bytes 983048 | tf_op jit(solution)/shard_map/ppermute | solution.py:92
  105.7 0.0 copy-done.1
  105.8 0.0 copy-done.2
  105.8 9.4 %prepare.1 = (f32[128,48,128]{2,1,0:T(8,128)}, f32[128,16,128]{2,1,0:T(8,128)}, f32[2,16,64,128]{3,2,1,0:T(8,128)}, f32[2,16,128]{2,1,0:T(8,128)S(1)}) custom-call(s32[128]{0:T(128)S(1)} %bitcast.24, s32[5]{0:T(128)S(1)} %stack.31.info_ref, bf16[256,48,128]{2,1,0:T(8,128)(2,1)} %bitcast.10.moved_hbm, bf16[128,128,128]{2,1,0:T(8,128)(2,1)} %weights_hbm.3, ...), custom_call_target="tpu_custom_call" | custom-call | flops 20000000000 | bytes 16000000 | tf_op jit(solution)/shard_map/prepare/pallas_call | solution.py:584
  115.1 0.0 collective-permute-done.2.above_hbm
  115.1 0.0 copy-start.3
  115.2 0.0 collective-permute-done.3.below_hbm
  115.2 0.0 copy-start.4
  115.2 0.0 all-to-all-done.3.smooth_ref
  115.2 0.7 copy-done.3
  115.9 0.1 copy-done.4
  116.0 8.7 %basis.1 = (f32[144,16,128]{2,1,0:T(8,128)S(1)}, f32[144,16,128]{2,1,0:T(8,128)S(1)}, f32[144,16,128]{2,1,0:T(8,128)S(1)}, f32[144,16,128]{2,1,0:T(8,128)S(1)}, ...) custom-call(s32[5]{0:T(128)S(1)} %stack.31.info_ref, ...), custom_call_target="tpu_custom_call" | custom-call | flops 40000000 | bytes 24000000 | tf_op jit(solution)/shard_map/basis/pallas_call | solution.py:794
  124.7 16.8 %all_to_all.39 = f32[128,1,128]{2,1,0:T(1,128)S(1)} all-to-all(f32[128,1,128]{2,1,0:T(1,128)S(1)} %bitcast.20), channel_id=1, replica_groups=mesh['lon'=32,'lat'=4] {'lon','lat'}, dimensions={0} | all-to-all | bytes 131072 | tf_op jit(solution)/shard_map/all_to_all | solution.py:29
  141.5 4.6 %finish.1 = f32[128,48,128]{2,1,0:T(8,128)} custom-call(s32[5]{0:T(128)S(1)} %stack.31.info_ref, f32[128,128]{1,0:T(8,128)S(1)} %bitcast.19, f32[128,48,128]{2,1,0:T(8,128)} %get-tuple-element.69.filtered_hbm, f32[16,48,128]{2,1,0:T(8,128)} %get-tuple-element.70.caps_hbm, f32[144,16,128]{2,1,0:T(8,128)S(1)} %get-tuple-element.71.t0, ...), custom_call_target="tpu_custom_call" | custom-call | flops 20000000 | bytes 17000000 | tf_op jit(solution)/shard_map/finish/pallas_call | solution.py:932
  (2 shorter events, 0.0 us)
Async XLA Ops:
  0.0 22.0 %copy-start = (bf16[128,3,16,128]{3,2,1,0:T(8,128)(2,1)S(1)}, bf16[128,3,16,128]{3,2,1,0:T(8,128)(2,1)}, u32[]{:S(2)}) copy-start(bf16[128,3,16,128]{3,2,1,0:T(8,128)(2,1)} %param.9) | copy-start | bytes 4718596
  24.7 5.7 %copy-start.5 = (s32[32]{0:T(128)S(1)}, s32[32]{0:T(128)}, u32[]{:S(2)}) copy-start(s32[32]{0:T(128)} %param.13) | copy-start | bytes 388
  24.7 47.3 %all-to-all-start.1 = ((bf16[128,2,3,16,128]{4,3,2,1,0:T(8,128)(2,1)}), bf16[128,2,3,16,128]{4,3,2,1,0:T(8,128)(2,1)}, u32[]{:S(2)}, u32[]{:S(2)}) async-start(bf16[128,2,3,16,128]{4,3,2,1,0:T(8,128)(2,1)} %bitcast.25), calls=%async_computation.1 | async-start | bytes 6291456 | tf_op jit(solution)/shard_map/all_to_all | solution.py:29
  75.3 13.8 %all-to-all-start.2 = ((f32[32,24,128]{2,1,0:T(8,128)}), f32[32,24,128]{2,1,0:T(8,128)S(1)}, u32[]{:S(2)}, u32[]{:S(2)}) async-start(f32[32,24,128]{2,1,0:T(8,128)} %bitcast.11), calls=%async_computation.2 | async-start | bytes 786432 | tf_op jit(solution)/shard_map/all_to_all | solution.py:29
  83.3 14.1 %collective-permute-start = (f32[8,64,128]{2,1,0:T(8,128)}, f32[8,64,128]{2,1,0:T(8,128)S(1)}, u32[]{:S(2)}, u32[]{:S(2)}) collective-permute-start(f32[8,64,128]{2,1,0:T(8,128)} %get-tuple-element.58), channel_id=1, source_target_pairs={{0,4},{4,8},{8,12},{12,16},{16,20},{20,24},{24,28},{28,32},{32,36}... | collective-permute-start | bytes 786440 | tf_op jit(solution)/shard_map/ppermute | solution.py:87
  84.5 14.5 %collective-permute-start.1 = (f32[8,64,128]{2,1,0:T(8,128)S(1)}, f32[8,64,128]{2,1,0:T(8,128)S(1)}, u32[]{:S(2)}, u32[]{:S(2)}) collective-permute-start(f32[8,64,128]{2,1,0:T(8,128)S(1)} %get-tuple-element.59), channel_id=1, source_target_pairs={{4,0},{8,4},{12,8},{16,12},{20,16},{24,20},{28,24},{32,28},{36,32}... | collective-permute-start | bytes 786440 | tf_op jit(solution)/shard_map/ppermute | solution.py:87
  92.5 22.6 %all-to-all-start.3 = ((f32[32,32,128]{2,1,0:T(8,128)}), f32[32,32,128]{2,1,0:T(8,128)S(1)}, u32[]{:S(2)}, u32[]{:S(2)}) async-start(f32[32,32,128]{2,1,0:T(8,128)} %low_pass.1), calls=%async_computation.3 | async-start | bytes 1048576 | tf_op jit(solution)/shard_map/all_to_all | solution.py:29
  97.4 8.4 %copy-start.1 = (f32[8,64,128]{2,1,0:T(8,128)}, f32[8,64,128]{2,1,0:T(8,128)S(1)}, u32[]{:S(2)}) copy-start(f32[8,64,128]{2,1,0:T(8,128)S(1)} %collective-permute-done.west_ref.west_hbm) | copy-start | bytes 786436
  99.0 6.8 %copy-start.2 = (f32[8,64,128]{2,1,0:T(8,128)}, f32[8,64,128]{2,1,0:T(8,128)S(1)}, u32[]{:S(2)}) copy-start(f32[8,64,128]{2,1,0:T(8,128)S(1)} %collective-permute-done.1.east_ref.east_hbm) | copy-start | bytes 786436
  99.1 16.1 %collective-permute-start.2 = (f32[10,64,128]{2,1,0:T(8,128)S(1)}, f32[10,64,128]{2,1,0:T(8,128)S(1)}, u32[]{:S(2)}, u32[]{:S(2)}) collective-permute-start(f32[10,64,128]{2,1,0:T(8,128)S(1)} %get-tuple-element.62), channel_id=1, source_target_pairs={{0,1},{1,2},{2,3},{4,5},{5,6},{6,7},{8,9},{9,10},{10,11},{12,13},{... | collective-permute-start | bytes 983048 | tf_op jit(solution)/shard_map/ppermute | solution.py:92
  103.8 11.3 %collective-permute-start.3 = (f32[10,64,128]{2,1,0:T(8,128)S(1)}, f32[10,64,128]{2,1,0:T(8,128)S(1)}, u32[]{:S(2)}, u32[]{:S(2)}) collective-permute-start(f32[10,64,128]{2,1,0:T(8,128)S(1)} %get-tuple-element.63), channel_id=1, source_target_pairs={{1,0},{2,1},{3,2},{5,4},{6,5},{7,6},{9,8},{10,9},{11,10},{13,12},{... | collective-permute-start | bytes 983048 | tf_op jit(solution)/shard_map/ppermute | solution.py:92
  115.1 0.7 copy-start.3
  115.2 0.9 copy-start.4

commit v5 on v4

--- a/solution.py
+++ b/solution.py
@@ -815,7 +815,7 @@
         cost_estimate=pl.CostEstimate(flops=40000000, bytes_accessed=24000000, transcendentals=0),
         compiler_params=params(16),
         name="basis",
-    )(info, *[in_hbm(x) for x in (above, below, begun, sides, stiffness)], ends, smooth)
+    )(info, above, below, *[in_hbm(x) for x in (begun, sides, stiffness)], ends, smooth)
 
 
 def solve(mu):

time: 147 us -> 146 us (level)
  no operation moved by 1% of the time
where the time goes in v5:
time: 146 us
  Pallas kernels  48.4 us (33%)
  blocking collectives  37.6 us (26%)
  waiting for transfers between devices  29.2 us (20%)
  starting transfers between devices  26 us (18%)
  local copies, waits for them, and re-layouts  4 us (3%)
    all_to_all x2, blocking collectives, exchange(): return lax.all_to_all(block, axes, split_axis=0, concat_axis=0, tiled=True)  37.6 us
    all_to_all x3, waiting for transfers between devices, exchange(): return lax.all_to_all(block, axes, split_axis=0, concat_axis=0, tiled=True)  26.7 us
    all_to_all x3, starting transfers between devices, exchange(): return lax.all_to_all(block, axes, split_axis=0, concat_axis=0, tiled=True)  13.5 us
    pallas_call x1, Pallas kernels, edge_weights(): pl.pallas_call(edge_weights_kernel, grid=(rows // FIELDS,), in_specs=[pl....  10.3 us
    pallas_call x1, Pallas kernels, prepare(): pl.pallas_call(prepare_kernel, in_specs=[pl.BlockSpec(memory_space=pltpu....  9.38 us
    pallas_call x1, Pallas kernels, make_basis(): pl.pallas_call(basis_kernel, in_specs=[pl.BlockSpec(memory_space=pltpu.SM...  8.66 us
    ppermute x2, starting transfers between devices, from_ends(): return (lax.ppermute(last, 'lat', north), lax.ppermute(first, 'lat', south))  6.77 us
    pallas_call x1, Pallas kernels, finish(): pl.pallas_call(finish_kernel, grid=(rows // block,), in_specs=[pl.BlockSp...  4.61 us
  transfers between devices with their start and end apart: 7, of which 3 were waited for; matrix products, arithmetic and copies ran while one was open for 1% of the time, Pallas kernels for 21%

profile of v5, /device:TPU:1, one launch (start us, length us, event | category | flops | bytes accessed | tf_op | source)
XLA Modules:
  0.0 145.5 jit_solution(12618335842735539478)
XLA Ops:
  0.0 0.0 copy-start
  0.0 1.0 requests.1
  1.0 20.8 %all_to_all.38 = s32[128,1,128]{2,1,0:T(1,128)S(1)} all-to-all(s32[128,1,128]{2,1,0:T(1,128)S(1)} %bitcast.21), channel_id=1, replica_groups=mesh['lon'=32,'lat'=4] {'lon','lat'}, dimensions={0} | all-to-all | bytes 131072 | tf_op jit(solution)/shard_map/all_to_all | solution.py:29
  21.9 0.1 reshape.21
  22.0 0.0 copy-done
  22.0 2.6 %gather_fusion = bf16[256,3,16,128]{3,2,1,0:T(8,128)(2,1)} fusion(bf16[128,3,16,128]{3,2,1,0:T(8,128)(2,1)S(1)} %copy-done, s32[1024]{0:T(1024)S(1)} %pad_clamp_fusion), kind=kCustom, calls=%fused_computation | custom fusion | bytes 6292480 | tf_op jit(solution)/shard_map/gather | solution.py:973
  24.7 0.0 copy-start.3
  24.7 5.7 %all-to-all-start.1 = ((bf16[128,2,3,16,128]{4,3,2,1,0:T(8,128)(2,1)}), bf16[128,2,3,16,128]{4,3,2,1,0:T(8,128)(2,1)}, u32[]{:S(2)}, u32[]{:S(2)}) async-start(bf16[128,2,3,16,128]{4,3,2,1,0:T(8,128)(2,1)} %bitcast.25), calls=%async_computation.1 | async-start | bytes 6291456 | tf_op jit(solution)/shard_map/all_to_all | solution.py:29
  30.4 0.0 copy-done.3
  30.4 0.6 dynamic_slice.3
  31.0 0.6 stack.31.info_ref
  31.6 3.3 %pack_stiffness.1 = (f32[8,16,128]{2,1,0:T(8,128)}, f32[8,16,128]{2,1,0:T(8,128)}, f32[16,16,128]{2,1,0:T(8,128)}) custom-call(f32[128,16,128]{2,1,0:T(8,128)} %stiffness_hbm.3), custom_call_target="tpu_custom_call" | custom-call | flops 1000000 | bytes 1300000 | tf_op jit(solution)/shard_map/pack_stiffness/pallas_call | solution.py:211
  34.9 10.3 %edge_weights.1.weights_hbm = bf16[16,128,128]{2,1,0:T(8,128)(2,1)} custom-call(bf16[128,128,128]{2,1,0:T(8,128)(2,1)} %weights_hbm.3), custom_call_target="tpu_custom_call" | custom-call | flops 2000000 | bytes 5000000 | tf_op jit(solution)/shard_map/edge_weights/pallas_call | solution.py:227
  45.2 26.7 %all-to-all-done.1 = bf16[128,2,3,16,128]{4,3,2,1,0:T(8,128)(2,1)} async-done(((bf16[128,2,3,16,128]{4,3,2,1,0:T(8,128)(2,1)}), bf16[128,2,3,16,128]{4,3,2,1,0:T(8,128)(2,1)}, u32[]{:S(2)}, u32[]{:S(2)}) %all-to-all-start.1) | async-done | bytes 3145760 | tf_op jit(solution)/shard_map/all_to_all | solution.py:29
  71.9 3.3 %caps.1 = (f32[16,48,128]{2,1,0:T(8,128)}, f32[9,64,128]{2,1,0:T(8,128)S(1)}, f32[9,64,128]{2,1,0:T(8,128)S(1)}) custom-call(s32[128]{0:T(128)S(1)} %bitcast.22, s32[5]{0:T(128)S(1)} %stack.31.info_ref, bf16[256,48,128]{2,1,0:T(8,128)(2,1)} %bitcast.10.moved_hbm, bf16[128,128,128]{2,1,0:T(8,128)(2,1)} %weights_hbm.3, f32[128,16,128]{2,1,0:T(8,128)} %stiffness_hbm.3), custom_call_target="tpu_custom_call" | custom-call | flops 60000000 | bytes 2400000 | tf_op jit(solution)/shard_map/caps/pallas_call | solution.py:177
  75.3 3.9 %all-to-all-start.2 = ((f32[32,24,128]{2,1,0:T(8,128)}), f32[32,24,128]{2,1,0:T(8,128)S(1)}, u32[]{:S(2)}, u32[]{:S(2)}) async-start(f32[32,24,128]{2,1,0:T(8,128)} %bitcast.11), calls=%async_computation.2 | async-start | bytes 786432 | tf_op jit(solution)/shard_map/all_to_all | solution.py:29
  79.2 4.2 %edges.1 = (f32[8,64,128]{2,1,0:T(8,128)}, f32[8,64,128]{2,1,0:T(8,128)}, f32[16,64,128]{2,1,0:T(8,128)}) custom-call(s32[128]{0:T(128)S(1)} %bitcast.23, bf16[256,48,128]{2,1,0:T(8,128)(2,1)} %bitcast.10.moved_hbm, f32[8,16,128]{2,1,0:T(8,128)} %get-tuple-element.54.east_hbm, f32[8,16,128]{2,1,0:T(8,128)} %get-tuple-element.55.west_hbm, ...), custom_call_target="tpu_custom_call" | custom-call | flops 10000000000 | bytes 5000000 | tf_op jit(solution)/shard_map/edges/pallas_call | solution.py:290
  83.4 1.2 collective-permute-start
  84.6 4.6 %collective-permute-start.1 = (f32[8,64,128]{2,1,0:T(8,128)}, f32[8,64,128]{2,1,0:T(8,128)S(1)}, u32[]{:S(2)}, u32[]{:S(2)}) collective-permute-start(f32[8,64,128]{2,1,0:T(8,128)} %get-tuple-element.59), channel_id=1, source_target_pairs={{4,0},{8,4},{12,8},{16,12},{20,16},{24,20},{28,24},{32,28},{36,32}... | collective-permute-start | bytes 786440 | tf_op jit(solution)/shard_map/ppermute | solution.py:87
  89.2 0.0 all-to-all-done.2.lines_ref
  89.2 3.5 %low_pass.1 = f32[32,32,128]{2,1,0:T(8,128)} custom-call(s32[5]{0:T(128)S(1)} %stack.31.info_ref, f32[32,24,128]{2,1,0:T(8,128)S(1)} %all-to-all-done.2.lines_ref, f32[34,128]{1,0:T(8,128)} %constant.42.clone.twist_hbm, bf16[2,256,256]{2,1,0:T(8,128)(2,1)} %constant.43.clone.forward_hbm, bf16[2,256,256]{2,1,0:T(8,128)(2,1)} %constant.44.clone.inverse_hbm), custom_call_target="tpu_custom_call" | custom-call | flops 700000000 | bytes 1400000 | tf_op jit(solution)/shard_map/low_pass/pallas_call | solution.py:460
  92.7 3.9 %all-to-all-start.3 = ((f32[32,32,128]{2,1,0:T(8,128)}), f32[32,32,128]{2,1,0:T(8,128)S(1)}, u32[]{:S(2)}, u32[]{:S(2)}) async-start(f32[32,32,128]{2,1,0:T(8,128)} %low_pass.1), calls=%async_computation.3 | async-start | bytes 1048576 | tf_op jit(solution)/shard_map/all_to_all | solution.py:29
  96.6 0.7 collective-permute-done.west_ref.west_hbm
  97.3 0.0 copy-start.1
  97.3 1.7 %collective-permute-done.1.east_ref.east_hbm = f32[8,64,128]{2,1,0:T(8,128)S(1)} collective-permute-done((f32[8,64,128]{2,1,0:T(8,128)}, f32[8,64,128]{2,1,0:T(8,128)S(1)}, u32[]{:S(2)}, u32[]{:S(2)}) %collective-permute-start.1) | collective-permute-done | bytes 262176 | tf_op jit(solution)/shard_map/ppermute | solution.py:87
  99.0 0.0 copy-start.2
  99.0 0.1 ends.1
  99.1 4.9 %collective-permute-start.2 = (f32[10,64,128]{2,1,0:T(8,128)S(1)}, f32[10,64,128]{2,1,0:T(8,128)S(1)}, u32[]{:S(2)}, u32[]{:S(2)}) collective-permute-start(f32[10,64,128]{2,1,0:T(8,128)S(1)} %get-tuple-element.62), channel_id=1, source_target_pairs={{0,1},{1,2},{2,3},{4,5},{5,6},{6,7},{8,9},{9,10},{10,11},{12,13},{... | collective-permute-start | bytes 983048 | tf_op jit(solution)/shard_map/ppermute | solution.py:92
  103.9 1.9 %collective-permute-start.3 = (f32[10,64,128]{2,1,0:T(8,128)S(1)}, f32[10,64,128]{2,1,0:T(8,128)S(1)}, u32[]{:S(2)}, u32[]{:S(2)}) collective-permute-start(f32[10,64,128]{2,1,0:T(8,128)S(1)} %get-tuple-element.63), channel_id=1, source_target_pairs={{1,0},{2,1},{3,2},{5,4},{6,5},{7,6},{9,8},{10,9},{11,10},{13,12},{... | collective-permute-start | bytes 983048 | tf_op jit(solution)/shard_map/ppermute | solution.py:92
  105.9 0.0 copy-done.1
  105.9 0.0 copy-done.2
  105.9 9.4 %prepare.1 = (f32[128,48,128]{2,1,0:T(8,128)}, f32[128,16,128]{2,1,0:T(8,128)}, f32[2,16,64,128]{3,2,1,0:T(8,128)}, f32[2,16,128]{2,1,0:T(8,128)S(1)}) custom-call(s32[128]{0:T(128)S(1)} %bitcast.24, s32[5]{0:T(128)S(1)} %stack.31.info_ref, bf16[256,48,128]{2,1,0:T(8,128)(2,1)} %bitcast.10.moved_hbm, bf16[128,128,128]{2,1,0:T(8,128)(2,1)} %weights_hbm.3, ...), custom_call_target="tpu_custom_call" | custom-call | flops 20000000000 | bytes 16000000 | tf_op jit(solution)/shard_map/prepare/pallas_call | solution.py:584
  115.3 0.0 collective-permute-done.2.above_hbm
  115.3 0.0 collective-permute-done.3.below_hbm
  115.3 0.0 all-to-all-done.3.smooth_ref
  115.3 8.7 %basis.1 = (f32[144,16,128]{2,1,0:T(8,128)S(1)}, f32[144,16,128]{2,1,0:T(8,128)S(1)}, f32[144,16,128]{2,1,0:T(8,128)S(1)}, f32[144,16,128]{2,1,0:T(8,128)S(1)}, ...) custom-call(s32[5]{0:T(128)S(1)} %stack.31.info_ref, ...), custom_call_target="tpu_custom_call" | custom-call | flops 40000000 | bytes 24000000 | tf_op jit(solution)/shard_map/basis/pallas_call | solution.py:794
  124.0 16.8 %all_to_all.39 = f32[128,1,128]{2,1,0:T(1,128)S(1)} all-to-all(f32[128,1,128]{2,1,0:T(1,128)S(1)} %bitcast.20), channel_id=1, replica_groups=mesh['lon'=32,'lat'=4] {'lon','lat'}, dimensions={0} | all-to-all | bytes 131072 | tf_op jit(solution)/shard_map/all_to_all | solution.py:29
  140.8 4.6 %finish.1 = f32[128,48,128]{2,1,0:T(8,128)} custom-call(s32[5]{0:T(128)S(1)} %stack.31.info_ref, f32[128,128]{1,0:T(8,128)S(1)} %bitcast.19, f32[128,48,128]{2,1,0:T(8,128)} %get-tuple-element.69.filtered_hbm, f32[16,48,128]{2,1,0:T(8,128)} %get-tuple-element.70.caps_hbm, f32[144,16,128]{2,1,0:T(8,128)S(1)} %get-tuple-element.71.t0, ...), custom_call_target="tpu_custom_call" | custom-call | flops 20000000 | bytes 17000000 | tf_op jit(solution)/shard_map/finish/pallas_call | solution.py:932
  (2 shorter events, 0.0 us)
Async XLA Ops:
  0.0 22.0 %copy-start = (bf16[128,3,16,128]{3,2,1,0:T(8,128)(2,1)S(1)}, bf16[128,3,16,128]{3,2,1,0:T(8,128)(2,1)}, u32[]{:S(2)}) copy-start(bf16[128,3,16,128]{3,2,1,0:T(8,128)(2,1)} %param.9) | copy-start | bytes 4718596
  24.7 5.7 %copy-start.3 = (s32[32]{0:T(128)S(1)}, s32[32]{0:T(128)}, u32[]{:S(2)}) copy-start(s32[32]{0:T(128)} %param.13) | copy-start | bytes 388
  24.7 47.3 %all-to-all-start.1 = ((bf16[128,2,3,16,128]{4,3,2,1,0:T(8,128)(2,1)}), bf16[128,2,3,16,128]{4,3,2,1,0:T(8,128)(2,1)}, u32[]{:S(2)}, u32[]{:S(2)}) async-start(bf16[128,2,3,16,128]{4,3,2,1,0:T(8,128)(2,1)} %bitcast.25), calls=%async_computation.1 | async-start | bytes 6291456 | tf_op jit(solution)/shard_map/all_to_all | solution.py:29
  75.3 13.9 %all-to-all-start.2 = ((f32[32,24,128]{2,1,0:T(8,128)}), f32[32,24,128]{2,1,0:T(8,128)S(1)}, u32[]{:S(2)}, u32[]{:S(2)}) async-start(f32[32,24,128]{2,1,0:T(8,128)} %bitcast.11), calls=%async_computation.2 | async-start | bytes 786432 | tf_op jit(solution)/shard_map/all_to_all | solution.py:29
  83.4 13.9 %collective-permute-start = (f32[8,64,128]{2,1,0:T(8,128)}, f32[8,64,128]{2,1,0:T(8,128)S(1)}, u32[]{:S(2)}, u32[]{:S(2)}) collective-permute-start(f32[8,64,128]{2,1,0:T(8,128)} %get-tuple-element.58), channel_id=1, source_target_pairs={{0,4},{4,8},{8,12},{12,16},{16,20},{20,24},{24,28},{28,32},{32,36}... | collective-permute-start | bytes 786440 | tf_op jit(solution)/shard_map/ppermute | solution.py:87
  84.6 14.4 %collective-permute-start.1 = (f32[8,64,128]{2,1,0:T(8,128)}, f32[8,64,128]{2,1,0:T(8,128)S(1)}, u32[]{:S(2)}, u32[]{:S(2)}) collective-permute-start(f32[8,64,128]{2,1,0:T(8,128)} %get-tuple-element.59), channel_id=1, source_target_pairs={{4,0},{8,4},{12,8},{16,12},{20,16},{24,20},{28,24},{32,28},{36,32}... | collective-permute-start | bytes 786440 | tf_op jit(solution)/shard_map/ppermute | solution.py:87
  92.7 22.6 %all-to-all-start.3 = ((f32[32,32,128]{2,1,0:T(8,128)}), f32[32,32,128]{2,1,0:T(8,128)S(1)}, u32[]{:S(2)}, u32[]{:S(2)}) async-start(f32[32,32,128]{2,1,0:T(8,128)} %low_pass.1), calls=%async_computation.3 | async-start | bytes 1048576 | tf_op jit(solution)/shard_map/all_to_all | solution.py:29
  97.3 8.6 %copy-start.1 = (f32[8,64,128]{2,1,0:T(8,128)}, f32[8,64,128]{2,1,0:T(8,128)S(1)}, u32[]{:S(2)}) copy-start(f32[8,64,128]{2,1,0:T(8,128)S(1)} %collective-permute-done.west_ref.west_hbm) | copy-start | bytes 786436
  99.0 6.9 %copy-start.2 = (f32[8,64,128]{2,1,0:T(8,128)}, f32[8,64,128]{2,1,0:T(8,128)S(1)}, u32[]{:S(2)}) copy-start(f32[8,64,128]{2,1,0:T(8,128)S(1)} %collective-permute-done.1.east_ref.east_hbm) | copy-start | bytes 786436
  99.1 16.2 %collective-permute-start.2 = (f32[10,64,128]{2,1,0:T(8,128)S(1)}, f32[10,64,128]{2,1,0:T(8,128)S(1)}, u32[]{:S(2)}, u32[]{:S(2)}) collective-permute-start(f32[10,64,128]{2,1,0:T(8,128)S(1)} %get-tuple-element.62), channel_id=1, source_target_pairs={{0,1},{1,2},{2,3},{4,5},{5,6},{6,7},{8,9},{9,10},{10,11},{12,13},{... | collective-permute-start | bytes 983048 | tf_op jit(solution)/shard_map/ppermute | solution.py:92
  103.9 11.3 %collective-permute-start.3 = (f32[10,64,128]{2,1,0:T(8,128)S(1)}, f32[10,64,128]{2,1,0:T(8,128)S(1)}, u32[]{:S(2)}, u32[]{:S(2)}) collective-permute-start(f32[10,64,128]{2,1,0:T(8,128)S(1)} %get-tuple-element.63), channel_id=1, source_target_pairs={{1,0},{2,1},{3,2},{5,4},{6,5},{7,6},{9,8},{10,9},{11,10},{13,12},{... | collective-permute-start | bytes 983048 | tf_op jit(solution)/shard_map/ppermute | solution.py:92
